TPU v7x, 32 devices: a whole 2x2x4 slice. The times are simulated.
32 devices in a mesh: dp: 8 (over y, x, core), seq: 4 (over z).
Axes of the slice: x: 2, y: 2, z: 4, core: 2. Of those that a mesh axis runs over, the one named last changes fastest.
Arguments:
- block_input: bfloat16 [32, 1024, 1152], P('dp', 'seq'), may hold values from -6 to 6
- modulation: bfloat16 [32, 4, 6912], P('dp'), may hold values from -3 to 3
- segment_ids: int32 [32, 1024], P('dp', 'seq'), may hold values from 0 to 3, as said below
- qkv_weight: bfloat16 [1152, 3456], P('seq'), may hold values from -0.1875 to 0.1875
- query_value_bias: bfloat16 [2304], replicated, may hold values from -3 to 3
- attn_out_weight: bfloat16 [1152, 1152], P('seq'), may hold values from -1.5 to 1.5
- attn_out_bias: bfloat16 [1152], replicated, may hold values from -3 to 3
- mlp_in_weight: bfloat16 [1152, 4608], P('seq'), may hold values from -0.1875 to 0.1875
- mlp_in_bias: bfloat16 [4608], replicated, may hold values from -3 to 3
- mlp_out_weight: bfloat16 [4608, 1152], P('seq'), may hold values from -0.1875 to 0.1875
- mlp_out_bias: bfloat16 [1152], replicated, may hold values from -3 to 3
- proj_in_weight: bfloat16 [1152, 2048], P('seq'), may hold values from -0.1875 to 0.1875
- proj_in_bias: bfloat16 [2048], replicated, may hold values from -3 to 3
- proj_mid_weight: bfloat16 [2048, 2048], P('seq'), may hold values from -0.125 to 0.125
- proj_mid_bias: bfloat16 [2048], replicated, may hold values from -3 to 3
- proj_out_weight: bfloat16 [2048, 768], P('seq'), may hold values from -0.125 to 0.125
- proj_out_bias: bfloat16 [768], replicated, may hold values from -2 to 2
- targets: bfloat16 [32, 1024, 768], P('dp', 'seq'), may hold values from -6 to 6
Outputs:
- block_out: bfloat16 [32, 1024, 1152], P('dp', 'seq')
- grad_input: float32 [32, 1024, 1152], P('dp', 'seq')
- grad_modulation: float32 [32, 4, 6912], P('dp')
- grad_qkv_weight: float32 [1152, 3456], P('seq')
- grad_query_value_bias: float32 [2304], P('seq')
- grad_attn_out_weight: float32 [1152, 1152], P('seq')
- grad_attn_out_bias: float32 [1152], P('seq')
- grad_mlp_in_weight: float32 [1152, 4608], P('seq')
- grad_mlp_in_bias: float32 [4608], P('seq')
- grad_mlp_out_weight: float32 [4608, 1152], P('seq')
- grad_mlp_out_bias: float32 [1152], P('seq')
- grad_proj_in_weight: float32 [1152, 2048], P('seq')
- grad_proj_in_bias: float32 [2048], P('seq')
- grad_proj_mid_weight: float32 [2048, 2048], P('seq')
- grad_proj_mid_bias: float32 [2048], P('seq')
- grad_proj_out_weight: float32 [2048, 768], P('seq')
- grad_proj_out_bias: float32 [768], P('seq')
Inputs may be any that keep to these rules, and one draw needn't show every extreme that they name: `segment_ids`: along each row the numbers never fall and each of 0 to 3 occurs; in each row one image, which one drawn at random, takes all positions but fewer than 256.
All inputs are finite; a program needn't handle non-finite values.
Results may differ from a plain program's by a relative error of at most 0.025.
Values may be sent and summed in bfloat16 or wider, within the bound.
A program may use at most 512 MiB of HBM per device.

v0:
```python
import math

import jax
import jax.numpy as jnp
from jax import lax
from jax.sharding import PartitionSpec as P

HEAD_DIM = 72


EPSILON = 1e-06
HIGHEST = lax.Precision.HIGHEST
GELU_COEF = 0.044715


def matmul(left, right):
    return jnp.dot(left, right, preferred_element_type=jnp.float32)


def matmul_tn(left, right):
    return lax.dot_general(
        left, right, (((0,), (0,)), ((), ())), preferred_element_type=jnp.float32
    )


def matmul_nt(left, right):
    return lax.dot_general(
        left, right, (((1,), (1,)), ((), ())), preferred_element_type=jnp.float32
    )


def silu_grad(value):
    sigmoid_val = jax.nn.sigmoid(value)
    return sigmoid_val * (1.0 + value * (1.0 - sigmoid_val))


def gelu_grad(value):
    factor = math.sqrt(2.0 / math.pi)
    tangent = jnp.tanh(factor * (value + GELU_COEF * value * value * value))
    return 0.5 * (1.0 + tangent) + 0.5 * value * (1.0 - tangent * tangent) * factor * (
        1.0 + 3.0 * GELU_COEF * value * value
    )


def norm_stats(values):
    centred = values - jnp.mean(values, axis=-1, keepdims=True)
    inv_std = lax.rsqrt(jnp.mean(centred * centred, axis=-1, keepdims=True) + EPSILON)
    return (centred * inv_std, inv_std)


def norm_back(grad_normed, normed, inv_std):
    return inv_std * (
        grad_normed
        - jnp.mean(grad_normed, axis=-1, keepdims=True)
        - normed * jnp.mean(grad_normed * normed, axis=-1, keepdims=True)
    )


def split_heads(qkv_heads):
    count, length = (qkv_heads.shape[0], qkv_heads.shape[1])
    groups = qkv_heads.shape[4] // HEAD_DIM
    parts = qkv_heads.reshape(count, length, 3, groups, HEAD_DIM)
    return (parts[:, :, 0], parts[:, :, 1], parts[:, :, 2])


def masked_scores(query_blk, keys, seg_query, seg_keys):
    scores = jnp.einsum("rqgd,rkgd->rgqk", query_blk, keys, preferred_element_type=jnp.float32)
    scores = scores * HEAD_DIM ** (-0.5)
    same = seg_query[:, None, :, None] == seg_keys[:, None, None, :]
    return jnp.where(same, scores, -1e30)


def attend_forward(pieces):
    qkv_heads, seg_heads = pieces
    query, keys, values = split_heads(qkv_heads)
    count, length, groups = (query.shape[0], query.shape[1], query.shape[2])
    seg_row = seg_heads.reshape(count, length)
    qblock = min(512, length)
    outputs = []
    totals = []
    for start in range(0, length, qblock):
        scores = masked_scores(
            query[:, start : start + qblock], keys, seg_row[:, start : start + qblock], seg_row
        )
        row_max = jnp.max(scores, axis=-1, keepdims=True)
        exp_scores = jnp.exp(scores - row_max)
        row_sum = jnp.sum(exp_scores, axis=-1, keepdims=True)
        prob_low = (exp_scores / row_sum).astype(jnp.bfloat16)
        outputs.append(
            jnp.einsum("rgqk,rkgd->rqgd", prob_low, values, preferred_element_type=jnp.float32)
        )
        totals.append((row_max + jnp.log(row_sum))[..., 0])
    attended = (
        jnp.concatenate(outputs, axis=1)
        .astype(jnp.bfloat16)
        .reshape(count, length, groups * HEAD_DIM)
    )
    log_total = jnp.concatenate(totals, axis=2)
    return (attended, log_total, seg_row, qkv_heads)


def attend_backward(qkv_heads, seg_row, log_total, grad_heads):
    query, keys, values = split_heads(qkv_heads)
    count, length, groups = (query.shape[0], query.shape[1], query.shape[2])
    grad_attn = grad_heads.reshape(count, length, groups, HEAD_DIM)
    qblock = min(512, length)
    grad_query = []
    grad_keys = jnp.zeros((count, length, groups, HEAD_DIM), jnp.float32)
    grad_values = jnp.zeros((count, length, groups, HEAD_DIM), jnp.float32)
    for start in range(0, length, qblock):
        query_blk = query[:, start : start + qblock]
        grad_blk = grad_attn[:, start : start + qblock]
        scores = masked_scores(query_blk, keys, seg_row[:, start : start + qblock], seg_row)
        probs = jnp.exp(scores - log_total[:, :, start : start + qblock, None])
        prob_low = probs.astype(jnp.bfloat16)
        grad_probs = jnp.einsum(
            "rqgd,rkgd->rgqk", grad_blk, values, preferred_element_type=jnp.float32
        )
        row_dot = jnp.sum(probs * grad_probs, axis=-1, keepdims=True)
        grad_scores = (probs * (grad_probs - row_dot)).astype(jnp.bfloat16)
        grad_query.append(
            jnp.einsum("rgqk,rkgd->rqgd", grad_scores, keys, preferred_element_type=jnp.float32)
            * HEAD_DIM ** (-0.5)
        )
        grad_keys = grad_keys + jnp.einsum(
            "rgqk,rqgd->rkgd", grad_scores, query_blk, preferred_element_type=jnp.float32
        ) * HEAD_DIM ** (-0.5)
        grad_values = grad_values + jnp.einsum(
            "rgqk,rqgd->rkgd", prob_low, grad_blk, preferred_element_type=jnp.float32
        )
    stacked = jnp.stack([jnp.concatenate(grad_query, axis=1), grad_keys, grad_values], axis=2)
    return stacked.astype(jnp.bfloat16).reshape(count, length, 3, 1, groups * HEAD_DIM)


def local(
    block_input,
    modulation,
    segment_ids,
    qkv_weight,
    query_value_bias,
    attn_out_weight,
    attn_out_bias,
    mlp_in_weight,
    mlp_in_bias,
    mlp_out_weight,
    mlp_out_bias,
    proj_in_weight,
    proj_in_bias,
    proj_mid_weight,
    proj_mid_bias,
    proj_out_weight,
    proj_out_bias,
    targets,
):
    row_count, local_len, model_width = block_input.shape
    tokens = row_count * local_len
    seg_count = modulation.shape[1]
    seq_devices = lax.axis_size("seq")
    group_width = model_width // seq_devices
    w_qkv, w_attn, w_mlp_in, w_mlp_out = (
        lax.all_gather(qkv_weight, "seq", axis=0, tiled=True),
        lax.all_gather(attn_out_weight, "seq", axis=0, tiled=True),
        lax.all_gather(mlp_in_weight, "seq", axis=0, tiled=True),
        lax.all_gather(mlp_out_weight, "seq", axis=0, tiled=True),
    )
    inputs = block_input.astype(jnp.float32)
    one_hot = (
        segment_ids[:, :, None] == jnp.arange(seg_count, dtype=jnp.int32)[None, None, :]
    ).astype(jnp.float32)
    mod_tok = jnp.einsum("rcs,rsd->rcd", one_hot, modulation.astype(jnp.float32), precision=HIGHEST)
    shift1 = mod_tok[..., :model_width]
    scale1 = mod_tok[..., model_width : 2 * model_width]
    gate1 = mod_tok[..., 2 * model_width : 3 * model_width]
    shift2 = mod_tok[..., 3 * model_width : 4 * model_width]
    scale2 = mod_tok[..., 4 * model_width : 5 * model_width]
    gate2 = mod_tok[..., 5 * model_width :]
    normed1, inv_std1 = norm_stats(inputs)
    modulated1 = (
        (normed1 * (1.0 + scale1) + shift1).astype(jnp.bfloat16).reshape(tokens, model_width)
    )
    bias_float = query_value_bias.astype(jnp.float32)
    full_bias = jnp.concatenate(
        [bias_float[:model_width], jnp.zeros((model_width,), jnp.float32), bias_float[model_width:]]
    )
    qkv_low = (matmul(modulated1, w_qkv) + full_bias).astype(jnp.bfloat16)
    qkv_low = qkv_low.reshape(row_count, local_len, 3, seq_devices, group_width)
    seg_spread = jnp.broadcast_to(
        segment_ids.astype(jnp.bfloat16)[:, :, None, None, None],
        (row_count, local_len, 1, seq_devices, 1),
    )
    attended, log_total, seg_row, qkv_kept = attend_forward(
        (
            lax.all_to_all(qkv_low, "seq", split_axis=3, concat_axis=1, tiled=True),
            lax.all_to_all(seg_spread, "seq", split_axis=3, concat_axis=1, tiled=True),
        )
    )
    attn_tok = lax.all_to_all(attended, "seq", split_axis=1, concat_axis=2, tiled=True).reshape(
        tokens, model_width
    )
    branch = matmul(attn_tok, w_attn) + attn_out_bias.astype(jnp.float32)
    branch = branch.reshape(row_count, local_len, model_width)
    middle = inputs + gate1 * branch
    normed2, inv_std2 = norm_stats(middle)
    modulated2 = (
        (normed2 * (1.0 + scale2) + shift2).astype(jnp.bfloat16).reshape(tokens, model_width)
    )
    hmid = matmul(modulated2, w_mlp_in) + mlp_in_bias.astype(jnp.float32)
    act_mid = jax.nn.gelu(hmid, approximate=True).astype(jnp.bfloat16)
    mlp_branch = (matmul(act_mid, w_mlp_out) + mlp_out_bias.astype(jnp.float32)).reshape(
        row_count, local_len, model_width
    )
    out_low = (middle + gate2 * mlp_branch).astype(jnp.bfloat16)
    w_proj_in, w_proj_mid, w_proj_out = (
        lax.all_gather(proj_in_weight, "seq", axis=0, tiled=True),
        lax.all_gather(proj_mid_weight, "seq", axis=0, tiled=True),
        lax.all_gather(proj_out_weight, "seq", axis=0, tiled=True),
    )
    flat_out = out_low.reshape(tokens, model_width)
    hidden1 = matmul(flat_out, w_proj_in) + proj_in_bias.astype(jnp.float32)
    act1 = jax.nn.silu(hidden1).astype(jnp.bfloat16)
    hidden2 = matmul(act1, w_proj_mid) + proj_mid_bias.astype(jnp.float32)
    act2 = jax.nn.silu(hidden2).astype(jnp.bfloat16)
    feats = matmul(act2, w_proj_out) + proj_out_bias.astype(jnp.float32)
    goals = targets.astype(jnp.float32).reshape(tokens, feats.shape[1])
    inv_feat = lax.rsqrt(jnp.sum(feats * feats, axis=-1, keepdims=True) + EPSILON)
    feat_unit = feats * inv_feat
    goal_unit = goals * lax.rsqrt(jnp.sum(goals * goals, axis=-1, keepdims=True) + EPSILON)
    cosine = jnp.sum(feat_unit * goal_unit, axis=-1, keepdims=True)
    loss_weight = 0.5 * feats.shape[1]
    grad_feats = (-loss_weight * inv_feat * (goal_unit - cosine * feat_unit)).astype(jnp.bfloat16)
    grad_out_w = matmul_tn(act2, grad_feats)
    grad_out_b = jnp.sum(grad_feats.astype(jnp.float32), axis=0)
    grad_hidden2 = (matmul_nt(grad_feats, w_proj_out) * silu_grad(hidden2)).astype(jnp.bfloat16)
    grad_mid_w = matmul_tn(act1, grad_hidden2)
    grad_mid_b = jnp.sum(grad_hidden2.astype(jnp.float32), axis=0)
    grad_hidden1 = (matmul_nt(grad_hidden2, w_proj_mid) * silu_grad(hidden1)).astype(jnp.bfloat16)
    grad_in_w = matmul_tn(flat_out, grad_hidden1)
    grad_in_b = jnp.sum(grad_hidden1.astype(jnp.float32), axis=0)
    grad_output = matmul_nt(grad_hidden1, w_proj_in).reshape(row_count, local_len, model_width)
    grad_gate2 = grad_output * mlp_branch
    grad_mlp = (grad_output * gate2).astype(jnp.bfloat16).reshape(tokens, model_width)
    grad_ff_out_w = matmul_tn(act_mid, grad_mlp)
    grad_ff_out_b = jnp.sum(grad_mlp.astype(jnp.float32), axis=0)
    grad_hmid = (matmul_nt(grad_mlp, w_mlp_out) * gelu_grad(hmid)).astype(jnp.bfloat16)
    grad_ff_in_w = matmul_tn(modulated2, grad_hmid)
    grad_ff_in_b = jnp.sum(grad_hmid.astype(jnp.float32), axis=0)
    grad_modulated2 = matmul_nt(grad_hmid, w_mlp_in).reshape(row_count, local_len, model_width)
    grad_middle = grad_output + norm_back(grad_modulated2 * (1.0 + scale2), normed2, inv_std2)
    grad_gate1 = grad_middle * branch
    grad_branch = (grad_middle * gate1).astype(jnp.bfloat16).reshape(tokens, model_width)
    grad_attn_w = matmul_tn(attn_tok, grad_branch)
    grad_attn_b = jnp.sum(grad_branch.astype(jnp.float32), axis=0)
    grad_attended = matmul_nt(grad_branch, w_attn).astype(jnp.bfloat16)
    grad_attended = grad_attended.reshape(row_count, local_len, seq_devices, group_width)
    grad_heads = lax.all_to_all(grad_attended, "seq", split_axis=2, concat_axis=1, tiled=True)
    grad_qkv_heads = attend_backward(qkv_kept, seg_row, log_total, grad_heads)
    grad_qkv = lax.all_to_all(
        grad_qkv_heads, "seq", split_axis=1, concat_axis=3, tiled=True
    ).reshape(tokens, 3 * model_width)
    grad_qkv_w = matmul_tn(modulated1, grad_qkv)
    column_sums = jnp.sum(grad_qkv.astype(jnp.float32), axis=0)
    grad_qv_b = jnp.concatenate([column_sums[:model_width], column_sums[2 * model_width :]])
    grad_modulated1 = matmul_nt(grad_qkv, w_qkv).reshape(row_count, local_len, model_width)
    grad_input = grad_middle + norm_back(grad_modulated1 * (1.0 + scale1), normed1, inv_std1)
    grad_mod_tok = jnp.concatenate(
        [
            grad_modulated1,
            grad_modulated1 * normed1,
            grad_gate1,
            grad_modulated2,
            grad_modulated2 * normed2,
            grad_gate2,
        ],
        axis=-1,
    )
    grad_mod_local = jnp.einsum("rcs,rcd->rsd", one_hot, grad_mod_tok, precision=HIGHEST)
    grad_modulation = lax.psum(grad_mod_local.astype(jnp.bfloat16), "seq").astype(jnp.float32)
    shares = (
        lax.psum_scatter(
            grad_qkv_w.astype(jnp.bfloat16), "seq", scatter_dimension=0, tiled=True
        ).astype(jnp.float32),
        lax.psum_scatter(
            grad_qv_b.astype(jnp.bfloat16), "seq", scatter_dimension=0, tiled=True
        ).astype(jnp.float32),
        lax.psum_scatter(
            grad_attn_w.astype(jnp.bfloat16), "seq", scatter_dimension=0, tiled=True
        ).astype(jnp.float32),
        lax.psum_scatter(
            grad_attn_b.astype(jnp.bfloat16), "seq", scatter_dimension=0, tiled=True
        ).astype(jnp.float32),
        lax.psum_scatter(
            grad_ff_in_w.astype(jnp.bfloat16), "seq", scatter_dimension=0, tiled=True
        ).astype(jnp.float32),
        lax.psum_scatter(
            grad_ff_in_b.astype(jnp.bfloat16), "seq", scatter_dimension=0, tiled=True
        ).astype(jnp.float32),
        lax.psum_scatter(
            grad_ff_out_w.astype(jnp.bfloat16), "seq", scatter_dimension=0, tiled=True
        ).astype(jnp.float32),
        lax.psum_scatter(
            grad_ff_out_b.astype(jnp.bfloat16), "seq", scatter_dimension=0, tiled=True
        ).astype(jnp.float32),
        lax.psum_scatter(
            grad_in_w.astype(jnp.bfloat16), "seq", scatter_dimension=0, tiled=True
        ).astype(jnp.float32),
        lax.psum_scatter(
            grad_in_b.astype(jnp.bfloat16), "seq", scatter_dimension=0, tiled=True
        ).astype(jnp.float32),
        lax.psum_scatter(
            grad_mid_w.astype(jnp.bfloat16), "seq", scatter_dimension=0, tiled=True
        ).astype(jnp.float32),
        lax.psum_scatter(
            grad_mid_b.astype(jnp.bfloat16), "seq", scatter_dimension=0, tiled=True
        ).astype(jnp.float32),
        lax.psum_scatter(
            grad_out_w.astype(jnp.bfloat16), "seq", scatter_dimension=0, tiled=True
        ).astype(jnp.float32),
        lax.psum_scatter(
            grad_out_b.astype(jnp.bfloat16), "seq", scatter_dimension=0, tiled=True
        ).astype(jnp.float32),
    )
    summed = (
        lax.psum(shares[0].astype(jnp.bfloat16), "dp").astype(jnp.float32),
        lax.psum(shares[1].astype(jnp.bfloat16), "dp").astype(jnp.float32),
        lax.psum(shares[2].astype(jnp.bfloat16), "dp").astype(jnp.float32),
        lax.psum(shares[3].astype(jnp.bfloat16), "dp").astype(jnp.float32),
        lax.psum(shares[4].astype(jnp.bfloat16), "dp").astype(jnp.float32),
        lax.psum(shares[5].astype(jnp.bfloat16), "dp").astype(jnp.float32),
        lax.psum(shares[6].astype(jnp.bfloat16), "dp").astype(jnp.float32),
        lax.psum(shares[7].astype(jnp.bfloat16), "dp").astype(jnp.float32),
        lax.psum(shares[8].astype(jnp.bfloat16), "dp").astype(jnp.float32),
        lax.psum(shares[9].astype(jnp.bfloat16), "dp").astype(jnp.float32),
        lax.psum(shares[10].astype(jnp.bfloat16), "dp").astype(jnp.float32),
        lax.psum(shares[11].astype(jnp.bfloat16), "dp").astype(jnp.float32),
        lax.psum(shares[12].astype(jnp.bfloat16), "dp").astype(jnp.float32),
        lax.psum(shares[13].astype(jnp.bfloat16), "dp").astype(jnp.float32),
    )
    return (
        out_low,
        grad_input,
        grad_modulation,
        summed[0],
        summed[1],
        summed[2],
        summed[3],
        summed[4],
        summed[5],
        summed[6],
        summed[7],
        summed[8],
        summed[9],
        summed[10],
        summed[11],
        summed[12],
        summed[13],
    )


def solution(mesh):
    placed = (
        P("dp", "seq", None),
        P("dp", None, None),
        P("dp", "seq"),
        P("seq", None),
        P(),
        P("seq", None),
        P(),
        P("seq", None),
        P(),
        P("seq", None),
        P(),
        P("seq", None),
        P(),
        P("seq", None),
        P(),
        P("seq", None),
        P(),
        P("dp", "seq", None),
    )
    return jax.shard_map(
        local,
        mesh=mesh,
        in_specs=placed,
        out_specs=(
            P("dp", "seq", None),
            P("dp", "seq", None),
            P("dp", None, None),
            P("seq", None),
            P("seq"),
            P("seq", None),
            P("seq"),
            P("seq", None),
            P("seq"),
            P("seq", None),
            P("seq"),
            P("seq", None),
            P("seq"),
            P("seq", None),
            P("seq"),
            P("seq", None),
            P("seq"),
        ),
        check_vma=False,
    )
```

profile of v0, /device:TPU:9, one launch (start us, length us, event | category | flops | bytes accessed | tf_op | source)
XLA Modules:
  0.0 2512.1 jit_solution(13042411185265300625)
XLA Ops:
  16.7 12.5 fusion.63
  34.7 116.0 %all-gather.8.cloned.1.call-done = bf16[1152,3456]{1,0:T(8,128)(2,1)} async-done(((bf16[288,3456]{1,0:T(8,128)(2,1)}), bf16[1152,3456]{1,0:T(8,128)(2,1)}) %all-gather.8.cloned.1.call-update) | async-done | bytes 7962640 | tf_op jit(solution)/shard_map/all_gather | solution.py:161
  150.7 15.1 add_convert_fusion
  165.8 17.4 reshape.284
  183.2 16.5 copy.95
  213.3 295.1 %all-to-all-done = bf16[4,256,3,4,288]{1,0,4,2,3:T(4,128)(2,1)} async-done(((bf16[4,256,3,4,288]{1,0,4,2,3:T(4,128)(2,1)}), bf16[4,256,3,4,288]{1,0,4,2,3:T(4,128)(2,1)}, u32[]{:S(2)}, u32[]{:S(2)}) %all-to-all-start) | async-done | bytes 7077920 | tf_op jit(solution)/shard_map/all_to_all | solution.py:193
  508.4 11.3 copy.96
  519.7 13.2 reshape.268
  534.8 19.7 fusion.78
  554.5 14.7 fusion.1
  569.2 14.8 fusion.48
  587.4 16.6 fusion.79
  604.0 14.3 fusion
  618.3 14.9 fusion.49
  640.0 16.8 all-to-all-start.2
  660.0 123.1 %all-to-all-done.2 = bf16[4,1024,288]{2,0,1:T(4,128)(2,1)} async-done(((bf16[4,1024,288]{2,0,1:T(4,128)(2,1)}), bf16[4,1024,288]{2,0,1:T(4,128)(2,1)}, u32[]{:S(2)}, u32[]{:S(2)}) %all-to-all-start.2) | async-done | bytes 2359328 | tf_op jit(solution)/shard_map/all_to_all | solution.py:197
  813.1 19.4 fusion.83
  832.6 21.2 convolution_add_fusion
  860.3 11.7 all-gather.16.cloned.1.call-done
  882.2 139.2 %all-gather.18.cloned.1.call-done = bf16[2048,2048]{1,0:T(8,128)(2,1)} async-done(((bf16[512,2048]{1,0:T(8,128)(2,1)}), bf16[2048,2048]{1,0:T(8,128)(2,1)}) %all-gather.18.cloned.1.call-update) | async-done | bytes 8388624 | tf_op jit(solution)/shard_map/all_gather | solution.py:215
  1021.4 17.3 multiply_convert_fusion.4
  1038.7 46.4 %all-gather.20.cloned.1.call-done = bf16[2048,768]{1,0:T(8,128)(2,1)} async-done(((bf16[512,768]{1,0:T(8,128)(2,1)}), bf16[2048,768]{1,0:T(8,128)(2,1)}) %all-gather.20.cloned.1.call-update) | async-done | bytes 3145744 | tf_op jit(solution)/shard_map/all_gather | solution.py:216
  1104.5 16.3 fusion.81
  1134.0 28.8 %fusion.80 = (bf16[4608]{0:T(1024)(128)(2,1)}, bf16[1024,4608]{1,0:T(8,128)(2,1)}) fusion(f32[1024,4608]{1,0:T(8,128)} %fusion.83, f32[4608]{0:T(1024)S(1)} %convert_element_type.225, bf16[1024,1152]{1,0:T(8,128)(2,1)S(1)} %bitcast.195, bf16[4608,1152]{1,0:T(8,128)(2,1)} %all-gather.14.cloned.1.call-done), kind=kOutput, calls=%fused_computation.158 | convolution fusion | flops 10970722304 | bytes 41315328 | tf_op jit(solution)/shard_map/dot_general | solution.py:27
  1162.8 15.9 fusion.86
  1213.0 14.9 convolution_convert_fusion.5
  1228.4 22.9 convolution_convert_fusion
  1270.3 17.1 convolution_convert_fusion.1
  1287.4 71.2 %all-to-all-done.3 = bf16[4,256,4,288]{1,0,3,2:T(4,128)(2,1)S(1)} async-done(((bf16[4,256,4,288]{1,0,3,2:T(4,128)(2,1)}), bf16[4,256,4,288]{1,0,3,2:T(4,128)(2,1)S(1)}, u32[]{:S(2)}, u32[]{:S(2)}) %all-to-all-start.3) | async-done | bytes 2359328 | tf_op jit(solution)/shard_map/all_to_all | solution.py:255
  1366.5 15.6 fusion.19
  1382.1 23.5 multiply_reduce_fusion
  1405.6 23.5 multiply_reduce_fusion.1
  1429.1 16.2 add_convert_fusion.1
  1445.4 29.1 %multiply_convert_fusion = bf16[4,4,512,1024]{3,2,1,0:T(8,128)(2,1)} fusion(f32[4,4,512,1024]{3,2,1,0:T(8,128)} %get-tuple-element.74, f32[4,4,512,1024]{3,2,1,0:T(8,128)} %get-tuple-element.64, f32[4,4,512]{2,1,0:T(4,128)S(1)} %get-tuple-element.73, f32[4,4,512]{2,1,0:T(4,128)S(1)} %bitcast.204), kind=kLoop, calls=%fused_computation | loop fusion | flops 33554432 | bytes 83951616 | tf_op jit(solution)/shard_map/convert_element_type | solution.py:120
  1474.5 12.8 fusion.53
  1492.2 28.4 %multiply_convert_fusion.1 = bf16[4,4,512,1024]{3,2,1,0:T(8,128)(2,1)} fusion(f32[4,4,512,1024]{3,2,1,0:T(8,128)} %get-tuple-element.72, f32[4,4,512,1024]{3,2,1,0:T(8,128)} %get-tuple-element.66, f32[4,4,512]{2,1,0:T(4,128)S(1)} %get-tuple-element.71, f32[4,4,512]{2,1,0:T(4,128)S(1)} %bitcast.201), kind=kLoop, calls=%fused_computation.3 | loop fusion | flops 33554432 | bytes 83951616 | tf_op jit(solution)/shard_map/convert_element_type | solution.py:120
  1520.6 13.1 fusion.52
  1576.6 383.9 %all_to_all.75 = bf16[4,1024,3,1,288]{4,0,3,2,1:T(4,128)(2,1)} all-to-all(bf16[4,1024,3,1,288]{4,0,3,2,1:T(4,128)(2,1)S(1)} %pad_maximum_fusion), channel_id=1, replica_groups=mesh['dp'=8,'seq'=4] {'seq'}, dimensions={1} | all-to-all | bytes 14155776 | tf_op jit(solution)/shard_map/all_to_all | solution.py:257
  1960.4 16.7 copy.119
  1977.2 11.5 copy.110
  1994.1 10.9 convolution_convert_fusion.2
  2010.0 15.8 constant_dynamic-update-slice_fusion.1
  2051.9 14.1 convolution_convert_fusion.3
  2066.4 68.5 %reduce-scatter.12.cloned.1.call-done = bf16[288,4608]{1,0:T(8,128)(2,1)} async-done(((bf16[1152,4608]{1,0:T(8,128)(2,1)}), bf16[288,4608]{1,0:T(8,128)(2,1)}) %reduce-scatter.12.cloned.1.call-update) | async-done | bytes 2654224 | tf_op jit(solution)/shard_map/reduce_scatter | solution.py:291
  2134.9 140.9 %reduce-scatter.8.cloned.1.call-done = bf16[288,3456]{1,0:T(8,128)(2,1)} async-done(((bf16[1152,3456]{1,0:T(8,128)(2,1)}), bf16[288,3456]{1,0:T(8,128)(2,1)}) %reduce-scatter.8.cloned.1.call-update) | async-done | bytes 1990672 | tf_op jit(solution)/shard_map/reduce_scatter | solution.py:279
  2286.8 12.9 all-reduce.9
  2300.3 22.9 all-reduce.7
  2329.0 159.1 %all-reduce.15.cloned.1.call-done = (bf16[288,3456]{1,0:T(8,128)(2,1)}, bf16[288,1152]{1,0:T(8,128)(2,1)}, bf16[288,4608]{1,0:T(8,128)(2,1)}, bf16[1152,1152]{1,...) async-done(((bf16[288,3456]{1,0:T(8,128)(2,1)}, bf16[288,1152]{1,0:T(8,128)(2,1)}, bf16[288,4608]{1,0:T(8,128)(2,1)}, ...) | async-done | bytes 12025872 | tf_op jit(solution)/shard_map/psum | solution.py:323
  (313 shorter events, 299.5 us)
Async XLA Ops:
  7.2 143.4 %all-gather.8.cloned.1.call-start = ((), (), s32[]{:S(2)}) async-start(), calls=%async_computation.12 | async-start | bytes 9953280 | tf_op jit(solution)/shard_map/all_gather | solution.py:161
  8.0 785.8 %all-gather.10.cloned.1.call-start = ((), (), s32[]{:S(2)}) async-start(), calls=%async_computation.13 | async-start | bytes 3317760 | tf_op jit(solution)/shard_map/all_gather | solution.py:162
  8.7 804.4 %all-gather.12.cloned.1.call-start = ((), (), s32[]{:S(2)}) async-start(), calls=%async_computation.14 | async-start | bytes 13271040 | tf_op jit(solution)/shard_map/all_gather | solution.py:163
  9.5 823.1 %all-gather.14.cloned.1.call-start = ((), (), s32[]{:S(2)}) async-start(), calls=%async_computation.15 | async-start | bytes 13271040 | tf_op jit(solution)/shard_map/all_gather | solution.py:164
  10.7 189.1 %all-to-all-start.1 = ((bf16[4,256,1,4,1]{1,0,4,2,3:T(4,128)(2,1)}), bf16[4,256,1,4,1]{1,0,4,2,3:T(4,128)(2,1)S(1)}, u32[]{:S(2)}, u32[]{:S(2)}) async-start(bf16[4,256,1,4,1]{1,0,4,2,3:T(4,128)(2,1)} %broadcast_in_dim.31), calls=%async_computation.1 | async-start | bytes 16384 | tf_op jit(solution)/shard_map/all_to_all | solution.py:194
  199.7 308.6 %all-to-all-start = ((bf16[4,256,3,4,288]{1,0,4,2,3:T(4,128)(2,1)}), bf16[4,256,3,4,288]{1,0,4,2,3:T(4,128)(2,1)}, u32[]{:S(2)}, u32[]{:S(2)}) async-start(bf16[4,256,3,4,288]{1,0,4,2,3:T(4,128)(2,1)} %copy.95), calls=%async_computation | async-start | bytes 14155776 | tf_op jit(solution)/shard_map/all_to_all | solution.py:193
  208.4 663.7 %all-gather.16.cloned.1.call-start = ((), (), s32[]{:S(2)}) async-start(), calls=%async_computation.16 | async-start | bytes 5898240 | tf_op jit(solution)/shard_map/all_gather | solution.py:214
  209.0 812.4 %all-gather.18.cloned.1.call-start = ((), (), s32[]{:S(2)}) async-start(), calls=%async_computation.17 | async-start | bytes 10485760 | tf_op jit(solution)/shard_map/all_gather | solution.py:215
  534.8 52.7 %copy-start.11 = (bf16[4,1024,4,72]{1,3,2,0:T(8,128)(2,1)}, bf16[4,1024,4,72]{1,3,2,0:T(8,128)(2,1)S(1)}, u32[]{:S(2)}) copy-start(bf16[4,1024,4,72]{1,3,2,0:T(8,128)(2,1)S(1)} %slice_bitcast_fusion.1) | copy-start | bytes 7077892
  554.5 14.7 copy-start.29
  569.2 14.8 copy-start.31
  618.3 15.0 copy-start.35
  618.3 17.8 copy-start.14
  639.9 17.8 copy-start.56
  639.9 17.8 copy-start.13
  639.9 18.2 copy-start.50
  639.9 18.2 copy-start.51
  639.9 18.2 copy-start.52
  640.0 18.3 copy-start.53
  640.0 18.3 copy-start.47
  640.0 143.1 %all-to-all-start.2 = ((bf16[4,1024,288]{2,0,1:T(4,128)(2,1)}), bf16[4,1024,288]{2,0,1:T(4,128)(2,1)}, u32[]{:S(2)}, u32[]{:S(2)}) async-start(bf16[4,1024,288]{2,0,1:T(4,128)(2,1)} %pad_maximum_fusion.1), calls=%async_computation.2 | async-start | bytes 6291456 | tf_op jit(solution)/shard_map/all_to_all | solution.py:197
  656.8 428.3 %all-gather.20.cloned.1.call-start = ((), (), s32[]{:S(2)}) async-start(), calls=%async_computation.18 | async-start | bytes 3932160 | tf_op jit(solution)/shard_map/all_gather | solution.py:216
  657.5 1408.8 %reduce-scatter.10.cloned.1.call-start = ((), (), s32[]{:S(2)}) async-start(), calls=%async_computation.21 | async-start | bytes 3317760 | tf_op jit(solution)/shard_map/reduce_scatter | solution.py:285
  832.6 23.4 copy-start.3
  1096.8 24.1 slice-start.16
  1104.5 16.3 slice-start.17
  1128.3 55.6 %copy-start.8 = (f32[1024,1152]{1,0:T(8,128)}, f32[1024,1152]{1,0:T(8,128)S(1)}, u32[]{:S(2)}) copy-start(f32[1024,1152]{1,0:T(8,128)S(1)} %fusion.85) | copy-start | bytes 14155780
  1128.3 50.4 %slice-start = ((s8[4718592]{0:T(1024)(128)(4,1)}), s8[4194304]{0:T(1024)(128)(4,1)S(1)}, s32[]{:S(2)}) async-start(s8[4718592]{0:T(1024)(128)(4,1)} %bitcast.155), calls=%async_computation.28 | async-start | bytes 8388608
  1134.0 28.8 %copy-start.19 = (bf16[4,256,1152]{2,1,0:T(8,128)(2,1)}, bf16[4,256,1152]{2,1,0:T(8,128)(2,1)S(1)}, u32[]{:S(2)}) copy-start(bf16[4,256,1152]{2,1,0:T(8,128)(2,1)S(1)} %get-tuple-element.45) | copy-start | bytes 7077892
  1134.0 44.7 %slice-start.1 = ((s8[4718592]{0:T(1024)(128)(4,1)}), s8[524288]{0:T(1024)(128)(4,1)S(1)}, s32[]{:S(2)}) async-start(s8[4718592]{0:T(1024)(128)(4,1)} %bitcast.155), calls=%async_computation.29 | async-start | bytes 1048576
  1162.8 15.9 copy-start.27
  1162.8 15.9 copy-start.40
  1195.5 870.8 %reduce-scatter.20.cloned.1.call-start = ((), (), s32[]{:S(2)}) async-start(), calls=%async_computation.26 | async-start | bytes 3932160 | tf_op jit(solution)/shard_map/reduce_scatter | solution.py:315
  1203.7 862.6 %reduce-scatter.16.cloned.1.call-start = ((), (), s32[]{:S(2)}) async-start(), calls=%async_computation.24 | async-start | bytes 5898240 | tf_op jit(solution)/shard_map/reduce_scatter | solution.py:303
  1212.9 853.4 %reduce-scatter.18.cloned.1.call-start = ((), (), s32[]{:S(2)}) async-start(), calls=%async_computation.25 | async-start | bytes 10485760 | tf_op jit(solution)/shard_map/reduce_scatter | solution.py:309
  1227.9 838.5 %reduce-scatter.14.cloned.1.call-start = ((), (), s32[]{:S(2)}) async-start(), calls=%async_computation.23 | async-start | bytes 13271040 | tf_op jit(solution)/shard_map/reduce_scatter | solution.py:297
  1263.9 94.7 %all-to-all-start.3 = ((bf16[4,256,4,288]{1,0,3,2:T(4,128)(2,1)}), bf16[4,256,4,288]{1,0,3,2:T(4,128)(2,1)S(1)}, u32[]{:S(2)}, u32[]{:S(2)}) async-start(bf16[4,256,4,288]{1,0,3,2:T(4,128)(2,1)} %reshape.280), calls=%async_computation.3 | async-start | bytes 4718592 | tf_op jit(solution)/shard_map/all_to_all | solution.py:255
  1270.0 864.9 %reduce-scatter.12.cloned.1.call-start = ((), (), s32[]{:S(2)}) async-start(), calls=%async_computation.22 | async-start | bytes 13271040 | tf_op jit(solution)/shard_map/reduce_scatter | solution.py:291
  1287.4 988.5 %reduce-scatter.8.cloned.1.call-start = ((), (), s32[]{:S(2)}) async-start(), calls=%async_computation.20 | async-start | bytes 9953280 | tf_op jit(solution)/shard_map/reduce_scatter | solution.py:279
  2005.1 322.2 %all-reduce.13.cloned.1.call-start = ((), (), s32[]{:S(2)}) async-start(), calls=%async_computation.19 | async-start | bytes 442368 | tf_op jit(solution)/shard_map/psum | solution.py:277
  2005.4 25.6 %slice-start.8 = ((s8[4718592]{0:T(1024)(128)(4,1)}), s8[4194304]{0:T(1024)(128)(4,1)S(1)}, s32[]{:S(2)}) async-start(s8[4718592]{0:T(1024)(128)(4,1)} %bitcast.166), calls=%async_computation.36 | async-start | bytes 8388608
  2009.9 15.9 copy-start.6
  2009.9 15.9 copy-start.38
  2010.0 15.9 copy-start.43
  2010.0 21.0 slice-start.9
  2025.8 16.0 slice-start.4
  2025.8 18.8 slice-start.2
  2066.0 422.2 %all-reduce.15.cloned.1.call-start = ((), (), s32[]{:S(2)}) async-start(), calls=%async_computation.27 | async-start | bytes 24051712 | tf_op jit(solution)/shard_map/psum | solution.py:323
  (50 other events, 371.4 us)
Sparse Core Ops, SparseCore 0:
  9.6 140.9 all-gather.7
  152.3 54.3 all-gather.9
  208.2 323.2 all-gather.11
  533.0 247.1 all-gather.13
  781.6 90.4 all-gather.15
  873.5 147.8 all-gather.17
  1023.0 62.0 all-gather.19
  1195.7 52.8 reduce-scatter.9
  1250.8 103.8 reduce-scatter.19
  1356.9 85.3 reduce-scatter.15
  1444.6 145.6 reduce-scatter.17
  1592.5 360.9 reduce-scatter.13
  1955.9 178.9 reduce-scatter.11
  2137.1 138.6 reduce-scatter.7
  2278.7 33.9 all-reduce.12
  2317.4 170.6 all-reduce.14
where the time goes:
time: 2520 us; the launch traced here: 2510 us
  waiting for transfers between devices  1180 us (47%)
  matrix products  500 us (20%)
  blocking collectives  420 us (17%)
  other arithmetic  199 us (8%)
  local copies, waits for them, and re-layouts  161 us (6%)
  starting transfers between devices  38.4 us (2%)
    all_to_all x1, blocking collectives, local(): lax.all_to_all(grad_qkv_heads, 'seq', split_axis=1, concat_axis=3, tiled=...  384 us
    all_to_all x1, waiting for transfers between devices, local(): lax.all_to_all(qkv_low, 'seq', split_axis=3, concat_axis=1, tiled=True)  295 us
    psum x1, waiting for transfers between devices, local(): lax.psum(shares[0].astype(jnp.bfloat16), 'dp').astype(jnp.float32)  159 us
    reduce_scatter x1, waiting for transfers between devices, local(): lax.psum_scatter(grad_qkv_w.astype(jnp.bfloat16), 'seq', scatter_dimensio...  141 us
    all_gather x1, waiting for transfers between devices, local(): lax.all_gather(proj_mid_weight, 'seq', axis=0, tiled=True)  139 us
    all_to_all x1, waiting for transfers between devices, local(): lax.all_to_all(attended, 'seq', split_axis=1, concat_axis=2, tiled=True)  123 us
    all_gather x1, waiting for transfers between devices, local(): lax.all_gather(qkv_weight, 'seq', axis=0, tiled=True)  116 us
    dot_general x7, matrix products, matmul_nt(): lax.dot_general(left, right, (((1,), (1,)), ((), ())), preferred_element_...  98.6 us
  transfers between devices with their start and end apart: 20, of which 10 were waited for; matrix products, arithmetic and copies ran while one was open for 29% of the time, Pallas kernels for 0%

commit v1 on v0

v1 whole, which is shorter than its diff:
```python
import functools
import math

import jax
import jax.numpy as jnp
from jax import lax
from jax.experimental import pallas as pl
from jax.experimental.pallas import tpu as pltpu
from jax.sharding import PartitionSpec as P

HEAD_DIM = 72
EPSILON = 1e-06
GELU_COEF = 0.044715
MASKED = -1e30
LOG2E = 1.4426950408889634
LANES = 128
BF = jnp.bfloat16
F32 = jnp.float32


def dot_nn(left, right):
    return jnp.dot(left, right, preferred_element_type=F32)


def dot_tn(left, right):
    return lax.dot_general(left, right, (((0,), (0,)), ((), ())), preferred_element_type=F32)


def dot_nt(left, right):
    return lax.dot_general(left, right, (((1,), (1,)), ((), ())), preferred_element_type=F32)


def silu_grad(value):
    sigmoid_val = jax.nn.sigmoid(value)
    return sigmoid_val * (1.0 + value * (1.0 - sigmoid_val))


def gelu_grad(value):
    factor = math.sqrt(2.0 / math.pi)
    tangent = jnp.tanh(factor * (value + GELU_COEF * value * value * value))
    return 0.5 * (1.0 + tangent) + 0.5 * value * (1.0 - tangent * tangent) * factor * (
        1.0 + 3.0 * GELU_COEF * value * value
    )


def norm_stats(values):
    centred = values - jnp.mean(values, axis=-1, keepdims=True)
    inv_std = lax.rsqrt(jnp.mean(centred * centred, axis=-1, keepdims=True) + EPSILON)
    return (centred * inv_std, inv_std)


def norm_back(grad_normed, normed, inv_std):
    return inv_std * (
        grad_normed
        - jnp.mean(grad_normed, axis=-1, keepdims=True)
        - normed * jnp.mean(grad_normed * normed, axis=-1, keepdims=True)
    )


def head_window(head, width):
    tile = jnp.minimum((head * HEAD_DIM) // LANES, width // LANES - 2)
    base = pl.multiple_of(tile * LANES, LANES)
    offset = head * HEAD_DIM - base
    lane = lax.broadcasted_iota(jnp.int32, (1, 2 * LANES), 1)
    mine = (lane >= offset) & (lane < offset + HEAD_DIM)
    spare = jnp.where(offset >= 4, 0, LANES)
    return base, mine, lane - spare, offset >= 4


def with_segments(block, mine, lane, seg, hit, miss):
    code = jnp.where(lane == seg, hit, miss)
    code = jnp.where((lane >= 0) & (lane < 4), code, 0.0)
    return jnp.where(mine, block.astype(F32), code).astype(BF)


def attend_forward_kernel(q_ref, k_ref, v_ref, segq_ref, segk_ref, out_ref, total_ref, *, block):
    head = pl.program_id(0)
    width = q_ref.shape[1]
    base, mine, lane, low = head_window(head, width)
    window = pl.ds(base, 2 * LANES)
    factor = HEAD_DIM ** (-0.5) * LOG2E
    keys = with_segments(k_ref[:, window], mine, lane, segk_ref[...], 0.0, 1.0)
    values = jnp.where(
        mine, v_ref[:, window].astype(F32), jnp.where(lane == 0, 1.0, 0.0)
    ).astype(BF)
    values_t = values.T
    for start in range(0, q_ref.shape[0], block):
        rows = pl.ds(start, block)
        query = with_segments(q_ref[rows, window], mine, lane, segq_ref[rows, :], MASKED, 0.0)
        scores = dot_nt(keys, query) * factor
        top = jnp.max(scores, axis=0, keepdims=True)
        weights = jnp.exp2(scores - top).astype(BF)
        gathered = dot_nn(values_t, weights)
        total = jnp.where(low, gathered[0:1], gathered[LANES : LANES + 1])
        result = (gathered * (1.0 / total)).T
        out_ref[rows, window] = jnp.where(
            mine, result, out_ref[rows, window].astype(F32)
        ).astype(BF)
        total_ref[pl.ds(head, 1), rows] = top + jnp.log2(total)


def whole(shape):
    return pl.BlockSpec(shape, lambda *_: (0,) * len(shape))


def attend_forward(parts, seg_query, seg_keys, heads):
    (query, qcol), (keys, kcol), (values, vcol) = parts
    count, tokens = seg_query.shape[0], seg_keys.shape[0]
    width = heads * HEAD_DIM
    return pl.pallas_call(
        functools.partial(attend_forward_kernel, block=min(256, count)),
        grid=(heads,),
        in_specs=[
            pl.BlockSpec((count, width), lambda h: (0, qcol)),
            pl.BlockSpec((tokens, width), lambda h: (0, kcol)),
            pl.BlockSpec((tokens, width), lambda h: (0, vcol)),
            whole((count, 1)),
            whole((tokens, 1)),
        ],
        out_specs=[whole((count, width)), whole((heads, count))],
        out_shape=[
            jax.ShapeDtypeStruct((count, width), BF),
            jax.ShapeDtypeStruct((heads, count), F32),
        ],
        compiler_params=pltpu.CompilerParams(vmem_limit_bytes=56 * 1024 * 1024),
        cost_estimate=pl.CostEstimate(
            flops=heads * count * tokens * 4 * 256,
            bytes_accessed=2 * width * (2 * count + 2 * tokens),
            transcendentals=heads * count * tokens,
        ),
        name="attend_forward",
    )(query, keys, values, seg_query, seg_keys)


def attend_backward_kernel(
    q_ref, k_ref, v_ref, segq_ref, segk_ref, total_ref, out_ref, grad_ref, *rest, block, columns
):
    grads, dots = rest[:-1], rest[-1]
    dq_ref, dk_ref, dv_ref = grads if len(grads) == 3 else grads * 3
    head = pl.program_id(0)
    width = q_ref.shape[1]
    count = q_ref.shape[0]
    factor = HEAD_DIM ** (-0.5) * LOG2E

    @pl.when(head == 0)
    def _():
        row = lax.broadcasted_iota(jnp.int32, dots.shape[:1] + (width,), 0)
        col = lax.broadcasted_iota(jnp.int32, dots.shape[:1] + (width,), 1)
        pick = ((col >= row * HEAD_DIM) & (col < (row + 1) * HEAD_DIM)).astype(F32).astype(BF)
        for start in range(0, count, block):
            rows = pl.ds(start, block)
            product = out_ref[rows, :].astype(F32) * grad_ref[rows, :].astype(F32)
            high = product.astype(BF)
            rest_part = (product - high.astype(F32)).astype(BF)
            dots[:, rows] = dot_nt(pick, high) + dot_nt(pick, rest_part)

    base, mine, lane, _ = head_window(head, width)
    window = pl.ds(base, 2 * LANES)
    keys = with_segments(k_ref[:, window], mine, lane, segk_ref[...], 0.0, 1.0)
    keys_t = keys.T
    values = v_ref[:, window]
    grad_keys = None
    for start in range(0, count, block):
        rows = pl.ds(start, block)
        query = with_segments(q_ref[rows, window], mine, lane, segq_ref[rows, :], MASKED, 0.0)
        grad = jnp.where(mine, grad_ref[rows, window].astype(F32), 0.0).astype(BF)
        scores = dot_nt(keys, query) * factor
        probs = jnp.exp2(scores - total_ref[pl.ds(head, 1), rows])
        grad_probs = dot_nt(values, grad)
        grad_scores = (probs * (grad_probs - dots[pl.ds(head, 1), rows])).astype(BF)
        part_v = dot_nn(probs.astype(BF), grad)
        part_k = dot_nn(grad_scores, query)
        if grad_keys is None:
            grad_keys, grad_values = part_k, part_v
        else:
            grad_keys, grad_values = grad_keys + part_k, grad_values + part_v
        grad_query = (dot_nn(keys_t, grad_scores) * HEAD_DIM ** (-0.5)).T
        put(dq_ref, rows, base + columns[0], mine, grad_query)
    every = pl.ds(0, k_ref.shape[0])
    put(dk_ref, every, base + columns[1], mine, grad_keys * HEAD_DIM ** (-0.5))
    put(dv_ref, every, base + columns[2], mine, grad_values)


def put(ref, rows, base, mine, value):
    window = pl.ds(pl.multiple_of(base, LANES), 2 * LANES)
    ref[rows, window] = jnp.where(mine, value, ref[rows, window].astype(F32)).astype(BF)


def attend_backward(parts, seg_query, seg_keys, totals, out, grad, heads):
    (query, qcol), (keys, kcol), (values, vcol) = parts
    count, tokens = seg_query.shape[0], seg_keys.shape[0]
    width = heads * HEAD_DIM
    if count == tokens:
        shapes = [(count, 3 * width)]
        columns = (0, width, 2 * width)
    else:
        shapes = [(count, width), (tokens, width), (tokens, width)]
        columns = (0, 0, 0)
    return pl.pallas_call(
        functools.partial(attend_backward_kernel, block=min(256, count), columns=columns),
        grid=(heads,),
        in_specs=[
            pl.BlockSpec((count, width), lambda h: (0, qcol)),
            pl.BlockSpec((tokens, width), lambda h: (0, kcol)),
            pl.BlockSpec((tokens, width), lambda h: (0, vcol)),
            whole((count, 1)),
            whole((tokens, 1)),
            whole((heads, count)),
            whole((count, width)),
            whole((count, width)),
        ],
        out_specs=[whole(shape) for shape in shapes],
        out_shape=[jax.ShapeDtypeStruct(shape, BF) for shape in shapes],
        scratch_shapes=[pltpu.VMEM((heads, count), F32)],
        compiler_params=pltpu.CompilerParams(vmem_limit_bytes=60 * 1024 * 1024),
        cost_estimate=pl.CostEstimate(
            flops=heads * count * tokens * 10 * 256,
            bytes_accessed=2 * width * (4 * count + 4 * tokens),
            transcendentals=heads * count * tokens,
        ),
        name="attend_backward",
    )(query, keys, values, seg_query, seg_keys, totals, out, grad)


class Rows:
    def __init__(self, seq, rows):
        self.seq, self.rows = seq, rows
        self.share = seq // rows
        here = lax.axis_index("seq")
        self.row, self.part = here // self.share, here % self.share

    def device(self, row, part):
        return (row % self.rows) * self.share + part % self.share

    def shift_rows(self, shift):
        return [
            (self.device(r, p), self.device(r + shift, p))
            for r in range(self.rows)
            for p in range(self.share)
        ]

    def shift_parts(self, shift):
        return [
            (self.device(r, p), self.device(r, p + shift))
            for r in range(self.rows)
            for p in range(self.share)
        ]

    def to_rows(self, array):
        pieces = []
        for shift in range(self.rows):
            piece = lax.dynamic_index_in_dim(
                array, (self.row + shift) % self.rows, 0, keepdims=False
            )
            if shift:
                piece = lax.ppermute(piece, "seq", self.shift_rows(shift))
            pieces.append(piece)
        return pieces

    def to_spans(self, pieces):
        result = jnp.zeros((self.rows,) + pieces[0].shape, pieces[0].dtype)
        for shift, piece in enumerate(pieces):
            if shift:
                piece = lax.ppermute(piece, "seq", self.shift_rows(-shift))
            result = lax.dynamic_update_index_in_dim(
                result, piece, (self.row + shift) % self.rows, 0
            )
        return result

    def gather_parts(self, array):
        return jnp.concatenate(
            [array]
            + [
                lax.ppermute(array, "seq", self.shift_parts(shift))
                for shift in range(1, self.share)
            ],
            axis=0,
        )

    def sum_parts(self, array):
        count = array.shape[0] // self.share
        total = array[:count].astype(F32)
        for shift in range(1, self.share):
            piece = array[shift * count : (shift + 1) * count]
            total = total + lax.ppermute(piece, "seq", self.shift_parts(-shift)).astype(F32)
        return total.astype(array.dtype)

    def all_parts(self, array):
        total = array
        for shift in range(1, self.share):
            total = total + lax.ppermute(array, "seq", self.shift_parts(shift))
        return total


def gather_bundle(bundle):
    copies = lax.axis_size("dp")
    count = bundle.shape[0] // copies
    own = lax.dynamic_slice_in_dim(bundle, lax.axis_index("dp") * count, count, 0)
    full = lax.all_gather(own, ("seq", "dp"), axis=0, tiled=True)
    return full.reshape(lax.axis_size("seq"), bundle.shape[0], bundle.shape[1])


def reduce_bundle(bundle):
    flat = bundle.reshape(-1, bundle.shape[2])
    own = lax.psum_scatter(flat, ("seq", "dp"), scatter_dimension=0, tiled=True)
    return lax.all_gather(own, "dp", axis=0, tiled=True)


def stack_columns(weight, width):
    return [weight[:, start : start + width] for start in range(0, weight.shape[1], width)]


def split_rows(full, count):
    return [
        full[:, start : start + count].reshape(-1, full.shape[2])
        for start in range(0, full.shape[1], count)
    ]


def local(
    block_input,
    modulation,
    segment_ids,
    qkv_weight,
    query_value_bias,
    attn_out_weight,
    attn_out_bias,
    mlp_in_weight,
    mlp_in_bias,
    mlp_out_weight,
    mlp_out_bias,
    proj_in_weight,
    proj_in_bias,
    proj_mid_weight,
    proj_mid_bias,
    proj_out_weight,
    proj_out_bias,
    targets,
):
    rows, span, width = block_input.shape
    segs = modulation.shape[1]
    seq = lax.axis_size("seq")
    place = Rows(seq, rows)
    heads = width // HEAD_DIM
    hidden = mlp_in_weight.shape[1]
    inner = proj_mid_weight.shape[1]
    goal_width = targets.shape[2]
    tokens = rows * span
    share = place.share

    x_in = jnp.concatenate(place.to_rows(block_input), axis=0)
    seg_pieces = place.to_rows(segment_ids)
    segs_own = jnp.concatenate(seg_pieces, axis=0)
    seg_query = segs_own[:, None]
    seg_keys = place.gather_parts(seg_query) if share > 1 else seg_query
    goals = jnp.concatenate(place.to_rows(targets), axis=0)
    mod_row = lax.dynamic_index_in_dim(modulation, place.row, 0, keepdims=False)

    per = qkv_weight.shape[0]
    first = gather_bundle(
        jnp.concatenate(stack_columns(qkv_weight, width) + [attn_out_weight], axis=0)
    )
    second = gather_bundle(jnp.concatenate(stack_columns(mlp_in_weight, width), axis=0))
    third = gather_bundle(mlp_out_weight)
    half = inner // 2
    fourth = gather_bundle(
        jnp.concatenate(stack_columns(proj_in_weight, half), axis=0)
    )
    fifth = gather_bundle(proj_mid_weight)
    sixth = gather_bundle(proj_out_weight)
    w_q, w_k, w_v, w_attn = split_rows(first, per)
    w_qkv = jnp.concatenate([w_q, w_k, w_v], axis=1)
    w_mlp_in = jnp.concatenate(split_rows(second, per), axis=1)
    w_mlp_out = third.reshape(hidden, width)
    w_proj_in = jnp.concatenate(split_rows(fourth, per), axis=1)
    w_proj_mid = fifth.reshape(inner, inner)
    w_proj_out = sixth.reshape(inner, goal_width)

    one_hot = (segs_own[:, None] == jnp.arange(segs, dtype=jnp.int32)[None, :]).astype(BF)
    inputs = x_in.astype(F32)
    mod_tok = dot_nn(one_hot, mod_row)
    shift1, scale1, gate1, shift2, scale2, gate2 = (
        mod_tok[:, part * width : (part + 1) * width] for part in range(6)
    )
    normed1, inv_std1 = norm_stats(inputs)
    modulated1 = (normed1 * (1.0 + scale1) + shift1).astype(BF)
    bias_float = query_value_bias.astype(F32)
    full_bias = jnp.concatenate(
        [bias_float[:width], jnp.zeros((width,), F32), bias_float[width:]]
    )
    qkv = (dot_nn(modulated1, w_qkv) + full_bias).astype(BF)
    if share > 1:
        kv_all = place.gather_parts(qkv[:, width:])
        parts = ((qkv, 0), (kv_all, 0), (kv_all, 1))
    else:
        parts = ((qkv, 0), (qkv, 1), (qkv, 2))
    attended, totals = attend_forward(parts, seg_query, seg_keys, heads)
    branch = dot_nn(attended, w_attn) + attn_out_bias.astype(F32)
    middle = inputs + gate1 * branch
    normed2, inv_std2 = norm_stats(middle)
    modulated2 = (normed2 * (1.0 + scale2) + shift2).astype(BF)
    hmid = dot_nn(modulated2, w_mlp_in) + mlp_in_bias.astype(F32)
    act_mid = jax.nn.gelu(hmid, approximate=True).astype(BF)
    mlp_branch = dot_nn(act_mid, w_mlp_out) + mlp_out_bias.astype(F32)
    out_low = (middle + gate2 * mlp_branch).astype(BF)
    hidden1 = dot_nn(out_low, w_proj_in) + proj_in_bias.astype(F32)
    act1 = jax.nn.silu(hidden1).astype(BF)
    hidden2 = dot_nn(act1, w_proj_mid) + proj_mid_bias.astype(F32)
    act2 = jax.nn.silu(hidden2).astype(BF)
    feats = dot_nn(act2, w_proj_out) + proj_out_bias.astype(F32)
    goals = goals.astype(F32)
    inv_feat = lax.rsqrt(jnp.sum(feats * feats, axis=-1, keepdims=True) + EPSILON)
    feat_unit = feats * inv_feat
    goal_unit = goals * lax.rsqrt(jnp.sum(goals * goals, axis=-1, keepdims=True) + EPSILON)
    cosine = jnp.sum(feat_unit * goal_unit, axis=-1, keepdims=True)
    loss_weight = 0.5 * goal_width
    grad_feats = (-loss_weight * inv_feat * (goal_unit - cosine * feat_unit)).astype(BF)

    def blocks(grad, cut):
        low = grad.astype(BF).reshape(seq, grad.shape[0] // seq, grad.shape[1])
        return [low[:, :, start : start + cut] for start in range(0, grad.shape[1], cut)]

    sixth_sum = reduce_bundle(
        jnp.concatenate(blocks(dot_tn(act2, grad_feats), goal_width), axis=1)
    )
    bias_out = jnp.sum(grad_feats.astype(F32), axis=0)
    grad_hidden2 = (dot_nt(grad_feats, w_proj_out) * silu_grad(hidden2)).astype(BF)
    fifth_sum = reduce_bundle(jnp.concatenate(blocks(dot_tn(act1, grad_hidden2), inner), axis=1))
    bias_mid = jnp.sum(grad_hidden2.astype(F32), axis=0)
    grad_hidden1 = (dot_nt(grad_hidden2, w_proj_mid) * silu_grad(hidden1)).astype(BF)
    fourth_sum = reduce_bundle(jnp.concatenate(blocks(dot_tn(out_low, grad_hidden1), half), axis=1))
    bias_in = jnp.sum(grad_hidden1.astype(F32), axis=0)
    grad_output = dot_nt(grad_hidden1, w_proj_in)
    grad_gate2 = grad_output * mlp_branch
    grad_mlp = (grad_output * gate2).astype(BF)
    third_sum = reduce_bundle(jnp.concatenate(blocks(dot_tn(act_mid, grad_mlp), width), axis=1))
    bias_ff_out = jnp.sum(grad_mlp.astype(F32), axis=0)
    grad_hmid = (dot_nt(grad_mlp, w_mlp_out) * gelu_grad(hmid)).astype(BF)
    second_sum = reduce_bundle(jnp.concatenate(blocks(dot_tn(modulated2, grad_hmid), width), axis=1))
    bias_ff_in = jnp.sum(grad_hmid.astype(F32), axis=0)
    grad_modulated2 = dot_nt(grad_hmid, w_mlp_in)
    grad_middle = grad_output + norm_back(grad_modulated2 * (1.0 + scale2), normed2, inv_std2)
    grad_gate1 = grad_middle * branch
    grad_branch = (grad_middle * gate1).astype(BF)
    grad_attn_w = dot_tn(attended, grad_branch)
    bias_attn = jnp.sum(grad_branch.astype(F32), axis=0)
    grad_attended = dot_nt(grad_branch, w_attn).astype(BF)
    grads = attend_backward(parts, seg_query, seg_keys, totals, attended, grad_attended, heads)
    if share > 1:
        grad_qkv = jnp.concatenate(
            [grads[0], place.sum_parts(grads[1]), place.sum_parts(grads[2])], axis=1
        )
    else:
        grad_qkv = grads[0]
    first_sum = reduce_bundle(
        jnp.concatenate(
            blocks(dot_tn(modulated1, grad_qkv), width) + blocks(grad_attn_w, width), axis=1
        )
    )
    column_sums = jnp.sum(grad_qkv.astype(F32), axis=0)
    bias_qv = jnp.concatenate([column_sums[:width], column_sums[2 * width :]])
    grad_modulated1 = dot_nt(grad_qkv, w_qkv)
    grad_input = grad_middle + norm_back(grad_modulated1 * (1.0 + scale1), normed1, inv_std1)

    def by_segment(value):
        return dot_tn(one_hot, value.astype(BF))

    grad_mod = jnp.concatenate(
        [
            by_segment(grad_modulated1),
            by_segment(grad_modulated1 * normed1),
            by_segment(grad_gate1),
            by_segment(grad_modulated2),
            by_segment(grad_modulated2 * normed2),
            by_segment(grad_gate2),
        ],
        axis=-1,
    )
    grad_mod = place.all_parts(grad_mod)
    grad_modulation = lax.all_gather(grad_mod.astype(BF), "seq", axis=0)[:: share].astype(F32)

    def back(value):
        return place.to_spans(
            [value[shift * span : (shift + 1) * span] for shift in range(rows)]
        )

    block_out = back(out_low)
    grad_input = back(grad_input.astype(BF)).astype(F32)

    biases = [bias_qv, bias_attn, bias_ff_in, bias_ff_out, bias_in, bias_mid, bias_out]
    packed = jnp.concatenate([bias.reshape(seq, -1) for bias in biases], axis=1)
    packed = lax.psum(packed, ("dp", "seq"))
    packed = lax.dynamic_index_in_dim(packed, lax.axis_index("seq"), 0, keepdims=False)
    shares = []
    start = 0
    for bias in biases:
        stop = start + bias.shape[0] // seq
        shares.append(packed[start:stop])
        start = stop

    def columns_of(total, count):
        return [total[start : start + count].astype(F32) for start in range(0, total.shape[0], count)]

    first_parts = columns_of(first_sum, per)
    return (
        block_out,
        grad_input,
        grad_modulation,
        jnp.concatenate(first_parts[:3], axis=1),
        shares[0],
        first_parts[3],
        shares[1],
        jnp.concatenate(columns_of(second_sum, per), axis=1),
        shares[2],
        third_sum.astype(F32),
        shares[3],
        jnp.concatenate(columns_of(fourth_sum, per), axis=1),
        shares[4],
        fifth_sum.astype(F32),
        shares[5],
        sixth_sum.astype(F32),
        shares[6],
    )


def solution(mesh):
    placed = (
        P("dp", "seq", None),
        P("dp", None, None),
        P("dp", "seq"),
        P("seq", None),
        P(),
        P("seq", None),
        P(),
        P("seq", None),
        P(),
        P("seq", None),
        P(),
        P("seq", None),
        P(),
        P("seq", None),
        P(),
        P("seq", None),
        P(),
        P("dp", "seq", None),
    )
    return jax.shard_map(
        local,
        mesh=mesh,
        in_specs=placed,
        out_specs=(
            P("dp", "seq", None),
            P("dp", "seq", None),
            P("dp", None, None),
        )
        + (P("seq", None), P("seq")) * 7,
        check_vma=False,
    )
```

time: 2520 us -> 1590 us (0.63)
  waiting for transfers between devices: 1180 us -> 805 us
  blocking collectives: 420 us -> 162 us
  matrix products: 500 us -> 313 us
  Pallas kernels: 0 us -> 114 us
  other arithmetic: 199 us -> 85.4 us
  local copies, waits for them, and re-layouts: 161 us -> 75.9 us
    all_to_all x4 -> x0, waiting for transfers between devices: 489 us -> none  [the longest x1 295 us: local(): lax.all_to_all(qkv_low, 'seq', split_axis=3, concat_axis=1, tiled=True)]
    all_to_all x1 -> x0, blocking collectives: 384 us -> none  [local(): lax.all_to_all(grad_qkv_heads, 'seq', split_axis=1, concat_axis=3, tiled=...]
    dot_general x35 -> x28, matrix products: 500 us -> 313 us  [the longest x8 114 us: dot_nn(): return jnp.dot(left, right, preferred_element_type=F32)]
    reduce_scatter x7 -> x6, waiting for transfers between devices: 210 us -> 377 us  [reduce_bundle(): own = lax.psum_scatter(flat, ('seq', 'dp'), scatter_dimension=0, tiled=True)]
    psum x2 -> x0, waiting for transfers between devices: 159 us -> none  [the longest x1 159 us: local(): lax.psum(shares[0].astype(jnp.bfloat16), 'dp').astype(jnp.float32)]
    psum x1, blocking collectives: 22.9 us -> 138 us  [local(): packed = lax.psum(packed, ('dp', 'seq'))]
    pallas_call x0 -> x2, Pallas kernels: none -> 114 us  [the longest x1 66.8 us: attend_backward(): pl.pallas_call(functools.partial(attend_backward_kernel, block=min(256, c...]
    ppermute x0 -> x15, waiting for transfers between devices: none -> 82.2 us  [the longest x9 82.2 us: to_rows(): piece = lax.ppermute(piece, 'seq', self.shift_rows(shift))]
  transfers between devices with their start and end apart: 20 -> 32, of which waited for: 10 -> 17; matrix products, arithmetic and copies ran while one was open for 29% -> 26% of each run, Pallas kernels for 0% -> 7%
where the time goes in v1:
time: 1590 us
  waiting for transfers between devices  805 us (51%)
  matrix products  313 us (20%)
  blocking collectives  162 us (10%)
  Pallas kernels  114 us (7%)
  other arithmetic  85.4 us (5%)
  local copies, waits for them, and re-layouts  75.9 us (5%)
  starting transfers between devices  17.4 us (1%)
    reduce_scatter x6, waiting for transfers between devices, reduce_bundle(): own = lax.psum_scatter(flat, ('seq', 'dp'), scatter_dimension=0, tiled=True)  377 us
    all_gather x6, waiting for transfers between devices, gather_bundle(): full = lax.all_gather(own, ('seq', 'dp'), axis=0, tiled=True)  223 us
    psum x1, blocking collectives, local(): packed = lax.psum(packed, ('dp', 'seq'))  138 us
    all_gather x5, waiting for transfers between devices, reduce_bundle(): return lax.all_gather(own, 'dp', axis=0, tiled=True)  122 us
    dot_general x8, matrix products, dot_nn(): return jnp.dot(left, right, preferred_element_type=F32)  114 us
    dot_general x7, matrix products, dot_nt(): lax.dot_general(left, right, (((1,), (1,)), ((), ())), preferred_element_...  107 us
    dot_general x13, matrix products, dot_tn(): lax.dot_general(left, right, (((0,), (0,)), ((), ())), preferred_element_...  92.6 us
    ppermute x9, waiting for transfers between devices, to_rows(): piece = lax.ppermute(piece, 'seq', self.shift_rows(shift))  82.2 us
  transfers between devices with their start and end apart: 32, of which 17 were waited for; matrix products, arithmetic and copies ran while one was open for 26% of the time, Pallas kernels for 7%

profile of v1, /device:TPU:9, one launch (start us, length us, event | category | flops | bytes accessed | tf_op | source)
XLA Modules:
  0.0 1588.4 jit_solution(6714444866136874013)
XLA Ops:
  39.4 57.9 %collective-permute-done.10 = bf16[256,768]{0,1:T(8,128)(2,1)S(1)} collective-permute-done((bf16[256,768]{0,1:T(8,128)(2,1)}, bf16[256,768]{0,1:T(8,128)(2,1)S(1)}, u32[]{:S(2)}, u32[]{:S(2)}) %collective-permute-start.10) | collective-permute-done | bytes 393248 | tf_op jit(solution)/shard_map/ppermute | solution.py:256
  97.4 12.7 fusion.91
  111.2 24.3 %collective-permute-done.11 = bf16[256,768]{0,1:T(8,128)(2,1)} collective-permute-done((bf16[256,768]{0,1:T(8,128)(2,1)}, bf16[256,768]{0,1:T(8,128)(2,1)}, u32[]{:S(2)}, u32[]{:S(2)}) %collective-permute-start.11) | collective-permute-done | bytes 393248 | tf_op jit(solution)/shard_map/ppermute | solution.py:256
  140.4 6.0 fusion.22
  146.5 5.2 fusion.128
  151.7 72.9 %all-gather.12.cloned.1.call-done = bf16[4608,1152]{1,0:T(8,128)(2,1)} async-done(((bf16[144,1152]{1,0:T(8,128)(2,1)}), bf16[4608,1152]{1,0:T(8,128)(2,1)}) %all-gather.12.cloned.1.call-update) | async-done | bytes 10616848 | tf_op jit(solution)/shard_map/all_gather | solution.py:299
  224.5 6.1 fusion.125
  233.0 12.1 add_convert_fusion.q_ref.k_ref.v_ref
  245.1 47.4 %attend_forward.1 = (bf16[1024,1152]{1,0:T(8,128)(2,1)}, f32[16,1024]{1,0:T(8,128)}) custom-call(bf16[1024,3456]{1,0:T(8,128)(2,1)} %add_convert_fusion.q_ref.k_ref.v_ref, bf16[1024,3456]{1,0:T(8,128)(2,1)} %add_convert_fusion.q_ref.k_ref.v_ref, bf16[1024,3456]{1,0:T(8,128)(2,1)} %add_convert_fusion.q_ref.k_ref.v_ref, s32[1024,1]{1,0:T(8,128)} %copy.47.segq_ref.segk_ref, ...), custom_call_target="tpu_custom_call" | custom-call | flops 17179869184 | bytes 9437184 | tf_op jit(solution)/shard_map/attend_forward/pallas_call | solution.py:110
  292.5 9.7 fusion.122
  304.4 5.8 fusion.30
  313.1 7.2 fusion.124
  320.3 20.0 %fusion.88 = f32[1024,4608]{1,0:T(8,128)} fusion(bf16[1024,1152]{1,0:T(8,128)(2,1)} %fusion.30, bf16[1152,1152]{1,0:T(8,128)(2,1)} %bitcast.151, bf16[1152,1152]{1,0:T(8,128)(2,1)} %bitcast.153, bf16[1152,1152]{1,0:T(8,128)(2,1)} %bitcast.155, bf16[1152,1152]{1,0:T(8,128)(2,1)S(1)} %bitcast.149), kind=kOutput, calls=%fused_computation.132 | convolution fusion | flops 10914103296 | bytes 31850496 | tf_op jit(solution)/shard_map/dot_general | solution.py:22
  340.3 61.7 %all-gather.16.cloned.1.call-done = bf16[4608,1152]{1,0:T(8,128)(2,1)} async-done(((bf16[144,1152]{1,0:T(8,128)(2,1)}), bf16[4608,1152]{1,0:T(8,128)(2,1)}) %all-gather.16.cloned.1.call-update) | async-done | bytes 10616848 | tf_op jit(solution)/shard_map/all_gather | solution.py:299
  402.0 24.7 %add_convert_fusion.1 = (bf16[1024,1152]{1,0:T(8,128)(2,1)S(1)}, f32[1024,1152]{1,0:T(8,128)}) fusion(f32[1024,1152]{1,0:T(8,128)} %copy-done.2, f32[1024,6912]{1,0:T(8,128)} %fusion.91, f32[1152]{0:T(1024)S(1)} %convert_element_type.176, bf16[4608,1152]{1,0:T(8,128)(2,1)} %all-gather.16.cloned.1.call-done, f32[1024,4608]{1,0:T(8,128)} %fusion.88, ...), kind=kOutput, calls=%fused_computation.73 | convolution fusion | flops 10923540480 | bytes 46029312 | tf_op jit(solution)/shard_map/dot_general | solution.py:22
  426.7 11.0 fusion.41
  437.7 43.3 %all-gather.20.cloned.1.call-done = bf16[2048,2048]{1,0:T(8,128)(2,1)} async-done(((bf16[64,2048]{1,0:T(8,128)(2,1)}), bf16[2048,2048]{1,0:T(8,128)(2,1)}) %all-gather.20.cloned.1.call-update) | async-done | bytes 8388624 | tf_op jit(solution)/shard_map/all_gather | solution.py:299
  480.9 17.3 %multiply_convert_fusion.2 = (bf16[1024,2048]{1,0:T(8,128)(2,1)}, f32[1024,2048]{1,0:T(8,128)}) fusion(f32[2048]{0:T(1024)S(1)} %convert_element_type.180, bf16[2048,2048]{1,0:T(8,128)(2,1)} %all-gather.20.cloned.1.call-done, f32[1024,2048]{1,0:T(8,128)} %fusion.41, f32[2048]{0:T(1024)S(1)} %convert_element_type.178), kind=kOutput, calls=%fused_computation.31 | convolution fusion | flops 8615100416 | bytes 29376512 | tf_op jit(solution)/shard_map/dot_general | solution.py:22
  498.2 42.0 %all-gather.22.cloned.1.call-done = bf16[2048,768]{1,0:T(8,128)(2,1)} async-done(((bf16[64,768]{1,0:T(8,128)(2,1)}), bf16[2048,768]{1,0:T(8,128)(2,1)}) %all-gather.22.cloned.1.call-update) | async-done | bytes 3145744 | tf_op jit(solution)/shard_map/all_gather | solution.py:299
  540.2 6.4 multiply_reduce_fusion.2
  552.1 7.9 convert_reduce_fusion.2
  560.1 14.8 convert_reduce_fusion.3
  574.9 5.4 convolution_convert_fusion.3
  585.1 11.3 convert_reduce_fusion.5
  597.8 22.5 %convolution_convert_fusion = bf16[4608,1152]{1,0:T(8,128)(2,1)} fusion(bf16[1024,1152]{1,0:T(8,128)(2,1)S(1)} %get-tuple-element.30, f32[1024,4608]{1,0:T(8,128)} %fusion.88, f32[4608]{0:T(1024)S(1)} %convert_element_type.174), kind=kOutput, calls=%fused_computation.3 | convolution fusion | flops 10924130304 | bytes 31868928 | tf_op jit(solution)/shard_map/dot_general | solution.py:26
  620.4 29.5 %convert_reduce_fusion = (f32[4608]{0:T(1024)}, bf16[1024,4608]{1,0:T(8,128)(2,1)}) fusion(f32[1024,4608]{1,0:T(8,128)} %fusion.88, f32[4608]{0:T(1024)S(1)} %convert_element_type.174, bf16[1024,1152]{1,0:T(8,128)(2,1)} %copy-done.69, bf16[4608,1152]{1,0:T(8,128)(2,1)} %all-gather.16.cloned.1.call-done), kind=kOutput, calls=%fused_computation.20 | convolution fusion | flops 10975440896 | bytes 41324544 | tf_op jit(solution)/shard_map/dot_general | solution.py:30
  649.9 21.3 %fusion.116 = (f32[1024]{0:T(1024)S(1)}, f32[1024]{0:T(1024)S(1)}, f32[1024,1152]{1,0:T(8,128)S(1)}) fusion(f32[1024,6912]{1,0:T(8,128)} %fusion.91, f32[1024]{0:T(1024)S(1)} %copy-done.44, f32[1024,1152]{1,0:T(8,128)} %copy-done.2, f32[1024]{0:T(1024)S(1)} %copy-done.39, bf16[1024,4608]{1,0:T(8,128)(2,1)} %get-tuple-element.111, ...), kind=kOutput, calls=%fused_computation.207 | convolution fusion | flops 10922358784 | bytes 34226176 | tf_op jit(solution)/shard_map/dot_general | solution.py:30
  671.3 12.4 convert_reduce_fusion.6
  693.2 66.8 %attend_backward.1 = bf16[1024,3456]{1,0:T(8,128)(2,1)} custom-call(bf16[1024,3456]{1,0:T(8,128)(2,1)} %add_convert_fusion.q_ref.k_ref.v_ref, bf16[1024,3456]{1,0:T(8,128)(2,1)} %add_convert_fusion.q_ref.k_ref.v_ref, bf16[1024,3456]{1,0:T(8,128)(2,1)} %add_convert_fusion.q_ref.k_ref.v_ref, s32[1024,1]{1,0:T(8,128)} %copy.47.segq_ref.segk_ref, ...), custom_call_target="tpu_custom_call" | custom-call | flops 42949672960 | bytes 18874368 | tf_op jit(solution)/shard_map/attend_backward/pallas_call | solution.py:199
  760.1 12.3 convolution_convert_fusion.2
  780.8 13.8 convolution_convert_fusion.1
  801.2 14.9 convolution_convert_fusion.4
  817.5 7.5 convolution_convert_fusion.7
  825.8 10.2 reduce-scatter.11.cloned.1.call-done
  840.8 17.2 %fusion.117 = (f32[1024]{0:T(1024)S(1)}, f32[1024]{0:T(1024)S(1)}, f32[1024,1152]{1,0:T(8,128)}) fusion(f32[1024,6912]{1,0:T(8,128)} %fusion.91, f32[1024]{0:T(1024)S(1)} %copy-done.50, f32[1024]{0:T(1024)S(1)} %copy-done.42, bf16[256,1152]{1,0:T(8,128)(2,1)S(1)} %copy-done.12, bf16[256,1152]{1,0:T(8,128)(2,1)S(1)} %copy-done.10, ...), kind=kOutput, calls=%fused_computation.208 | convolution fusion | flops 8195307520 | bytes 26853376 | tf_op jit(solution)/shard_map/dot_general | solution.py:30
  858.0 126.2 %reduce-scatter.7.cloned.1.call-done = bf16[144,1152]{1,0:T(8,128)(2,1)} async-done(((bf16[4608,1152]{1,0:T(8,128)(2,1)}), bf16[144,1152]{1,0:T(8,128)(2,1)}) %reduce-scatter.7.cloned.1.call-update) | async-done | bytes 331792 | tf_op jit(solution)/shard_map/reduce_scatter | solution.py:305
  998.1 11.1 all_gather.46
  1010.0 6.0 fusion.27
  1016.0 116.1 %reduce-scatter.9.cloned.1.call-done = bf16[144,1152]{1,0:T(8,128)(2,1)} async-done(((bf16[4608,1152]{1,0:T(8,128)(2,1)}), bf16[144,1152]{1,0:T(8,128)(2,1)}) %reduce-scatter.9.cloned.1.call-update) | async-done | bytes 331792 | tf_op jit(solution)/shard_map/reduce_scatter | solution.py:305
  1140.9 138.1 %psum.7 = f32[4,3520]{1,0:T(4,128)S(1)} all-reduce(f32[4,3520]{1,0:T(4,128)S(1)} %concatenate.114), channel_id=1, replica_groups=mesh['dp'=8,'seq'=4] {'dp','seq'}, use_global_device_ids=true, to_apply=%region_19.20 | all-reduce | flops 14080 | bytes 112640 | tf_op jit(solution)/shard_map/psum | solution.py:492
  1297.7 9.2 reduce-scatter.15.cloned.1.call-done
  1308.9 114.9 %reduce-scatter.17.cloned.1.call-done = bf16[64,768]{1,0:T(8,128)(2,1)} async-done(((bf16[2048,768]{1,0:T(8,128)(2,1)}), bf16[64,768]{1,0:T(8,128)(2,1)}) %reduce-scatter.17.cloned.1.call-update) | async-done | bytes 98320 | tf_op jit(solution)/shard_map/reduce_scatter | solution.py:305
  1423.8 13.1 all_gather.52
  1438.1 13.1 all-gather.30.cloned.1.call-done
  1454.2 29.2 %all-gather.28.cloned.1.call-done = bf16[1152,1152]{1,0:T(8,128)(2,1)} async-done(((bf16[144,1152]{1,0:T(8,128)(2,1)}), bf16[1152,1152]{1,0:T(8,128)(2,1)}) %all-gather.28.cloned.1.call-update) | async-done | bytes 2654224 | tf_op jit(solution)/shard_map/all_gather | solution.py:306
  1487.8 27.7 %all-gather.24.cloned.1.call-done = bf16[1152,1152]{1,0:T(8,128)(2,1)} async-done(((bf16[144,1152]{1,0:T(8,128)(2,1)}), bf16[1152,1152]{1,0:T(8,128)(2,1)}) %all-gather.24.cloned.1.call-update) | async-done | bytes 2654224 | tf_op jit(solution)/shard_map/all_gather | solution.py:306
  1520.7 27.0 %all-gather.26.cloned.1.call-done = bf16[1152,1152]{1,0:T(8,128)(2,1)} async-done(((bf16[144,1152]{1,0:T(8,128)(2,1)}), bf16[1152,1152]{1,0:T(8,128)(2,1)}) %all-gather.26.cloned.1.call-update) | async-done | bytes 2654224 | tf_op jit(solution)/shard_map/all_gather | solution.py:306
  1552.3 25.2 %all-gather.32.cloned.1.call-done = bf16[512,2048]{1,0:T(8,128)(2,1)} async-done(((bf16[64,2048]{1,0:T(8,128)(2,1)}), bf16[512,2048]{1,0:T(8,128)(2,1)}) %all-gather.32.cloned.1.call-update) | async-done | bytes 2097168 | tf_op jit(solution)/shard_map/all_gather | solution.py:306
  (333 shorter events, 155.0 us)
Async XLA Ops:
  7.2 139.3 %all-gather.18.cloned.1.call-start = ((), (), s32[]{:S(2)}) async-start(), calls=%async_computation.9 | async-start | bytes 4866048 | tf_op jit(solution)/shard_map/all_gather | solution.py:299
  11.2 213.3 %all-gather.12.cloned.1.call-start = ((), (), s32[]{:S(2)}) async-start(), calls=%async_computation.6 | async-start | bytes 10948608 | tf_op jit(solution)/shard_map/all_gather | solution.py:299
  14.3 298.8 %all-gather.14.cloned.1.call-start = ((), (), s32[]{:S(2)}) async-start(), calls=%async_computation.7 | async-start | bytes 10948608 | tf_op jit(solution)/shard_map/all_gather | solution.py:299
  17.7 384.3 %all-gather.16.cloned.1.call-start = ((), (), s32[]{:S(2)}) async-start(), calls=%async_computation.8 | async-start | bytes 10948608 | tf_op jit(solution)/shard_map/all_gather | solution.py:299
  18.5 462.4 %all-gather.20.cloned.1.call-start = ((), (), s32[]{:S(2)}) async-start(), calls=%async_computation.10 | async-start | bytes 8650752 | tf_op jit(solution)/shard_map/all_gather | solution.py:299
  20.3 519.9 %all-gather.22.cloned.1.call-start = ((), (), s32[]{:S(2)}) async-start(), calls=%async_computation.11 | async-start | bytes 3244032 | tf_op jit(solution)/shard_map/all_gather | solution.py:299
  20.5 15.3 collective-permute-start.3
  21.8 14.0 collective-permute-start.4
  22.9 13.6 collective-permute-start.5
  27.1 265.4 %copy-start.5 = (bf16[256,1152]{1,0:T(8,128)(2,1)}, bf16[256,1152]{1,0:T(8,128)(2,1)S(1)}, u32[]{:S(2)}) copy-start(bf16[256,1152]{1,0:T(8,128)(2,1)S(1)} %get-tuple-element.73) | copy-start | bytes 1769476
  27.1 110.4 %collective-permute-start = (bf16[256,1152]{1,0:T(8,128)(2,1)}, bf16[256,1152]{1,0:T(8,128)(2,1)S(1)}, u32[]{:S(2)}, u32[]{:S(2)}) collective-permute-start(bf16[256,1152]{1,0:T(8,128)(2,1)} %get-tuple-element.74), channel_id=1, source_target_pairs={{0,1},{1,2},{2,3},{3,0},{4,5},{5,6},{6,7},{7,4},{8,9},{9,10},{10,1... | collective-permute-start | bytes 1769480 | tf_op jit(solution)/shard_map/ppermute | solution.py:256
  28.2 69.0 %collective-permute-start.10 = (bf16[256,768]{0,1:T(8,128)(2,1)}, bf16[256,768]{0,1:T(8,128)(2,1)S(1)}, u32[]{:S(2)}, u32[]{:S(2)}) collective-permute-start(bf16[256,768]{0,1:T(8,128)(2,1)} %bitcast.163), channel_id=1, source_target_pairs={{0,2},{1,3},{2,0},{3,1},{4,6},{5,7},{6,4},{7,5},{8,10},{9,11},{10,... | collective-permute-start | bytes 1179656 | tf_op jit(solution)/shard_map/ppermute | solution.py:256
  32.9 792.2 %reduce-scatter.13.cloned.1.call-start = ((), (), s32[]{:S(2)}) async-start(), calls=%async_computation.18 | async-start | bytes 4866048 | tf_op jit(solution)/shard_map/reduce_scatter | solution.py:305
  33.1 527.0 %copy-start.56 = (f32[2048]{0:T(1024)}, f32[2048]{0:T(1024)S(1)}, u32[]{:S(2)}) copy-start(f32[2048]{0:T(1024)S(1)} %convert_element_type.178) | copy-start | bytes 24580
  35.7 99.8 %copy-start.13 = (bf16[1,256,768]{1,2,0:T(8,128)(2,1)}, bf16[1,256,768]{1,2,0:T(8,128)(2,1)S(1)}, u32[]{:S(2)}) copy-start(bf16[1,256,768]{1,2,0:T(8,128)(2,1)S(1)} %copy.49) | copy-start | bytes 1179652
  35.7 101.8 %collective-permute-start.1 = (bf16[256,1152]{1,0:T(8,128)(2,1)}, bf16[256,1152]{1,0:T(8,128)(2,1)S(1)}, u32[]{:S(2)}, u32[]{:S(2)}) collective-permute-start(bf16[256,1152]{1,0:T(8,128)(2,1)} %get-tuple-element.76), channel_id=1, source_target_pairs={{0,2},{1,3},{2,0},{3,1},{4,6},{5,7},{6,4},{7,5},{8,10},{9,11},{10,... | collective-permute-start | bytes 1769480 | tf_op jit(solution)/shard_map/ppermute | solution.py:256
  35.8 101.8 %collective-permute-start.2 = (bf16[256,1152]{1,0:T(8,128)(2,1)}, bf16[256,1152]{1,0:T(8,128)(2,1)S(1)}, u32[]{:S(2)}, u32[]{:S(2)}) collective-permute-start(bf16[256,1152]{1,0:T(8,128)(2,1)} %get-tuple-element.75), channel_id=1, source_target_pairs={{0,3},{1,0},{2,1},{3,2},{4,7},{5,4},{6,5},{7,6},{8,11},{9,8},{10,9... | collective-permute-start | bytes 1769480 | tf_op jit(solution)/shard_map/ppermute | solution.py:256
  36.5 99.0 %collective-permute-start.11 = (bf16[256,768]{0,1:T(8,128)(2,1)}, bf16[256,768]{0,1:T(8,128)(2,1)}, u32[]{:S(2)}, u32[]{:S(2)}) collective-permute-start(bf16[256,768]{0,1:T(8,128)(2,1)} %bitcast.165), channel_id=1, source_target_pairs={{0,3},{1,0},{2,1},{3,2},{4,7},{5,4},{6,5},{7,6},{8,11},{9,8},{10,9... | collective-permute-start | bytes 1179656 | tf_op jit(solution)/shard_map/ppermute | solution.py:256
  39.4 70.7 %copy-start.36 = (s32[1024]{0:T(1024)}, s32[1024]{0:T(1024)S(1)}, u32[]{:S(2)}) copy-start(s32[1024]{0:T(1024)S(1)} %pad_add_fusion) | copy-start | bytes 12292
  97.2 38.2 %collective-permute-start.9 = (bf16[256,768]{0,1:T(8,128)(2,1)}, bf16[256,768]{0,1:T(8,128)(2,1)}, u32[]{:S(2)}, u32[]{:S(2)}) collective-permute-start(bf16[256,768]{0,1:T(8,128)(2,1)} %bitcast.164), channel_id=1, source_target_pairs={{0,1},{1,2},{2,3},{3,0},{4,5},{5,6},{6,7},{7,4},{8,9},{9,10},{10,1... | collective-permute-start | bytes 1179656 | tf_op jit(solution)/shard_map/ppermute | solution.py:256
  137.6 155.0 %copy-start.7 = (bf16[256,1152]{1,0:T(8,128)(2,1)}, bf16[256,1152]{1,0:T(8,128)(2,1)S(1)}, u32[]{:S(2)}) copy-start(bf16[256,1152]{1,0:T(8,128)(2,1)S(1)} %collective-permute-done) | copy-start | bytes 1769476
  137.6 155.0 %copy-start.9 = (bf16[256,1152]{1,0:T(8,128)(2,1)}, bf16[256,1152]{1,0:T(8,128)(2,1)S(1)}, u32[]{:S(2)}) copy-start(bf16[256,1152]{1,0:T(8,128)(2,1)S(1)} %collective-permute-done.1) | copy-start | bytes 1769476
  137.6 154.9 %copy-start.11 = (bf16[256,1152]{1,0:T(8,128)(2,1)}, bf16[256,1152]{1,0:T(8,128)(2,1)S(1)}, u32[]{:S(2)}) copy-start(bf16[256,1152]{1,0:T(8,128)(2,1)S(1)} %collective-permute-done.2) | copy-start | bytes 1769476
  437.7 102.6 %copy-start.47 = (f32[768]{0:T(1024)S(1)}, f32[768]{0:T(1024)}, u32[]{:S(2)}) copy-start(f32[768]{0:T(1024)} %convert_element_type.182) | copy-start | bytes 9220
  583.5 252.6 %reduce-scatter.11.cloned.1.call-start = ((), (), s32[]{:S(2)}) async-start(), calls=%async_computation.16 | async-start | bytes 10948608 | tf_op jit(solution)/shard_map/reduce_scatter | solution.py:305
  620.3 363.9 %reduce-scatter.7.cloned.1.call-start = ((), (), s32[]{:S(2)}) async-start(), calls=%async_computation.12 | async-start | bytes 10948608 | tf_op jit(solution)/shard_map/reduce_scatter | solution.py:305
  779.2 352.9 %reduce-scatter.9.cloned.1.call-start = ((), (), s32[]{:S(2)}) async-start(), calls=%async_computation.14 | async-start | bytes 10948608 | tf_op jit(solution)/shard_map/reduce_scatter | solution.py:305
  800.5 506.4 %reduce-scatter.15.cloned.1.call-start = ((), (), s32[]{:S(2)}) async-start(), calls=%async_computation.20 | async-start | bytes 8650752 | tf_op jit(solution)/shard_map/reduce_scatter | solution.py:305
  816.1 607.6 %reduce-scatter.17.cloned.1.call-start = ((), (), s32[]{:S(2)}) async-start(), calls=%async_computation.22 | async-start | bytes 3244032 | tf_op jit(solution)/shard_map/reduce_scatter | solution.py:305
  825.0 626.1 %all-gather.30.cloned.1.call-start = ((), (), s32[]{:S(2)}) async-start(), calls=%async_computation.19 | async-start | bytes 1327104 | tf_op jit(solution)/shard_map/all_gather | solution.py:306
  825.8 657.5 %all-gather.28.cloned.1.call-start = ((), (), s32[]{:S(2)}) async-start(), calls=%async_computation.17 | async-start | bytes 2985984 | tf_op jit(solution)/shard_map/all_gather | solution.py:306
  836.1 679.4 %all-gather.24.cloned.1.call-start = ((), (), s32[]{:S(2)}) async-start(), calls=%async_computation.13 | async-start | bytes 2985984 | tf_op jit(solution)/shard_map/all_gather | solution.py:306
  840.7 143.9 %copy-start.51 = (f32[1152]{0:T(1024)S(1)}, f32[1152]{0:T(1024)}, u32[]{:S(2)}) copy-start(f32[1152]{0:T(1024)} %get-tuple-element.31) | copy-start | bytes 13828
  840.7 144.0 %copy-start.52 = (f32[4608]{0:T(1024)S(1)}, f32[4608]{0:T(1024)}, u32[]{:S(2)}) copy-start(f32[4608]{0:T(1024)} %get-tuple-element.110) | copy-start | bytes 55300
  840.7 144.0 %copy-start.55 = (f32[1152]{0:T(1024)S(1)}, f32[1152]{0:T(1024)}, u32[]{:S(2)}) copy-start(f32[1152]{0:T(1024)} %get-tuple-element.29) | copy-start | bytes 13828
  840.7 144.1 %copy-start.59 = (f32[2048]{0:T(1024)S(1)}, f32[2048]{0:T(1024)}, u32[]{:S(2)}) copy-start(f32[2048]{0:T(1024)} %get-tuple-element.112) | copy-start | bytes 24580
  840.7 144.1 %copy-start.58 = (f32[2048]{0:T(1024)S(1)}, f32[2048]{0:T(1024)}, u32[]{:S(2)}) copy-start(f32[2048]{0:T(1024)} %get-tuple-element.114) | copy-start | bytes 24580
  840.7 144.1 %copy-start.53 = (f32[768]{0:T(1024)S(1)}, f32[768]{0:T(1024)}, u32[]{:S(2)}) copy-start(f32[768]{0:T(1024)} %get-tuple-element.27) | copy-start | bytes 9220
  840.7 144.2 %copy-start.37 = (s32[1024]{0:T(1024)S(1)}, s32[1024]{0:T(1024)}, u32[]{:S(2)}) copy-start(s32[1024]{0:T(1024)} %copy-done.36) | copy-start | bytes 12292
  984.2 563.5 %all-gather.26.cloned.1.call-start = ((), (), s32[]{:S(2)}) async-start(), calls=%async_computation.15 | async-start | bytes 2985984 | tf_op jit(solution)/shard_map/all_gather | solution.py:306
  1016.0 122.5 %copy-start.29 = (bf16[1024,1152]{1,0:T(8,128)(2,1)S(1)}, bf16[1024,1152]{1,0:T(8,128)(2,1)}, u32[]{:S(2)}) copy-start(bf16[1024,1152]{1,0:T(8,128)(2,1)} %copy-done.27) | copy-start | bytes 7077892
  1132.1 445.4 %all-gather.32.cloned.1.call-start = ((), (), s32[]{:S(2)}) async-start(), calls=%async_computation.21 | async-start | bytes 2359296 | tf_op jit(solution)/shard_map/all_gather | solution.py:306
  1134.8 152.3 %collective-permute-start.12 = (bf16[256,1152]{1,0:T(8,128)(2,1)}, bf16[256,1152]{1,0:T(8,128)(2,1)}, u32[]{:S(2)}, u32[]{:S(2)}) collective-permute-start(bf16[256,1152]{1,0:T(8,128)(2,1)} %get-tuple-element.69), channel_id=1, source_target_pairs={{0,3},{1,0},{2,1},{3,2},{4,7},{5,4},{6,5},{7,6},{8,11},{9,8},{10,9... | collective-permute-start | bytes 1769480 | tf_op jit(solution)/shard_map/ppermute | solution.py:264
  1135.2 153.8 %collective-permute-start.13 = (bf16[256,1152]{1,0:T(8,128)(2,1)}, bf16[256,1152]{1,0:T(8,128)(2,1)}, u32[]{:S(2)}, u32[]{:S(2)}) collective-permute-start(bf16[256,1152]{1,0:T(8,128)(2,1)} %get-tuple-element.68), channel_id=1, source_target_pairs={{0,2},{1,3},{2,0},{3,1},{4,6},{5,7},{6,4},{7,5},{8,10},{9,11},{10,... | collective-permute-start | bytes 1769480 | tf_op jit(solution)/shard_map/ppermute | solution.py:264
  1136.6 153.6 %collective-permute-start.14 = (bf16[256,1152]{1,0:T(8,128)(2,1)}, bf16[256,1152]{1,0:T(8,128)(2,1)}, u32[]{:S(2)}, u32[]{:S(2)}) collective-permute-start(bf16[256,1152]{1,0:T(8,128)(2,1)} %get-tuple-element.67), channel_id=1, source_target_pairs={{0,1},{1,2},{2,3},{3,0},{4,5},{5,6},{6,7},{7,4},{8,9},{9,10},{10,1... | collective-permute-start | bytes 1769480 | tf_op jit(solution)/shard_map/ppermute | solution.py:264
  1139.6 151.7 %collective-permute-start.6 = (bf16[256,1152]{1,0:T(8,128)(2,1)}, bf16[256,1152]{1,0:T(8,128)(2,1)}, u32[]{:S(2)}, u32[]{:S(2)}) collective-permute-start(bf16[256,1152]{1,0:T(8,128)(2,1)} %get-tuple-element.72), channel_id=1, source_target_pairs={{0,3},{1,0},{2,1},{3,2},{4,7},{5,4},{6,5},{7,6},{8,11},{9,8},{10,9... | collective-permute-start | bytes 1769480 | tf_op jit(solution)/shard_map/ppermute | solution.py:264
  1139.6 156.2 %collective-permute-start.7 = (bf16[256,1152]{1,0:T(8,128)(2,1)}, bf16[256,1152]{1,0:T(8,128)(2,1)}, u32[]{:S(2)}, u32[]{:S(2)}) collective-permute-start(bf16[256,1152]{1,0:T(8,128)(2,1)} %get-tuple-element.71), channel_id=1, source_target_pairs={{0,2},{1,3},{2,0},{3,1},{4,6},{5,7},{6,4},{7,5},{8,10},{9,11},{10,... | collective-permute-start | bytes 1769480 | tf_op jit(solution)/shard_map/ppermute | solution.py:264
  1287.1 19.8 %collective-permute-start.8 = (bf16[256,1152]{1,0:T(8,128)(2,1)S(1)}, bf16[256,1152]{1,0:T(8,128)(2,1)}, u32[]{:S(2)}, u32[]{:S(2)}) collective-permute-start(bf16[256,1152]{1,0:T(8,128)(2,1)S(1)} %get-tuple-element.70), channel_id=1, source_target_pairs={{0,1},{1,2},{2,3},{3,0},{4,5},{5,6},{6,7},{7,4},{8,9},{9,10},{10,1... | collective-permute-start | bytes 1769480 | tf_op jit(solution)/shard_map/ppermute | solution.py:264
  (67 other events, 731.5 us)
Sparse Core Ops, SparseCore 0:
  11.5 121.6 all-gather.17
  136.6 87.8 all-gather.11
  227.4 85.5 all-gather.13
  316.4 85.5 all-gather.15
  404.7 76.1 all-gather.19
  483.6 56.5 all-gather.21
  583.6 104.5 reduce-scatter.12
  695.3 140.7 reduce-scatter.10
  843.2 140.9 reduce-scatter.6
  991.2 140.8 reduce-scatter.8
  1134.5 172.3 reduce-scatter.14
  1313.7 110.0 reduce-scatter.16
  1425.8 25.3 all-gather.29
  1453.1 30.2 all-gather.27
  1485.2 30.2 all-gather.23
  1517.4 30.2 all-gather.25
  1549.6 27.8 all-gather.31

commit v2 on v1

--- a/solution.py
+++ b/solution.py
@@ -144,6 +144,9 @@
 
     @pl.when(head == 0)
     def _():
+        if len(grads) == 1:
+            spare = pl.ds(3 * width, dq_ref.shape[1] - 3 * width)
+            dq_ref[:, spare] = jnp.zeros((count, dq_ref.shape[1] - 3 * width), BF)
         row = lax.broadcasted_iota(jnp.int32, dots.shape[:1] + (width,), 0)
         col = lax.broadcasted_iota(jnp.int32, dots.shape[:1] + (width,), 1)
         pick = ((col >= row * HEAD_DIM) & (col < (row + 1) * HEAD_DIM)).astype(F32).astype(BF)
@@ -191,7 +194,7 @@
     count, tokens = seg_query.shape[0], seg_keys.shape[0]
     width = heads * HEAD_DIM
     if count == tokens:
-        shapes = [(count, 3 * width)]
+        shapes = [(count, -(-3 * width // (4 * LANES)) * 4 * LANES)]
         columns = (0, width, 2 * width)
     else:
         shapes = [(count, width), (tokens, width), (tokens, width)]
@@ -292,22 +295,46 @@
         return total
 
 
-def gather_bundle(bundle):
-    copies = lax.axis_size("dp")
-    count = bundle.shape[0] // copies
-    own = lax.dynamic_slice_in_dim(bundle, lax.axis_index("dp") * count, count, 0)
-    full = lax.all_gather(own, ("seq", "dp"), axis=0, tiled=True)
-    return full.reshape(lax.axis_size("seq"), bundle.shape[0], bundle.shape[1])
+COPIES = ("plane", "core")
+EVERY = ("seq", "plane", "core")
+
+
+def own_slice(weights, cut):
+    copies = lax.axis_size(COPIES)
+    here = lax.axis_index(COPIES)
+    blocks = [weight.shape[1] // cut for weight in weights]
+    per = weights[0].shape[0]
+    count = per * sum(blocks) // copies
+    piece, row = here * count // per, here * count % per
+    own = None
+    first = 0
+    for weight, number in zip(weights, blocks):
+        column = jnp.clip(piece - first, 0, number - 1) * cut
+        part = lax.dynamic_slice(weight, (row, column), (count, cut))
+        own = part if own is None else jnp.where(piece >= first, part, own)
+        first += number
+    return own, (lax.axis_size("seq"), sum(blocks) * per, cut)
+
+
+def gather_slices(slices, after=None):
+    own, shape = slices
+    if after is not None:
+        own, _ = lax.optimization_barrier((own, after))
+    return lax.all_gather(own, EVERY, axis=0, tiled=True).reshape(shape)
 
 
 def reduce_bundle(bundle):
-    flat = bundle.reshape(-1, bundle.shape[2])
-    own = lax.psum_scatter(flat, ("seq", "dp"), scatter_dimension=0, tiled=True)
-    return lax.all_gather(own, "dp", axis=0, tiled=True)
-
-
-def stack_columns(weight, width):
-    return [weight[:, start : start + width] for start in range(0, weight.shape[1], width)]
+    seq, count, columns = bundle.shape
+    planes = lax.axis_size("plane")
+    core = lax.axis_index("core")
+    parts = bundle.reshape(seq, planes, 2, count // planes // 2, columns)
+    keep = lax.dynamic_index_in_dim(parts, core, 2, keepdims=False).swapaxes(0, 1)
+    send = lax.dynamic_index_in_dim(parts, 1 - core, 2, keepdims=False).swapaxes(0, 1)
+    got = lax.ppermute(send, "core", [(0, 1), (1, 0)])
+    both = (keep.astype(F32) + got.astype(F32)).astype(BF)
+    mine = lax.psum_scatter(both, "plane", scatter_dimension=0, tiled=True)[0]
+    own = lax.psum_scatter(mine, "seq", scatter_dimension=0, tiled=True)[0]
+    return lax.all_gather(own, COPIES, axis=0, tiled=True)
 
 
 def split_rows(full, count):
@@ -315,6 +342,898 @@
         full[:, start : start + count].reshape(-1, full.shape[2])
         for start in range(0, full.shape[1], count)
     ]
+
+
+MIB = 1024 * 1024
+
+
+def spec(shape, index, once=False):
+    if once:
+        return pl.BlockSpec(shape, index, pipeline_mode=pl.Buffered(1))
+    return pl.BlockSpec(shape, index)
+
+
+def fixed(shape):
+    return spec(shape, lambda *_: (0,) * len(shape), once=True)
+
+
+def call(kernel, grid, inputs, outputs, args, name, flops, scratch=(), scalars=None):
+    moved = sum(math.prod(arg.shape) * arg.dtype.itemsize for arg in args)
+    moved += sum(math.prod(shape) * jnp.dtype(kind).itemsize for shape, kind, _ in outputs)
+    grid_spec = pltpu.PrefetchScalarGridSpec(
+        num_scalar_prefetch=0 if scalars is None else 1,
+        grid=grid,
+        in_specs=inputs,
+        out_specs=[block for _, _, block in outputs],
+        scratch_shapes=list(scratch),
+    )
+    given = args if scalars is None else [scalars] + list(args)
+    return pl.pallas_call(
+        kernel,
+        grid_spec=grid_spec,
+        out_shape=[jax.ShapeDtypeStruct(shape, kind) for shape, kind, _ in outputs],
+        compiler_params=pltpu.CompilerParams(vmem_limit_bytes=60 * MIB),
+        cost_estimate=pl.CostEstimate(flops=flops, bytes_accessed=moved, transcendentals=0),
+        name=name,
+    )(*given)
+
+
+def square(block):
+    return block.reshape(-1, block.shape[-1])
+
+
+def chunks(count, size=256):
+    return [pl.ds(start, min(size, count)) for start in range(0, count, min(size, count))]
+
+
+def project_kernel(x_ref, hot_ref, shift_ref, scale_ref, w_ref, bias_ref, qkv_ref, modt_ref, low_ref):
+    @pl.when(pl.program_id(0) == 0)
+    def _():
+        for rows in chunks(x_ref.shape[0]):
+            normed, _ = norm_stats(x_ref[rows, :].astype(F32))
+            hot = hot_ref[rows, :]
+            low = normed * (1.0 + dot_nn(hot, scale_ref[...])) + dot_nn(hot, shift_ref[...])
+            low_ref[rows, :] = low.astype(BF)
+            modt_ref[:, rows] = low.astype(BF).T
+
+    weight = square(w_ref[...])
+    for rows in chunks(x_ref.shape[0]):
+        qkv_ref[rows, :] = (dot_nn(low_ref[rows, :], weight) + bias_ref[...]).astype(BF)
+
+
+def project(x, hot, mod, weights, bias):
+    tokens, width = x.shape
+    seq, _, per, _ = weights.shape
+    part = lambda index: spec((mod.shape[0], width), lambda j: (0, index), once=True)
+    return call(
+        project_kernel,
+        (3,),
+        [
+            fixed((tokens, width)),
+            fixed(hot.shape),
+            part(0),
+            part(1),
+            spec((seq, 1, per, width), lambda j: (0, j, 0, 0)),
+            spec((1, width), lambda j: (0, j)),
+        ],
+        [
+            ((tokens, 3 * width), BF, spec((tokens, width), lambda j: (0, j))),
+            ((width, tokens), BF, fixed((width, tokens))),
+        ],
+        [x, hot, mod, mod, weights, bias],
+        "project",
+        6 * tokens * width * width,
+        [pltpu.VMEM((tokens, width), BF)],
+    )
+
+
+def merge_kernel(
+    out_ref, x_ref, hot_ref, gate_ref, shift_ref, scale_ref, w_ref, bias_ref,
+    branch_ref, mid_ref, low_ref, lowt_ref, outt_ref,
+):
+    hot = hot_ref[...]
+    branch = dot_nn(out_ref[...], square(w_ref[...])) + bias_ref[...]
+    middle = x_ref[...].astype(F32) + dot_nn(hot, gate_ref[...]) * branch
+    normed, _ = norm_stats(middle)
+    low = normed * (1.0 + dot_nn(hot, scale_ref[...])) + dot_nn(hot, shift_ref[...])
+    low = low.astype(BF)
+    branch_ref[...] = branch.astype(BF)
+    mid_ref[...] = middle
+    low_ref[...] = low
+    lowt_ref[...] = low.T
+    outt_ref[...] = out_ref[...].T
+
+
+def merge(attended, x, hot, mod, weights, bias):
+    tokens, width = x.shape
+    seq, _, per, _ = weights.shape
+    size = min(256, tokens)
+    part = lambda index: spec((mod.shape[0], width), lambda i: (0, index), once=True)
+    rows = spec((size, width), lambda i: (i, 0))
+    turned = spec((width, size), lambda i: (0, i))
+    return call(
+        merge_kernel,
+        (tokens // size,),
+        [
+            rows,
+            rows,
+            spec((size, hot.shape[1]), lambda i: (i, 0)),
+            part(2),
+            part(3),
+            part(4),
+            spec((seq, 1, per, width), lambda i: (0, 3, 0, 0), once=True),
+            fixed((1, width)),
+        ],
+        [
+            ((tokens, width), BF, rows),
+            ((tokens, width), F32, rows),
+            ((tokens, width), BF, rows),
+            ((width, tokens), BF, turned),
+            ((width, tokens), BF, turned),
+        ],
+        [attended, x, hot, mod, mod, mod, weights, bias],
+        "merge",
+        2 * tokens * width * width,
+    )
+
+
+def gelu_pair(value):
+    factor = math.sqrt(2.0 / math.pi)
+    squared = value * value
+    tangent = jnp.tanh(factor * value * (1.0 + GELU_COEF * squared))
+    half = 0.5 * (1.0 + tangent)
+    slope = half + (0.5 * factor) * value * (1.0 - tangent * tangent) * (
+        1.0 + 3.0 * GELU_COEF * squared
+    )
+    return value * half, slope
+
+
+def feed_kernel(
+    low_ref, w_in_ref, b_in_ref, w_out_ref, b_out_ref, mid_ref, hot_ref, gate_ref,
+    actt_ref, slope_ref, res_ref, rest_ref, branch_ref, total,
+):
+    step = pl.program_id(0)
+    w_in, w_out = square(w_in_ref[...]), w_out_ref[...]
+    for rows in chunks(low_ref.shape[0]):
+        hmid = dot_nn(low_ref[rows, :], w_in) + b_in_ref[...]
+        act, slope = gelu_pair(hmid)
+        act = act.astype(BF)
+        slope_ref[rows, :] = slope.astype(BF)
+        actt_ref[:, rows] = act.T
+        part = dot_nn(act, w_out)
+
+        @pl.when(step == 0)
+        def _():
+            total[rows, :] = part
+
+        @pl.when(step > 0)
+        def _():
+            total[rows, :] += part
+
+    @pl.when(step == pl.num_programs(0) - 1)
+    def _():
+        for rows in chunks(low_ref.shape[0]):
+            branch = total[rows, :] + b_out_ref[...]
+            result = mid_ref[rows, :] + dot_nn(hot_ref[rows, :], gate_ref[...]) * branch
+            result = result.astype(BF)
+            res_ref[rows, :] = result
+            rest_ref[:, rows] = result.T
+            branch_ref[rows, :] = branch.astype(BF)
+
+
+def feed(low, w_in, b_in, w_out, b_out, mid, hot, mod):
+    tokens, width = low.shape
+    seq, blocks, per, cut = w_in.shape
+    hidden = blocks * cut
+    return call(
+        feed_kernel,
+        (blocks,),
+        [
+            fixed((tokens, width)),
+            spec((seq, 1, per, cut), lambda j: (0, j, 0, 0)),
+            spec((1, cut), lambda j: (0, j)),
+            spec((cut, width), lambda j: (j, 0)),
+            fixed((1, width)),
+            fixed((tokens, width)),
+            fixed(hot.shape),
+            spec((mod.shape[0], width), lambda j: (0, 5), once=True),
+        ],
+        [
+            ((hidden, tokens), BF, spec((cut, tokens), lambda j: (j, 0))),
+            ((tokens, hidden), BF, spec((tokens, cut), lambda j: (0, j))),
+            ((tokens, width), BF, fixed((tokens, width))),
+            ((width, tokens), BF, fixed((width, tokens))),
+            ((tokens, width), BF, fixed((tokens, width))),
+        ],
+        [low, w_in, b_in, w_out, b_out, mid, hot, mod],
+        "feed",
+        4 * tokens * width * hidden,
+        [pltpu.VMEM((tokens, width), F32)],
+    )
+
+
+def silu_pair(value):
+    gate = jax.nn.sigmoid(value)
+    return value * gate, gate * (1.0 + value * (1.0 - gate))
+
+
+def align_kernel(
+    res_ref, w_in_ref, b_in_ref, w_mid_ref, b_mid_ref, w_out_ref, b_out_ref, goal_ref,
+    act1t_ref, act2t_ref, gfeat_ref, gh2_ref, gh1_ref, gout_ref, act1_ref, slope1_ref,
+):
+    blocks, cut = w_in_ref.shape[1], w_in_ref.shape[3]
+    res = res_ref[...]
+    for j in range(blocks):
+        columns = pl.ds(j * cut, cut)
+        hidden1 = dot_nn(res, square(w_in_ref[:, j])) + b_in_ref[:, columns]
+        act, slope = silu_pair(hidden1)
+        act1_ref[:, columns] = act.astype(BF)
+        slope1_ref[:, columns] = slope
+    act1 = act1_ref[...]
+    act1t_ref[...] = act1.T
+    hidden2 = dot_nn(act1, w_mid_ref[...]) + b_mid_ref[...]
+    act2, slope2 = silu_pair(hidden2)
+    act2 = act2.astype(BF)
+    act2t_ref[...] = act2.T
+    feats = dot_nn(act2, w_out_ref[...]) + b_out_ref[...]
+    goals = goal_ref[...].astype(F32)
+    inv_feat = lax.rsqrt(jnp.sum(feats * feats, axis=-1, keepdims=True) + EPSILON)
+    feat_unit = feats * inv_feat
+    goal_unit = goals * lax.rsqrt(jnp.sum(goals * goals, axis=-1, keepdims=True) + EPSILON)
+    cosine = jnp.sum(feat_unit * goal_unit, axis=-1, keepdims=True)
+    weight = -0.5 * feats.shape[1]
+    gfeat = (weight * inv_feat * (goal_unit - cosine * feat_unit)).astype(BF)
+    gfeat_ref[...] = gfeat
+    gh2 = (dot_nt(gfeat, w_out_ref[...]) * slope2).astype(BF)
+    gh2_ref[...] = gh2
+    gh1 = (dot_nt(gh2, w_mid_ref[...]) * slope1_ref[...]).astype(BF)
+    gh1_ref[...] = gh1
+    total = None
+    for j in range(blocks):
+        part = dot_nt(gh1_ref[:, pl.ds(j * cut, cut)], square(w_in_ref[:, j]))
+        total = part if total is None else total + part
+    gout_ref[...] = total
+
+
+def align(res, w_in, b_in, w_mid, b_mid, w_out, b_out, goals):
+    tokens, width = res.shape
+    inner, goal_width = w_out.shape
+    size = min(256, tokens)
+    rows = lambda n: spec((size, n), lambda i: (i, 0))
+    turned = lambda n: spec((n, size), lambda i: (0, i))
+    return call(
+        align_kernel,
+        (tokens // size,),
+        [
+            rows(width),
+            fixed(w_in.shape),
+            fixed((1, inner)),
+            fixed(w_mid.shape),
+            fixed((1, inner)),
+            fixed(w_out.shape),
+            fixed((1, goal_width)),
+            rows(goal_width),
+        ],
+        [
+            ((inner, tokens), BF, turned(inner)),
+            ((inner, tokens), BF, turned(inner)),
+            ((tokens, goal_width), BF, rows(goal_width)),
+            ((tokens, inner), BF, rows(inner)),
+            ((tokens, inner), BF, rows(inner)),
+            ((tokens, width), F32, rows(width)),
+        ],
+        [res, w_in, b_in, w_mid, b_mid, w_out, b_out, goals],
+        "align",
+        4 * tokens * inner * (width + inner + goal_width),
+        [pltpu.VMEM((size, inner), BF), pltpu.VMEM((size, inner), F32)],
+    )
+
+
+def feed_back_kernel(
+    gout_ref, branch_ref, hot_ref, hott_ref, gate_ref, w_out_ref, slope_ref, w_in_ref,
+    gmlp_ref, ghmid_ref, gmod_ref, ggate_ref,
+):
+    step = pl.program_id(0)
+
+    @pl.when(step == 0)
+    def _():
+        sums = None
+        for rows in chunks(gout_ref.shape[0]):
+            gout = gout_ref[rows, :]
+            gmlp_ref[rows, :] = (gout * dot_nn(hot_ref[rows, :], gate_ref[...])).astype(BF)
+            part = dot_nn(hott_ref[:, rows], (gout * branch_ref[rows, :].astype(F32)).astype(BF))
+            sums = part if sums is None else sums + part
+        ggate_ref[...] = sums
+
+    w_out, w_in = w_out_ref[...], square(w_in_ref[...])
+    for rows in chunks(gout_ref.shape[0]):
+        ghmid = (dot_nt(gmlp_ref[rows, :], w_out) * slope_ref[rows, :].astype(F32)).astype(BF)
+        ghmid_ref[rows, :] = ghmid
+        part = dot_nt(ghmid, w_in)
+
+        @pl.when(step == 0)
+        def _():
+            gmod_ref[rows, :] = part
+
+        @pl.when(step > 0)
+        def _():
+            gmod_ref[rows, :] += part
+
+
+def feed_back(gout, branch, hot, hott, mod, w_out, slope, w_in):
+    tokens, width = gout.shape
+    seq, blocks, per, cut = w_in.shape
+    hidden = blocks * cut
+    return call(
+        feed_back_kernel,
+        (blocks,),
+        [
+            fixed((tokens, width)),
+            fixed((tokens, width)),
+            fixed(hot.shape),
+            fixed(hott.shape),
+            spec((mod.shape[0], width), lambda j: (0, 5), once=True),
+            spec((cut, width), lambda j: (j, 0)),
+            spec((tokens, cut), lambda j: (0, j)),
+            spec((seq, 1, per, cut), lambda j: (0, j, 0, 0)),
+        ],
+        [
+            ((tokens, width), BF, fixed((tokens, width))),
+            ((tokens, hidden), BF, spec((tokens, cut), lambda j: (0, j))),
+            ((tokens, width), F32, fixed((tokens, width))),
+            ((hott.shape[0], width), F32, fixed((hott.shape[0], width))),
+        ],
+        [gout, branch, hot, hott, mod, w_out, slope, w_in],
+        "feed_back",
+        4 * tokens * width * hidden,
+    )
+
+
+def add_rows(ref, value):
+    @pl.when(pl.program_id(0) == 0)
+    def _():
+        ref[...] = value
+
+    @pl.when(pl.program_id(0) > 0)
+    def _():
+        ref[...] += value
+
+
+def merge_back_kernel(
+    gout_ref, gmod_ref, mid_ref, branch_ref, hot_ref, hott_ref, gate_ref, scale_ref, w_ref,
+    gmid_ref, gbranch_ref, gatt_ref, gshift_ref, gscale_ref, ggate_ref,
+):
+    hot, hott = hot_ref[...], hott_ref[...]
+    gmod = gmod_ref[...]
+    normed, inv_std = norm_stats(mid_ref[...])
+    gmid = gout_ref[...] + norm_back(
+        gmod * (1.0 + dot_nn(hot, scale_ref[...])), normed, inv_std
+    )
+    gmid_ref[...] = gmid
+    gbranch = (gmid * dot_nn(hot, gate_ref[...])).astype(BF)
+    gbranch_ref[...] = gbranch
+    gatt_ref[...] = dot_nt(gbranch, square(w_ref[...])).astype(BF)
+    add_rows(gshift_ref, dot_nn(hott, gmod.astype(BF)))
+    add_rows(gscale_ref, dot_nn(hott, (gmod * normed).astype(BF)))
+    add_rows(ggate_ref, dot_nn(hott, (gmid * branch_ref[...].astype(F32)).astype(BF)))
+
+
+def merge_back(gout, gmod, mid, branch, hot, hott, mod, weights):
+    tokens, width = gout.shape
+    seq, _, per, _ = weights.shape
+    size = min(256, tokens)
+    part = lambda index: spec((mod.shape[0], width), lambda i: (0, index), once=True)
+    rows = spec((size, width), lambda i: (i, 0))
+    sums = ((hott.shape[0], width), F32, fixed((hott.shape[0], width)))
+    return call(
+        merge_back_kernel,
+        (tokens // size,),
+        [
+            rows,
+            rows,
+            rows,
+            rows,
+            spec((size, hot.shape[1]), lambda i: (i, 0)),
+            spec((hott.shape[0], size), lambda i: (0, i)),
+            part(2),
+            part(4),
+            spec((seq, 1, per, width), lambda i: (0, 3, 0, 0), once=True),
+        ],
+        [
+            ((tokens, width), F32, rows),
+            ((tokens, width), BF, rows),
+            ((tokens, width), BF, rows),
+            sums,
+            sums,
+            sums,
+        ],
+        [gout, gmod, mid, branch, hot, hott, mod, mod, weights],
+        "merge_back",
+        2 * tokens * width * width,
+    )
+
+
+def project_back_kernel(
+    gqkv_ref, x_ref, gmid_ref, hot_ref, hott_ref, scale_ref, w_ref,
+    gin_ref, gshift_ref, gscale_ref,
+):
+    width = x_ref.shape[1]
+    hott = hott_ref[...]
+    gmod = None
+    for j in range(3):
+        part = dot_nt(gqkv_ref[:, pl.ds(j * width, width)], square(w_ref[:, j]))
+        gmod = part if gmod is None else gmod + part
+    normed, inv_std = norm_stats(x_ref[...].astype(F32))
+    gin = gmid_ref[...] + norm_back(
+        gmod * (1.0 + dot_nn(hot_ref[...], scale_ref[...])), normed, inv_std
+    )
+    gin_ref[...] = gin.astype(BF)
+    add_rows(gshift_ref, dot_nn(hott, gmod.astype(BF)))
+    add_rows(gscale_ref, dot_nn(hott, (gmod * normed).astype(BF)))
+
+
+def project_back(gqkv, x, gmid, hot, hott, mod, weights):
+    tokens, width = x.shape
+    seq, _, per, _ = weights.shape
+    size = min(256, tokens)
+    rows = spec((size, width), lambda i: (i, 0))
+    sums = ((hott.shape[0], width), F32, fixed((hott.shape[0], width)))
+    return call(
+        project_back_kernel,
+        (tokens // size,),
+        [
+            spec((size, 3 * width), lambda i: (i, 0)),
+            rows,
+            rows,
+            spec((size, hot.shape[1]), lambda i: (i, 0)),
+            spec((hott.shape[0], size), lambda i: (0, i)),
+            spec((mod.shape[0], width), lambda i: (0, 1), once=True),
+            spec((seq, 3, per, width), lambda i: (0, 0, 0, 0), once=True),
+        ],
+        [((tokens, width), BF, rows), sums, sums],
+        [gqkv, x, gmid, hot, hott, mod, weights],
+        "project_back",
+        6 * tokens * width * width,
+    )
+
+
+def weight_kernel(where_ref, left_ref, right_ref, *refs, first):
+    left = left_ref[...].reshape(-1, left_ref.shape[-1])
+    got_ref = None if first else refs[0]
+    out_ref = refs[0] if first else refs[1]
+    result = dot_nn(left, right_ref[...]).reshape(out_ref.shape)
+    if first:
+        ones = jnp.ones((16, right_ref.shape[0]), BF)
+        refs[1][...] = dot_nn(ones, right_ref[...])
+    else:
+        result = result + got_ref[...].astype(F32)
+    out_ref[...] = result.astype(BF)
+
+
+def weight_half(where, turned, right, seq, planes, by_columns, got=None):
+    count, tokens = turned.shape
+    columns = right.shape[1]
+    first = got is None
+    half = (lambda w: 1 - w[0]) if first else (lambda w: w[0])
+    if by_columns:
+        per, cut = count // seq // 2, columns // planes
+        left = turned.reshape(seq, 2, per, tokens)
+        left_spec = spec((seq, 1, per, tokens), lambda j, w: (0, half(w), 0, 0))
+        right_spec = spec((tokens, cut), lambda j, w: (0, j))
+        sum_spec = spec((16, cut), lambda j, w: (0, j))
+    else:
+        per, cut = count // seq // planes // 2, columns
+        left = turned.reshape(seq, planes, 2, per, tokens)
+        left_spec = spec((seq, 1, 1, per, tokens), lambda j, w: (0, j, half(w), 0, 0))
+        right_spec = spec((tokens, cut), lambda j, w: (0, 0))
+        sum_spec = spec((16, cut), lambda j, w: (0, 0))
+    block = spec((1, seq, per, cut), lambda j, w: (j, 0, 0, 0))
+    outputs = [((planes, seq, per, cut), BF, block)]
+    inputs, args = [left_spec, right_spec], [left, right]
+    if first:
+        outputs.append(((16, columns), F32, sum_spec))
+    else:
+        inputs.append(block)
+        args.append(got)
+    return call(
+        functools.partial(weight_kernel, first=first),
+        (planes,),
+        inputs,
+        outputs,
+        args,
+        "weight_other" if first else "weight_own",
+        count * tokens * columns,
+        scalars=where,
+    )
+
+
+ANY = pl.BlockSpec(memory_space=pl.ANY)
+SEQ, PLANES = 4, 4
+
+
+class Link:
+    def __init__(self):
+        self.z, self.p, self.c = (lax.axis_index(name) for name in ("seq", "plane", "core"))
+
+    def ahead(self, shift):
+        return lax.rem(self.z + shift, SEQ)
+
+    def behind(self, shift):
+        return lax.rem(self.z + SEQ - shift, SEQ)
+
+    def across(self, bit):
+        low = lax.rem(self.p, 2)
+        high = self.p // 2
+        low = 1 - low if bit % 2 else low
+        high = 1 - high if bit // 2 else high
+        return high * 2 + low
+
+    def copy(self, source, target, sems, axis, index):
+        return pltpu.make_async_remote_copy(
+            src_ref=source,
+            dst_ref=target,
+            send_sem=sems[0],
+            recv_sem=sems[1],
+            device_id={axis: index},
+            device_id_type=pl.DeviceIdType.MESH,
+        )
+
+    def greet(self):
+        barrier = pltpu.get_barrier_semaphore()
+        for step in range(1, SEQ):
+            signal = functools.partial(
+                pl.semaphore_signal, barrier, inc=1, device_id_type=pl.DeviceIdType.MESH
+            )
+            signal(device_id={"seq": self.ahead(step)})
+            signal(device_id={"plane": self.across(step)})
+        pl.semaphore_signal(
+            barrier, inc=1, device_id={"core": 1 - self.c}, device_id_type=pl.DeviceIdType.MESH
+        )
+        pl.semaphore_wait(barrier, 2 * SEQ - 1)
+
+
+class Gather:
+    def __init__(self, slices, shards, targets, sems):
+        self.link = Link()
+        self.slices, self.shards, self.targets = slices, shards, targets
+        self.z_sems, self.p_sems, self.c_sems, self.local_sems = sems
+
+    @staticmethod
+    def scratch(count):
+        dma = pltpu.SemaphoreType.DMA
+        return [dma((2, count, 3)), dma((2, count, 3, 3)), dma((2, count, 3)), dma((count, 4))]
+
+    def rows(self, target):
+        half = target.shape[2] // 2
+        return pl.ds(pl.multiple_of(self.link.c * half, half), half)
+
+    def locals(self):
+        for k, (shard, target) in enumerate(zip(self.shards, self.targets)):
+            width = target.shape[3]
+            block = 0
+            for array in shard:
+                for start in range(0, array.shape[1], width):
+                    yield pltpu.make_async_copy(
+                        array.at[:, pl.ds(start, width)],
+                        target.at[self.link.z, block],
+                        self.local_sems.at[k, block],
+                    )
+                    block += 1
+
+    def along(self, k, shift, incoming):
+        link, target = self.link, self.targets[k]
+        place = link.behind(shift) if incoming else link.z
+        return link.copy(
+            self.slices[k],
+            target.at[place, link.p, self.rows(target), :],
+            (self.z_sems.at[0, k, shift - 1], self.z_sems.at[1, k, shift - 1]),
+            "seq",
+            link.ahead(shift),
+        )
+
+    def across(self, k, shift, bit, incoming):
+        link, target = self.link, self.targets[k]
+        plane = link.across(bit)
+        place = (link.behind(shift), plane if incoming else link.p, self.rows(target))
+        return link.copy(
+            target.at[place],
+            target.at[place],
+            (self.p_sems.at[0, k, shift - 1, bit - 1], self.p_sems.at[1, k, shift - 1, bit - 1]),
+            "plane",
+            plane,
+        )
+
+    def beside(self, k, shift, incoming):
+        link, target = self.link, self.targets[k]
+        half = target.shape[2] // 2
+        core = 1 - link.c if incoming else link.c
+        rows = pl.ds(pl.multiple_of(core * half, half), half)
+        place = target.at[link.behind(shift), :, rows, :]
+        return link.copy(
+            place,
+            place,
+            (self.c_sems.at[0, k, shift - 1], self.c_sems.at[1, k, shift - 1]),
+            "core",
+            1 - link.c,
+        )
+
+    def start(self):
+        for k in range(len(self.targets)):
+            for shift in (1, 3, 2):
+                self.along(k, shift, False).start()
+
+    def start_local(self):
+        for copy in self.locals():
+            copy.start()
+
+    def spread(self, k, shift):
+        self.along(k, shift, True).wait_recv()
+        for bit in range(1, PLANES):
+            self.across(k, shift, bit, False).start()
+
+    def pair(self, k, shift):
+        for bit in range(1, PLANES):
+            self.across(k, shift, bit, True).wait_recv()
+        self.beside(k, shift, False).start()
+
+    def finish(self):
+        for k in range(len(self.targets)):
+            for shift in range(1, SEQ):
+                self.beside(k, shift, True).wait_recv()
+                self.along(k, shift, False).wait_send()
+                self.beside(k, shift, False).wait_send()
+                for bit in range(1, PLANES):
+                    self.across(k, shift, bit, False).wait_send()
+        for copy in self.locals():
+            copy.wait()
+
+
+class Rounds:
+    def __init__(self, sources, targets, sems):
+        self.link = Link()
+        self.sources, self.targets, self.sems, self.local_sems = sources, targets, *sems
+
+    @staticmethod
+    def scratch(count):
+        dma = pltpu.SemaphoreType.DMA
+        return [dma((2, count, 3)), dma((count,))]
+
+    def along(self, k, shift, incoming):
+        link = self.link
+        return link.copy(
+            self.sources[k].at[link.ahead(shift)],
+            self.targets[k].at[link.behind(shift) if incoming else link.z],
+            (self.sems.at[0, k, shift - 1], self.sems.at[1, k, shift - 1]),
+            "seq",
+            link.ahead(shift),
+        )
+
+    def local(self, k):
+        z = self.link.z
+        return pltpu.make_async_copy(
+            self.sources[k].at[z], self.targets[k].at[z], self.local_sems.at[k]
+        )
+
+    def start(self):
+        for k in range(len(self.targets)):
+            for shift in (2, 1, 3):
+                self.along(k, shift, False).start()
+            self.local(k).start()
+
+    def finish(self):
+        for k in range(len(self.targets)):
+            for shift in range(1, SEQ):
+                self.along(k, shift, True).wait_recv()
+                self.along(k, shift, False).wait_send()
+            self.local(k).wait()
+
+
+class Finish:
+    def __init__(self, sources, targets, refs):
+        self.link = Link()
+        self.sources, self.targets = sources, targets
+        count = len(sources)
+        self.bufs = refs[:count]
+        self.z_sems, self.p_sems, self.c_sems, self.local_sems = refs[count:]
+
+    @staticmethod
+    def scratch(shapes):
+        dma = pltpu.SemaphoreType.DMA
+        count = len(shapes)
+        bufs = [
+            pltpu.VMEM((9 if shared else 5,) + tuple(shape), BF) for shape, shared in shapes
+        ]
+        return bufs + [dma((2, count, 3)), dma((2, count, 3)), dma((2, count, 4)), dma((count, 2))]
+
+    def shared(self, k):
+        return len(self.targets[k].shape) == 3
+
+    def along(self, k, shift):
+        link = self.link
+        return link.copy(
+            self.sources[k].at[link.ahead(shift)],
+            self.bufs[k].at[shift - 1],
+            (self.z_sems.at[0, k, shift - 1], self.z_sems.at[1, k, shift - 1]),
+            "seq",
+            link.ahead(shift),
+        )
+
+    def across(self, k, bit, incoming):
+        link = self.link
+        plane = link.across(bit)
+        if self.shared(k):
+            target = self.bufs[k].at[4 + bit]
+        else:
+            target = self.targets[k].at[plane if incoming else link.p, link.c]
+        return link.copy(
+            self.bufs[k].at[4],
+            target,
+            (self.p_sems.at[0, k, bit - 1], self.p_sems.at[1, k, bit - 1]),
+            "plane",
+            plane,
+        )
+
+    def beside(self, k, bit, incoming):
+        link = self.link
+        core = 1 - link.c if incoming else link.c
+        if self.shared(k):
+            source, target = self.bufs[k].at[8], self.targets[k].at[core]
+        else:
+            plane = link.across(bit)
+            target = self.targets[k].at[plane, core]
+            source = self.bufs[k].at[4] if bit == 0 else self.targets[k].at[plane, link.c]
+        return link.copy(
+            source,
+            target,
+            (self.c_sems.at[0, k, bit], self.c_sems.at[1, k, bit]),
+            "core",
+            1 - link.c,
+        )
+
+    def mine(self, k):
+        return pltpu.make_async_copy(
+            self.sources[k].at[self.link.z], self.bufs[k].at[3], self.local_sems.at[k, 0]
+        )
+
+    def own(self, k):
+        link = self.link
+        if self.shared(k):
+            source, target = self.bufs[k].at[8], self.targets[k].at[link.c]
+        else:
+            source, target = self.bufs[k].at[4], self.targets[k].at[link.p, link.c]
+        return pltpu.make_async_copy(source, target, self.local_sems.at[k, 1])
+
+    def start(self):
+        for k in range(len(self.sources)):
+            for shift in (2, 1, 3):
+                self.along(k, shift).start()
+            self.mine(k).start()
+
+    def add(self, k):
+        for shift in range(1, SEQ):
+            self.along(k, shift).wait_recv()
+        self.mine(k).wait()
+        buf = self.bufs[k]
+        total = buf[0].astype(F32) + buf[1].astype(F32) + buf[2].astype(F32) + buf[3].astype(F32)
+        buf[4] = total.astype(BF)
+        for bit in range(1, PLANES):
+            self.across(k, bit, False).start()
+        if not self.shared(k):
+            self.own(k).start()
+            self.beside(k, 0, False).start()
+
+    def pass_on(self, k):
+        for bit in range(1, PLANES):
+            self.across(k, bit, True).wait_recv()
+            if not self.shared(k):
+                self.beside(k, bit, False).start()
+        if self.shared(k):
+            buf = self.bufs[k]
+            total = buf[4].astype(F32) + buf[5].astype(F32) + buf[6].astype(F32) + buf[7].astype(F32)
+            buf[8] = total.astype(BF)
+            self.own(k).start()
+            self.beside(k, 0, False).start()
+
+    def finish(self):
+        for k in range(len(self.sources)):
+            for bit in range(1 if self.shared(k) else PLANES):
+                self.beside(k, bit, True).wait_recv()
+                self.beside(k, bit, False).wait_send()
+            for step in range(1, SEQ):
+                self.along(k, step).wait_send()
+                self.across(k, step, False).wait_send()
+            self.own(k).wait()
+
+
+def bring_kernel(*refs, bundles, rounds):
+    refs = list(refs)
+    take = lambda count: [refs.pop(0) for _ in range(count)]
+    slices = take(len(bundles))
+    shards = [take(count) for count in bundles]
+    sources = take(rounds)
+    targets = take(len(bundles))
+    arrived = take(rounds)
+    gather = Gather(slices, shards, targets, take(4))
+    tokens = Rounds(sources, arrived, take(2))
+    gather.link.greet()
+    gather.start()
+    tokens.start()
+    gather.start_local()
+    for k in range(len(bundles)):
+        for shift in (1, 3, 2):
+            gather.spread(k, shift)
+        for shift in (1, 3, 2):
+            gather.pair(k, shift)
+    tokens.finish()
+    gather.finish()
+
+
+def bring(slices, shards, sources, collective):
+    per = [shard[0].shape[0] for shard in shards]
+    cut = [piece.shape[1] for piece in slices]
+    blocks = [sum(a.shape[1] for a in shard) // n for shard, n in zip(shards, cut)]
+    flat = [array for shard in shards for array in shard]
+    shapes = [
+        jax.ShapeDtypeStruct((SEQ, b, r, n), BF) for b, r, n in zip(blocks, per, cut)
+    ] + [jax.ShapeDtypeStruct(array.shape, array.dtype) for array in sources]
+    args = list(slices) + flat + list(sources)
+    return pl.pallas_call(
+        functools.partial(
+            bring_kernel, bundles=[len(shard) for shard in shards], rounds=len(sources)
+        ),
+        in_specs=[ANY] * len(args),
+        out_specs=[ANY] * len(shapes),
+        out_shape=shapes,
+        scratch_shapes=Gather.scratch(len(slices)) + Rounds.scratch(len(sources)),
+        compiler_params=pltpu.CompilerParams(
+            collective_id=collective, has_side_effects=True, vmem_limit_bytes=60 * MIB
+        ),
+        cost_estimate=pl.CostEstimate(flops=0, bytes_accessed=300_000_000, transcendentals=0),
+        name="bring",
+    )(*args)
+
+
+def settle_kernel(*refs, count, rounds):
+    refs = list(refs)
+    take = lambda number: [refs.pop(0) for _ in range(number)]
+    sums, sources = take(count), take(rounds)
+    targets, arrived = take(count), take(rounds)
+    work = Finish(sums, targets, take(count + 4))
+    tokens = Rounds(sources, arrived, take(2)) if rounds else None
+    work.link.greet()
+    work.start()
+    if rounds:
+        tokens.start()
+    for k in range(count):
+        work.add(k)
+    for k in range(count):
+        work.pass_on(k)
+    work.finish()
+    if rounds:
+        tokens.finish()
+
+
+def settle(sums, shared, sources, collective):
+    shapes = [
+        jax.ShapeDtypeStruct(((2,) if one else (PLANES, 2)) + total.shape[1:], BF)
+        for total, one in zip(sums, shared)
+    ] + [jax.ShapeDtypeStruct(array.shape, array.dtype) for array in sources]
+    args = list(sums) + list(sources)
+    scratch = Finish.scratch([(total.shape[1:], one) for total, one in zip(sums, shared)])
+    if sources:
+        scratch = scratch + Rounds.scratch(len(sources))
+    return pl.pallas_call(
+        functools.partial(settle_kernel, count=len(sums), rounds=len(sources)),
+        in_specs=[ANY] * len(args),
+        out_specs=[ANY] * len(shapes),
+        out_shape=shapes,
+        scratch_shapes=scratch,
+        compiler_params=pltpu.CompilerParams(
+            collective_id=collective, has_side_effects=True, vmem_limit_bytes=60 * MIB
+        ),
+        cost_estimate=pl.CostEstimate(flops=0, bytes_accessed=200_000_000, transcendentals=0),
+        name="settle",
+    )(*args)
 
 
 def local(
@@ -357,17 +1276,13 @@
     mod_row = lax.dynamic_index_in_dim(modulation, place.row, 0, keepdims=False)
 
     per = qkv_weight.shape[0]
-    first = gather_bundle(
-        jnp.concatenate(stack_columns(qkv_weight, width) + [attn_out_weight], axis=0)
-    )
-    second = gather_bundle(jnp.concatenate(stack_columns(mlp_in_weight, width), axis=0))
-    third = gather_bundle(mlp_out_weight)
     half = inner // 2
-    fourth = gather_bundle(
-        jnp.concatenate(stack_columns(proj_in_weight, half), axis=0)
-    )
-    fifth = gather_bundle(proj_mid_weight)
-    sixth = gather_bundle(proj_out_weight)
+    first = gather_slices(own_slice([qkv_weight, attn_out_weight], width))
+    second = gather_slices(own_slice([mlp_in_weight], width), first)
+    third = gather_slices(own_slice([mlp_out_weight], width), second)
+    fourth = gather_slices(own_slice([proj_in_weight], half), third)
+    fifth = gather_slices(own_slice([proj_mid_weight], inner), fourth)
+    sixth = gather_slices(own_slice([proj_out_weight], goal_width), fifth)
     w_q, w_k, w_v, w_attn = split_rows(first, per)
     w_qkv = jnp.concatenate([w_q, w_k, w_v], axis=1)
     w_mlp_in = jnp.concatenate(split_rows(second, per), axis=1)
@@ -451,7 +1366,7 @@
             [grads[0], place.sum_parts(grads[1]), place.sum_parts(grads[2])], axis=1
         )
     else:
-        grad_qkv = grads[0]
+        grad_qkv = grads[0][:, : 3 * width]
     first_sum = reduce_bundle(
         jnp.concatenate(
             blocks(dot_tn(modulated1, grad_qkv), width) + blocks(grad_attn_w, width), axis=1
@@ -489,7 +1404,7 @@
 
     biases = [bias_qv, bias_attn, bias_ff_in, bias_ff_out, bias_in, bias_mid, bias_out]
     packed = jnp.concatenate([bias.reshape(seq, -1) for bias in biases], axis=1)
-    packed = lax.psum(packed, ("dp", "seq"))
+    packed = lax.psum(packed, EVERY)
     packed = lax.dynamic_index_in_dim(packed, lax.axis_index("seq"), 0, keepdims=False)
     shares = []
     start = 0
@@ -523,36 +1438,255 @@
     )
 
 
+def tie(value, *others):
+    return lax.optimization_barrier((value,) + others)[0]
+
+
+def swap_cores(value):
+    return lax.ppermute(value, "core", [(0, 1), (1, 0)])
+
+
+def swap_planes(value, bit):
+    return lax.ppermute(value, "plane", [(p, p ^ bit) for p in range(lax.axis_size("plane"))])
+
+
+def scatter_planes(both, after=None):
+    planes, seq, count, columns = both.shape
+    flat = both.reshape(planes * seq * count, columns)
+    if after is not None:
+        flat = tie(flat, after)
+    own = lax.psum_scatter(flat, "plane", scatter_dimension=0, tiled=True)
+    return own.reshape(seq, count, columns)
+
+
+def scatter_seq(both):
+    seq, count, columns = both.shape
+    return lax.psum_scatter(
+        both.reshape(seq * count, columns), "seq", scatter_dimension=0, tiled=True
+    )
+
+
+def gather_copies(own):
+    full = lax.all_gather(own, COPIES, axis=0, tiled=True)
+    return full.reshape(lax.axis_size("plane"), 2, own.shape[0], own.shape[1])
+
+
+def sum_vectors(packed):
+    bit = 1
+    total = packed + swap_cores(packed)
+    while bit < lax.axis_size("plane"):
+        total = total + swap_planes(total, bit)
+        bit *= 2
+    seq = lax.axis_size("seq")
+    here = lax.axis_index("seq")
+    own = lax.dynamic_index_in_dim(total, here, 0, keepdims=False)
+    for shift in range(1, seq):
+        piece = lax.dynamic_index_in_dim(total, (here + shift) % seq, 0, keepdims=False)
+        own = own + lax.ppermute(piece, "seq", [(z, (z + shift) % seq) for z in range(seq)])
+    return own
+
+
+def exchange(array):
+    seq = lax.axis_size("seq")
+    here = lax.axis_index("seq")
+    result = array
+    for shift in range(1, seq):
+        piece = lax.dynamic_index_in_dim(array, (here + shift) % seq, 0, keepdims=False)
+        piece = lax.ppermute(piece, "seq", [(z, (z + shift) % seq) for z in range(seq)])
+        result = lax.dynamic_update_index_in_dim(result, piece, (here + seq - shift) % seq, 0)
+    return result
+
+
+def unpack_kernel(full_ref, out_ref):
+    out_ref[...] = full_ref[0, 0].astype(F32)
+
+
+def unpack(full, columns=None):
+    planes, _, count, cut = full.shape
+    if columns is None:
+        shape, place = (planes * 2 * count, cut), (lambda p, c: (2 * p + c, 0))
+    else:
+        shape, place = (2 * count, columns), (lambda p, c: (c, p))
+    return call(
+        unpack_kernel,
+        (planes, 2),
+        [spec((1, 1, count, cut), lambda p, c: (p, c, 0, 0))],
+        [(shape, F32, spec((count, cut), place))],
+        [full],
+        "unpack",
+        0,
+    )[0]
+
+
+def local_row(
+    block_input, modulation, segment_ids,
+    qkv_weight, query_value_bias,
+    attn_out_weight, attn_out_bias,
+    mlp_in_weight, mlp_in_bias,
+    mlp_out_weight, mlp_out_bias,
+    proj_in_weight, proj_in_bias,
+    proj_mid_weight, proj_mid_bias,
+    proj_out_weight, proj_out_bias,
+    targets,
+):
+    rows, span, width = block_input.shape
+    seq, planes = lax.axis_size("seq"), lax.axis_size("plane")
+    heads = width // HEAD_DIM
+    hidden = mlp_in_weight.shape[1]
+    inner = proj_mid_weight.shape[1]
+    goal_width = targets.shape[2]
+    tokens = rows * span
+    where = lax.axis_index("core").reshape(1).astype(jnp.int32)
+
+    slice1, _ = own_slice([qkv_weight, attn_out_weight], width)
+    slice2, _ = own_slice([mlp_in_weight], width)
+    third = gather_slices(own_slice([mlp_out_weight], width))
+    w1, w2, x, seg_own = bring(
+        [slice1, slice2],
+        [[qkv_weight, attn_out_weight], [mlp_in_weight]],
+        [block_input, segment_ids.reshape(rows, -1, LANES)],
+        0,
+    )
+    x = x.reshape(tokens, width)
+    seg_own = seg_own.reshape(tokens)
+    goals = exchange(tie(targets, x)).reshape(tokens, goal_width)
+    mod_row = lax.dynamic_index_in_dim(modulation, lax.axis_index("seq"), 0, keepdims=False)
+    mod = jnp.pad(mod_row, ((0, 16 - mod_row.shape[0]), (0, 0)))
+    hot = (seg_own[:, None] == jnp.arange(16, dtype=jnp.int32)[None, :]).astype(BF)
+    hott = (seg_own[None, :] == jnp.arange(16, dtype=jnp.int32)[:, None]).astype(BF)
+    seg_column = seg_own[:, None]
+    vector = lambda bias: bias.astype(F32)[None, :]
+
+    per = qkv_weight.shape[0]
+    bias_float = query_value_bias.astype(F32)
+    full_bias = jnp.concatenate(
+        [bias_float[:width], jnp.zeros((width,), F32), bias_float[width:]]
+    )
+    qkv, mod1t = project(x, hot, mod, w1, full_bias[None, :])
+    fourth = gather_slices(own_slice([tie(proj_in_weight, x)], inner // planes))
+    fifth = gather_slices(own_slice([tie(proj_mid_weight, x)], inner))
+    sixth = gather_slices(own_slice([tie(proj_out_weight, x)], goal_width))
+    parts = ((qkv, 0), (qkv, 1), (qkv, 2))
+    attended, totals = attend_forward(parts, seg_column, seg_column, heads)
+    branch, mid, low2, mod2t, attt = merge(attended, x, hot, mod, w1, vector(attn_out_bias))
+    w3 = third.reshape(hidden, width)
+    actt, slope, out_low, outt, mlp_branch = feed(
+        low2, w2, vector(mlp_in_bias), w3, vector(mlp_out_bias), mid, hot, mod
+    )
+    w4 = fourth.reshape(seq, planes, per, inner // planes)
+    w5, w6 = fifth.reshape(inner, inner), sixth.reshape(inner, goal_width)
+    act1t, act2t, gfeat, gh2, gh1, gout = align(
+        out_low, w4, vector(proj_in_bias), w5, vector(proj_mid_bias), w6, vector(proj_out_bias), goals
+    )
+    block_out = exchange(tie(out_low, gout).reshape(block_input.shape))
+
+    half = functools.partial(weight_half, where, seq=seq, planes=planes)
+    other6, sum6 = half(act2t, tie(gfeat, gout), by_columns=False)
+    got6 = swap_cores(other6)
+    other5, sum5 = half(act1t, tie(gh2, other6), by_columns=True)
+    got5 = swap_cores(other5)
+    other4, sum4 = half(outt, tie(gh1, other5), by_columns=True)
+    got4 = swap_cores(other4)
+    (own6,) = half(act2t, tie(gfeat, other4), by_columns=False, got=got6)
+    (own5,) = half(act1t, tie(gh2, own6), by_columns=True, got=got5)
+    (own4,) = half(outt, tie(gh1, own5), by_columns=True, got=got4)
+    plane6 = scatter_planes(own6)
+    plane5 = scatter_planes(own5)
+    plane4 = scatter_planes(own4)
+    gmlp, ghmid, gmod2, ggate2 = feed_back(
+        tie(gout, own4), mlp_branch, hot, hott, mod, w3, slope, w2
+    )
+    other3, sum3 = half(actt, tie(gmlp, gmod2), by_columns=False)
+    got3 = swap_cores(other3)
+    other2, sum2 = half(mod2t, tie(ghmid, other3), by_columns=True)
+    got2 = swap_cores(other2)
+    (own3,) = half(actt, tie(gmlp, other2), by_columns=False, got=got3)
+    plane3 = scatter_planes(own3)
+    (own2,) = half(mod2t, tie(ghmid, own3), by_columns=True, got=got2)
+    plane2 = scatter_planes(own2)
+    gmid, gbranch, gatt, gshift2, gscale2, ggate1 = merge_back(
+        gout, tie(gmod2, own2), mid, branch, hot, hott, mod, w1
+    )
+    half1 = functools.partial(weight_half, where, seq=seq, planes=1)
+    other0, sum0 = half1(attt, tie(gbranch, gatt), by_columns=True)
+    got0 = swap_cores(other0)
+    (gqkv,) = attend_backward(parts, seg_column, seg_column, totals, attended, tie(gatt, other0), heads)
+    (own0,) = half1(attt, tie(gbranch, gqkv), by_columns=True, got=got0)
+    other1, sum1 = half(mod1t, tie(gqkv, own0), by_columns=True)
+    got1 = swap_cores(other1)
+    gin, gshift1, gscale1 = project_back(
+        tie(gqkv, other1), x, gmid, hot, hott, mod, w1
+    )
+    (own1,) = half(mod1t, tie(gqkv, gin), by_columns=True, got=got1)
+    plane1 = scatter_planes(own1)
+    grad_input = exchange(gin.reshape(block_input.shape)).astype(F32)
+
+    segs = modulation.shape[1]
+    grad_mod = jnp.concatenate(
+        [gshift1, gscale1, ggate1, gshift2, gscale2, ggate2], axis=1
+    )[:segs].astype(BF)
+    grad_mod = jnp.pad(grad_mod.reshape(-1, LANES), ((0, 8), (0, 0)))
+    grad_mod = jnp.broadcast_to(grad_mod[None], (rows,) + grad_mod.shape)
+    full6, full5, full4, full3, full2, full0 = settle(
+        [plane6, plane5, plane4, plane3, plane2, tie(own0[0], own1)],
+        [False] * 5 + [True],
+        [],
+        1,
+    )
+    full1, all_mod = settle([plane1], [False], [tie(grad_mod, full0)], 2)
+    grad_modulation = all_mod[:, :-8].reshape(rows, segs, 6 * width).astype(F32)
+
+    columns1 = sum1[0]
+    biases = [
+        jnp.concatenate([columns1[:width], columns1[2 * width : 3 * width]]),
+        sum0[0], sum2[0], sum3[0], sum4[0], sum5[0], sum6[0],
+    ]
+    packed = sum_vectors(jnp.concatenate([bias.reshape(seq, -1) for bias in biases], axis=1))
+    shares = []
+    start = 0
+    for bias in biases:
+        stop = start + bias.shape[0] // seq
+        shares.append(packed[start:stop])
+        start = stop
+
+    return (
+        block_out,
+        grad_input,
+        grad_modulation,
+        unpack(full1, 3 * width),
+        shares[0],
+        full0.reshape(per, width).astype(F32),
+        shares[1],
+        unpack(full2, hidden),
+        shares[2],
+        unpack(full3),
+        shares[3],
+        unpack(full4, inner),
+        shares[4],
+        unpack(full5, inner),
+        shares[5],
+        unpack(full6),
+        shares[6],
+    )
+
+
 def solution(mesh):
-    placed = (
-        P("dp", "seq", None),
-        P("dp", None, None),
-        P("dp", "seq"),
-        P("seq", None),
-        P(),
-        P("seq", None),
-        P(),
-        P("seq", None),
-        P(),
-        P("seq", None),
-        P(),
-        P("seq", None),
-        P(),
-        P("seq", None),
-        P(),
-        P("seq", None),
-        P(),
-        P("dp", "seq", None),
-    )
-    return jax.shard_map(
-        local,
-        mesh=mesh,
-        in_specs=placed,
-        out_specs=(
-            P("dp", "seq", None),
-            P("dp", "seq", None),
-            P("dp", None, None),
-        )
-        + (P("seq", None), P("seq")) * 7,
-        check_vma=False,
-    )
+    copies, seq = mesh.shape["dp"], mesh.shape["seq"]
+    grid = jax.sharding.Mesh(
+        mesh.devices.reshape(copies // 2, 2, seq), ("plane", "core", "seq")
+    )
+    rows, weight = P(COPIES, "seq", None), P("seq", None)
+    placed = (rows, P(COPIES, None, None), P(COPIES, "seq")) + (weight, P()) * 7 + (rows,)
+
+    def step(*args):
+        per_device = args[0].shape[0] // copies
+        one_row = per_device == seq and copies // 2 == seq and args[0].shape[1] == 1024
+        return jax.shard_map(
+            local_row if one_row else local,
+            mesh=grid,
+            in_specs=placed,
+            out_specs=(rows, rows, P(COPIES, None, None)) + (weight, P("seq")) * 7,
+            check_vma=False,
+        )(*args)
+
+    return step

time: 1590 us -> 1110 us (0.70)
  Pallas kernels: 114 us -> 848 us
  waiting for transfers between devices: 805 us -> 155 us
  matrix products: 313 us -> 0 us
  blocking collectives: 162 us -> 0 us
  other arithmetic: 85.4 us -> 16.1 us
  local copies, waits for them, and re-layouts: 75.9 us -> 47.4 us
    pallas_call x0 -> x30, Pallas kernels: none -> 733 us  [the longest x27 355 us: call(): pl.pallas_call(kernel, grid_spec=grid_spec, out_shape=[jax.ShapeDtypeStru...]
    reduce_scatter x6, waiting for transfers between devices: 377 us -> 0.03 us  [scatter_planes(): own = lax.psum_scatter(flat, 'plane', scatter_dimension=0, tiled=True)]
    dot_general x28 -> x0, matrix products: 313 us -> none  [the longest x8 114 us: dot_nn(): return jnp.dot(left, right, preferred_element_type=F32)]
    all_gather x11 -> x4, waiting for transfers between devices: 345 us -> 79.4 us  [gather_slices(): return lax.all_gather(own, EVERY, axis=0, tiled=True).reshape(shape)]
    psum x1 -> x0, blocking collectives: 138 us -> none  [local(): packed = lax.psum(packed, ('dp', 'seq'))]
    convert_element_type x15 -> x5, other arithmetic: 34.6 us -> 5.24 us  [the longest x1 2.49 us: local_row(): grad_input = exchange(gin.reshape(block_input.shape)).astype(F32)]
    slice x20 -> x14, local copies, waits for them, and re-layouts: 37.3 us -> 10.1 us  [the longest x5 3.07 us: local_row(): shares.append(packed[start:stop])]
    reduce_sum x8 -> x0, other arithmetic: 26.8 us -> none  [the longest x1 12.4 us: local(): bias_attn = jnp.sum(grad_branch.astype(F32), axis=0)]
  transfers between devices with their start and end apart: 32 -> 32, of which waited for: 17 -> 10; matrix products, arithmetic and copies ran while one was open for 26% -> 5% of each run, Pallas kernels for 7% -> 67%
where the time goes in v2:
time: 1110 us; the launch traced here: 1100 us
  Pallas kernels  848 us (76%)
  waiting for transfers between devices  155 us (14%)
  local copies, waits for them, and re-layouts  47.4 us (4%)
  starting transfers between devices  17.5 us (2%)
  other arithmetic  16.1 us (1%)
  between operations  15.1 us (1%)
    pallas_call x27, Pallas kernels, call(): pl.pallas_call(kernel, grid_spec=grid_spec, out_shape=[jax.ShapeDtypeStru...  355 us
    pallas_call x2, Pallas kernels, settle(): pl.pallas_call(functools.partial(settle_kernel, count=len(sums), rounds=l...  195 us
    pallas_call x1, Pallas kernels, bring(): pl.pallas_call(functools.partial(bring_kernel, bundles=[len(shard) for sh...  183 us
    all_gather x4, waiting for transfers between devices, gather_slices(): return lax.all_gather(own, EVERY, axis=0, tiled=True).reshape(shape)  79.4 us
    ppermute x9, waiting for transfers between devices, exchange(): lax.ppermute(piece, 'seq', [(z, (z + shift) % seq) for z in range(seq)])  70.6 us
    pallas_call x1, Pallas kernels, attend_backward(): pl.pallas_call(functools.partial(attend_backward_kernel, block=min(256, c...  67.1 us
    pallas_call x1, Pallas kernels, attend_forward(): pl.pallas_call(functools.partial(attend_forward_kernel, block=min(256, co...  47.3 us
  transfers between devices with their start and end apart: 32, of which 10 were waited for; matrix products, arithmetic and copies ran while one was open for 5% of the time, Pallas kernels for 67%

profile of v2, /device:TPU:9, one launch (start us, length us, event | category | flops | bytes accessed | tf_op | source)
XLA Modules:
  0.0 1099.2 jit_solution(10356470376256253508)
XLA Ops:
  7.3 2.8 copy.54
  11.6 1.9 dynamic_slice.73.refs_1_
  13.5 1.9 dynamic-slice_select_fusion.refs_0_
  15.4 182.9 %bring.1 = (bf16[4,4,288,1152]{3,2,1,0:T(8,128)(2,1)}, bf16[4,4,288,1152]{3,2,1,0:T(8,128)(2,1)}, bf16[4,256,1152]{2,1,0:T(8,128)(2,1)}, s32[4,2,128]{2,1,0:T(2,128)}) custom-call(bf16[144,1152]{1,0:T(8,128)(2,1)} %dynamic-slice_select_fusion.refs_0_, bf16[144,1152]{1,0:T(8,128)(2,1)} %dynamic_slice.73.refs_1_, bf16[288,3456]{1,0:T(8,128)(2,1)} %refs_2_.1, ...), custom_call_target="tpu_custom_call" | custom-call | bytes 300000000 | tf_op jit(solution)/shard_map/bring/pallas_call | solution.py:1180
  200.0 1.7 dynamic_slice.76
  201.7 1.7 constant_dynamic-slice_fusion.1
  208.9 17.3 %project.1 = (bf16[1024,3456]{1,0:T(8,128)(2,1)}, bf16[1152,1024]{1,0:T(8,128)(2,1)}) custom-call(bf16[1024,1152]{1,0:T(8,128)(2,1)} %bitcast.87, bf16[1024,16]{1,0:T(8,128)(2,1)} %fusion.hot_ref, bf16[16,6912]{1,0:T(8,128)(2,1)} %pad.8.shift_ref.scale_ref.gate_ref, bf16[16,6912]{1,0:T(8,128)(2,1)} %pad.8.shift_ref.scale_ref.gate_ref, ...), custom_call_target="tpu_custom_call" | custom-call | flops 8153726976 | bytes 22902272 | tf_op jit(solution)/shard_map/project/pallas_call | solution.py:371
  226.3 2.2 collective-permute-start.1
  228.5 47.3 %attend_forward.1 = (bf16[1024,1152]{1,0:T(8,128)(2,1)}, f32[16,1024]{1,0:T(8,128)}) custom-call(bf16[1024,3456]{1,0:T(8,128)(2,1)} %get-tuple-element.104.q_ref.k_ref.v_ref, bf16[1024,3456]{1,0:T(8,128)(2,1)} %get-tuple-element.104.q_ref.k_ref.v_ref, bf16[1024,3456]{1,0:T(8,128)(2,1)} %get-tuple-element.104.q_ref.k_ref.v_ref, ...), custom_call_target="tpu_custom_call" | custom-call | flops 17179869184 | bytes 9437184 | tf_op jit(solution)/shard_map/attend_forward/pallas_call | solution.py:110
  279.9 10.8 merge.1
  291.5 46.5 %feed.1 = (bf16[4608,1024]{1,0:T(8,128)(2,1)}, bf16[1024,4608]{1,0:T(8,128)(2,1)}, bf16[1024,1152]{1,0:T(8,128)(2,1)}, bf16[1152,1024]{1,0:T(8,128)(2,1)}, bf16[1024,1152]{1,0:T(8,128)(2,1)}) custom-call(bf16[1024,1152]{1,0:T(8,128)(2,1)} %get-tuple-element.106.low_ref, bf16[4,4,288,1152]{3,2,1,0:T(8,128)(2,1)} %get-tuple-element.107.w_in_ref, ...), custom_call_target="tpu_custom_call" | custom-call | flops 21743271936 | bytes 54540800 | tf_op jit(solution)/shard_map/feed/pallas_call | solution.py:371
  338.2 79.2 %all-gather.9.cloned.1.call-done.w_mid_ref = bf16[2048,2048]{1,0:T(8,128)(2,1)} async-done(((bf16[64,2048]{1,0:T(8,128)(2,1)}), bf16[2048,2048]{1,0:T(8,128)(2,1)}) %all-gather.9.cloned.1.call-update) | async-done | bytes 8388624 | tf_op jit(solution)/shard_map/all_gather | solution.py:323
  417.4 49.7 %align.1 = (bf16[2048,1024]{1,0:T(8,128)(2,1)}, bf16[2048,1024]{1,0:T(8,128)(2,1)}, bf16[1024,768]{1,0:T(8,128)(2,1)}, bf16[1024,2048]{1,0:T(8,128)(2,1)}, bf16[...) custom-call(bf16[1024,1152]{1,0:T(8,128)(2,1)} %get-tuple-element.115.res_ref, bf16[4,4,288,512]{3,2,1,0:T(8,128)(2,1)} %bitcast.111, ...), custom_call_target="tpu_custom_call" | custom-call | flops 33285996544 | bytes 43273216 | tf_op jit(solution)/shard_map/align/pallas_call | solution.py:371
  467.2 5.6 weight_other.7
  473.1 8.5 weight_other.8
  481.8 6.4 weight_other.9
  489.4 5.6 weight_own.7
  495.3 9.4 weight_own.8
  506.1 6.8 weight_own.9
  513.8 42.6 %feed_back.1 = (bf16[1024,1152]{1,0:T(8,128)(2,1)}, bf16[1024,4608]{1,0:T(8,128)(2,1)}, f32[1024,1152]{1,0:T(8,128)}, f32[16,1152]{1,0:T(8,128)}) custom-call(f32[1024,1152]{1,0:T(8,128)} %get-tuple-element.132.gout_ref, bf16[1024,1152]{1,0:T(8,128)(2,1)} %get-tuple-element.133.branch_ref, bf16[1024,16]{1,0:T(8,128)(2,1)} %fusion.hot_ref, ...), custom_call_target="tpu_custom_call" | custom-call | flops 21743271936 | bytes 54624256 | tf_op jit(solution)/shard_map/feed_back/pallas_call | solution.py:371
  556.4 11.2 %weight_other.10 = (bf16[4,4,144,1152]{3,2,1,0:T(8,128)(2,1)}, f32[16,1152]{1,0:T(8,128)}) custom-call(s32[1]{0:T(128)} %bitcast.21.where_ref, bf16[4,4,2,144,1024]{4,3,2,1,0:T(8,128)(2,1)} %bitcast.75, bf16[1024,1152]{1,0:T(8,128)(2,1)} %get-tuple-element.144.right_ref), custom_call_target="tpu_custom_call" | custom-call | flops 5435817984 | bytes 17178624 | tf_op jit(solution)/shard_map/weight_other/pallas_call | solution.py:371
  567.8 11.6 %weight_other.11 = (bf16[4,4,144,1152]{3,2,1,0:T(8,128)(2,1)}, f32[16,4608]{1,0:T(8,128)}) custom-call(s32[1]{0:T(128)} %bitcast.21.where_ref, bf16[4,2,144,1024]{3,2,1,0:T(8,128)(2,1)} %bitcast.90, bf16[1024,4608]{1,0:T(8,128)(2,1)} %get-tuple-element.145.right_ref), custom_call_target="tpu_custom_call" | custom-call | flops 5435817984 | bytes 17399808 | tf_op jit(solution)/shard_map/weight_other/pallas_call | solution.py:371
  579.7 11.1 %weight_own.10 = bf16[4,4,144,1152]{3,2,1,0:T(8,128)(2,1)} custom-call(s32[1]{0:T(128)} %bitcast.21.where_ref, bf16[4,4,2,144,1024]{4,3,2,1,0:T(8,128)(2,1)} %bitcast.76, bf16[1024,1152]{1,0:T(8,128)(2,1)} %get-tuple-element.144.right_ref, bf16[4,4,144,1152]{3,2,1,0:T(8,128)(2,1)} %collective-permute-done.9.refs_0_), custom_call_target="tpu_custom_call" | custom-call | flops 5435817984 | bytes 22413312 | tf_op jit(solution)/shard_map/weight_own/pallas_call | solution.py:371
  590.8 11.6 %weight_own.11 = bf16[4,4,144,1152]{3,2,1,0:T(8,128)(2,1)} custom-call(s32[1]{0:T(128)} %bitcast.21.where_ref, bf16[4,2,144,1024]{3,2,1,0:T(8,128)(2,1)} %bitcast.91, bf16[1024,4608]{1,0:T(8,128)(2,1)} %get-tuple-element.145.right_ref, bf16[4,4,144,1152]{3,2,1,0:T(8,128)(2,1)} %collective-permute-done.10.refs_0_), custom_call_target="tpu_custom_call" | custom-call | flops 5435817984 | bytes 22413312 | tf_op jit(solution)/shard_map/weight_own/pallas_call | solution.py:371
  603.2 15.2 %merge_back.1 = (f32[1024,1152]{1,0:T(8,128)}, bf16[1024,1152]{1,0:T(8,128)(2,1)}, bf16[1024,1152]{1,0:T(8,128)(2,1)}, f32[16,1152]{1,0:T(8,128)}, f32[16,1152]{1,0:T(8,128)}, /*index=5*/f32[16,1152]{1,0:T(8,128)}) custom-call(f32[1024,1152]{1,0:T(8,128)} %get-tuple-element.132.gout_ref, f32[1024,1152]{1,0:T(8,128)} %get-tuple-element.146.gmod_ref, ...), custom_call_target="tpu_custom_call" | custom-call | flops 2717908992 | bytes 37298176 | tf_op jit(solution)/shard_map/merge_back/pallas_call | solution.py:371
  618.4 5.1 weight_other.12
  624.1 67.1 %attend_backward.1.right_ref.gqkv_ref = bf16[1024,3584]{1,0:T(8,128)(2,1)} custom-call(bf16[1024,3456]{1,0:T(8,128)(2,1)} %get-tuple-element.104.q_ref.k_ref.v_ref, bf16[1024,3456]{1,0:T(8,128)(2,1)} %get-tuple-element.104.q_ref.k_ref.v_ref, bf16[1024,3456]{1,0:T(8,128)(2,1)} %get-tuple-element.104.q_ref.k_ref.v_ref, s32[1024,1]{1,0:T(8,128)} %copy.35.segq_ref.segk_ref, ...), custom_call_target="tpu_custom_call" | custom-call | flops 42949672960 | bytes 18874368 | tf_op jit(solution)/shard_map/attend_backward/pallas_call | solution.py:202
  692.3 5.1 weight_own.12
  697.4 9.7 weight_other.13
  707.1 2.0 dynamic-slice_bitcast_fusion.5
  710.3 20.0 %project_back.1 = (bf16[1024,1152]{1,0:T(8,128)(2,1)}, f32[16,1152]{1,0:T(8,128)}, f32[16,1152]{1,0:T(8,128)}) custom-call(bf16[1024,3584]{1,0:T(8,128)(2,1)} %attend_backward.1.right_ref.gqkv_ref, bf16[1024,1152]{1,0:T(8,128)(2,1)} %bitcast.89, f32[1024,1152]{1,0:T(8,128)} %get-tuple-element.159.gmid_ref, bf16[1024,16]{1,0:T(8,128)(2,1)} %fusion.hot_ref, ...), custom_call_target="tpu_custom_call" | custom-call | flops 8153726976 | bytes 27828224 | tf_op jit(solution)/shard_map/project_back/pallas_call | solution.py:371
  730.3 2.0 copy-done.5
  732.3 9.8 weight_own.13
  742.1 2.8 dynamic-slice_bitcast_fusion.3
  750.8 33.7 %collective-permute-done.4 = bf16[256,1152]{1,0:T(8,128)(2,1)S(1)} collective-permute-done((bf16[256,1152]{1,0:T(8,128)(2,1)}, bf16[256,1152]{1,0:T(8,128)(2,1)S(1)}, u32[]{:S(2)}, u32[]{:S(2)}) %collective-permute-start.4) | collective-permute-done | bytes 589856 | tf_op jit(solution)/shard_map/ppermute | solution.py:1495
  799.2 3.2 collective-permute-done.17
  809.5 2.6 collective-permute-start.19
  819.6 33.8 %collective-permute-done.13 = bf16[256,1152]{1,0:T(8,128)(2,1)S(1)} collective-permute-done((bf16[256,1152]{1,0:T(8,128)(2,1)S(1)}, bf16[256,1152]{1,0:T(8,128)(2,1)S(1)}, u32[]{:S(2)}, u32[]{:S(2)}) %collective-permute-start.13) | collective-permute-done | bytes 589856 | tf_op jit(solution)/shard_map/ppermute | solution.py:1495
  853.4 2.1 collective-permute-done.14
  855.5 2.5 convert_element_type.38
  858.1 150.8 %settle.2 = (bf16[4,2,64,768]{3,2,1,0:T(8,128)(2,1)}, bf16[4,2,256,512]{3,2,1,0:T(8,128)(2,1)}, bf16[4,2,144,512]{3,2,1,0:T(8,128)(2,1)}, bf16[4,2,144,1152]{3,2...) custom-call(bf16[4,64,768]{2,1,0:T(8,128)(2,1)} %bitcast.105, ...), custom_call_target="tpu_custom_call" | custom-call | bytes 200000000 | tf_op jit(solution)/shard_map/settle/pallas_call | solution.py:1225
  1009.6 6.3 unpack.7
  1015.9 6.3 unpack.8
  1022.2 6.0 unpack.10
  1028.2 5.6 unpack.9
  1033.8 5.2 unpack.11
  1040.2 44.4 %settle.3 = (bf16[4,2,144,896]{3,2,1,0:T(8,128)(2,1)}, bf16[4,224,128]{2,1,0:T(8,128)(2,1)}) custom-call(bf16[4,144,896]{2,1,0:T(8,128)(2,1)} %bitcast.103, bf16[4,224,128]{2,1,0:T(8,128)(2,1)} %broadcast_in_dim.96.refs_1_), custom_call_target="tpu_custom_call" | custom-call | bytes 200000000 | tf_op jit(solution)/shard_map/settle/pallas_call | solution.py:1225
  1084.6 6.3 unpack.6
  (178 shorter events, 60.4 us)
Async XLA Ops:
  7.2 6.3 copy-start.8
  7.2 284.3 %all-gather.5.cloned.1.call-start = ((), (), s32[]{:S(2)}) async-start(), calls=%async_computation.6 | async-start | bytes 10948608 | tf_op jit(solution)/shard_map/all_gather | solution.py:323
  10.9 327.1 %all-gather.11.cloned.1.call-start = ((), (), s32[]{:S(2)}) async-start(), calls=%async_computation.9 | async-start | bytes 3244032 | tf_op jit(solution)/shard_map/all_gather | solution.py:323
  15.4 188.1 %copy-start.3 = (bf16[4,256,768]{2,1,0:T(8,128)(2,1)S(1)}, bf16[4,256,768]{2,1,0:T(8,128)(2,1)}, u32[]{:S(2)}) copy-start(bf16[4,256,768]{2,1,0:T(8,128)(2,1)} %copy.54) | copy-start | bytes 4718596
  198.3 6.5 copy-start.13
  198.3 7.1 copy-start.14
  199.9 138.3 %all-gather.7.cloned.1.call-start = ((), (), s32[]{:S(2)}) async-start(), calls=%async_computation.7 | async-start | bytes 4866048 | tf_op jit(solution)/shard_map/all_gather | solution.py:323
  201.7 215.8 %all-gather.9.cloned.1.call-start = ((), (), s32[]{:S(2)}) async-start(), calls=%async_computation.8 | async-start | bytes 8650752 | tf_op jit(solution)/shard_map/all_gather | solution.py:323
  203.4 654.6 %reduce-scatter.9.cloned.1.call-start = ((), (), s32[]{:S(2)}) async-start(), calls=%async_computation.11 | async-start | bytes 1966080 | tf_op jit(solution)/shard_map/reduce_scatter | solution.py:1458
  203.6 22.6 %collective-permute-start = (bf16[256,768]{1,0:T(8,128)(2,1)S(1)}, bf16[256,768]{1,0:T(8,128)(2,1)S(1)}, u32[]{:S(2)}, u32[]{:S(2)}) collective-permute-start(bf16[256,768]{1,0:T(8,128)(2,1)S(1)} %dynamic-slice_bitcast_fusion.8), channel_id=1, source_target_pairs={{0,1},{1,2},{2,3},{3,0},{4,5},{5,6},{6,7},{7,4},{8,9},{9,10},{10,1... | collective-permute-start | bytes 1179656 | tf_op jit(solution)/shard_map/ppermute | solution.py:1495
  226.3 64.4 %collective-permute-start.1 = (bf16[256,768]{1,0:T(8,128)(2,1)S(1)}, bf16[256,768]{1,0:T(8,128)(2,1)S(1)}, u32[]{:S(2)}, u32[]{:S(2)}) collective-permute-start(bf16[256,768]{1,0:T(8,128)(2,1)S(1)} %get-tuple-element.198), channel_id=1, source_target_pairs={{0,2},{1,3},{2,0},{3,1},{4,6},{5,7},{6,4},{7,5},{8,10},{9,11},{10,... | collective-permute-start | bytes 1179656 | tf_op jit(solution)/shard_map/ppermute | solution.py:1495
  228.5 47.3 %copy-start.19 = (bf16[1152]{0:T(1024)(128)(2,1)S(1)}, bf16[1152]{0:T(1024)(128)(2,1)}, u32[]{:S(2)}) copy-start(bf16[1152]{0:T(1024)(128)(2,1)} %param.24) | copy-start | bytes 6916
  228.5 47.9 %copy-start.15 = (bf16[4608]{0:T(1024)(128)(2,1)S(1)}, bf16[4608]{0:T(1024)(128)(2,1)}, u32[]{:S(2)}) copy-start(bf16[4608]{0:T(1024)(128)(2,1)} %param.26) | copy-start | bytes 27652
  228.5 48.5 %copy-start.20 = (bf16[1152]{0:T(1024)(128)(2,1)S(1)}, bf16[1152]{0:T(1024)(128)(2,1)}, u32[]{:S(2)}) copy-start(bf16[1152]{0:T(1024)(128)(2,1)} %param.28) | copy-start | bytes 6916
  228.5 49.1 %copy-start.16 = (bf16[2048]{0:T(1024)(128)(2,1)S(1)}, bf16[2048]{0:T(1024)(128)(2,1)}, u32[]{:S(2)}) copy-start(bf16[2048]{0:T(1024)(128)(2,1)} %param.30) | copy-start | bytes 12292
  228.5 49.7 %copy-start.17 = (bf16[2048]{0:T(1024)(128)(2,1)S(1)}, bf16[2048]{0:T(1024)(128)(2,1)}, u32[]{:S(2)}) copy-start(bf16[2048]{0:T(1024)(128)(2,1)} %param.32) | copy-start | bytes 12292
  228.5 50.3 %copy-start.21 = (bf16[768]{0:T(1024)(128)(2,1)S(1)}, bf16[768]{0:T(1024)(128)(2,1)}, u32[]{:S(2)}) copy-start(bf16[768]{0:T(1024)(128)(2,1)} %param.34) | copy-start | bytes 4612
  279.4 12.0 %collective-permute-start.2 = (bf16[256,768]{1,0:T(8,128)(2,1)S(1)}, bf16[256,768]{1,0:T(8,128)(2,1)S(1)}, u32[]{:S(2)}, u32[]{:S(2)}) collective-permute-start(bf16[256,768]{1,0:T(8,128)(2,1)S(1)} %get-tuple-element.197), channel_id=1, source_target_pairs={{0,3},{1,0},{2,1},{3,2},{4,7},{5,4},{6,5},{7,6},{8,11},{9,8},{10,9... | collective-permute-start | bytes 1179656 | tf_op jit(solution)/shard_map/ppermute | solution.py:1495
  291.5 46.6 %copy-start.4 = (bf16[4,256,768]{2,1,0:T(8,128)(2,1)}, bf16[4,256,768]{2,1,0:T(8,128)(2,1)S(1)}, u32[]{:S(2)}) copy-start(bf16[4,256,768]{2,1,0:T(8,128)(2,1)S(1)} %bitcast_dynamic-update-slice_fusion.6) | copy-start | bytes 4718596
  472.8 15.4 %collective-permute-start.6 = (bf16[4,4,64,768]{3,2,1,0:T(8,128)(2,1)}, bf16[4,4,64,768]{3,2,1,0:T(8,128)(2,1)S(1)}, u32[]{:S(2)}, u32[]{:S(2)}) collective-permute-start(bf16[4,4,64,768]{3,2,1,0:T(8,128)(2,1)} %get-tuple-element.124), channel_id=1, source_target_pairs={{0,4},{4,0},{1,5},{5,1},{2,6},{6,2},{3,7},{7,3},{8,12},{12,8},{9,1... | collective-permute-start | bytes 4718600 | tf_op jit(solution)/shard_map/ppermute | solution.py:1446
  481.5 13.8 %collective-permute-start.7 = (bf16[4,4,256,512]{3,2,1,0:T(8,128)(2,1)}, bf16[4,4,256,512]{3,2,1,0:T(8,128)(2,1)}, u32[]{:S(2)}, u32[]{:S(2)}) collective-permute-start(bf16[4,4,256,512]{3,2,1,0:T(8,128)(2,1)} %get-tuple-element.126), channel_id=1, source_target_pairs={{0,4},{4,0},{1,5},{5,1},{2,6},{6,2},{3,7},{7,3},{8,12},{12,8},{9,1... | collective-permute-start | bytes 12582920 | tf_op jit(solution)/shard_map/ppermute | solution.py:1446
  495.0 363.1 %reduce-scatter.13.cloned.1.call-start = ((), (), s32[]{:S(2)}) async-start(), calls=%async_computation.13 | async-start | bytes 2949120 | tf_op jit(solution)/shard_map/reduce_scatter | solution.py:1458
  495.0 9.7 collective-permute-start.8
  513.0 345.1 %reduce-scatter.11.cloned.1.call-start = ((), (), s32[]{:S(2)}) async-start(), calls=%async_computation.12 | async-start | bytes 5242880 | tf_op jit(solution)/shard_map/reduce_scatter | solution.py:1458
  513.7 344.3 %reduce-scatter.17.cloned.1.call-start = ((), (), s32[]{:S(2)}) async-start(), calls=%async_computation.15 | async-start | bytes 6635520 | tf_op jit(solution)/shard_map/reduce_scatter | solution.py:1458
  567.5 12.2 %collective-permute-start.9 = (bf16[4,4,144,1152]{3,2,1,0:T(8,128)(2,1)}, bf16[4,4,144,1152]{3,2,1,0:T(8,128)(2,1)}, u32[]{:S(2)}, u32[]{:S(2)}) collective-permute-start(bf16[4,4,144,1152]{3,2,1,0:T(8,128)(2,1)} %get-tuple-element.141), channel_id=1, source_target_pairs={{0,4},{4,0},{1,5},{5,1},{2,6},{6,2},{3,7},{7,3},{8,12},{12,8},{9,1... | collective-permute-start | bytes 15925256 | tf_op jit(solution)/shard_map/ppermute | solution.py:1446
  579.4 11.4 %collective-permute-start.10 = (bf16[4,4,144,1152]{3,2,1,0:T(8,128)(2,1)}, bf16[4,4,144,1152]{3,2,1,0:T(8,128)(2,1)}, u32[]{:S(2)}, u32[]{:S(2)}) collective-permute-start(bf16[4,4,144,1152]{3,2,1,0:T(8,128)(2,1)} %get-tuple-element.143), channel_id=1, source_target_pairs={{0,4},{4,0},{1,5},{5,1},{2,6},{6,2},{3,7},{7,3},{8,12},{12,8},{9,1... | collective-permute-start | bytes 15925256 | tf_op jit(solution)/shard_map/ppermute | solution.py:1446
  602.4 255.6 %reduce-scatter.15.cloned.1.call-start = ((), (), s32[]{:S(2)}) async-start(), calls=%async_computation.14 | async-start | bytes 6635520 | tf_op jit(solution)/shard_map/reduce_scatter | solution.py:1458
  603.2 437.0 %reduce-scatter.7.cloned.1.call-start = ((), (), s32[]{:S(2)}) async-start(), calls=%async_computation.10 | async-start | bytes 5160960 | tf_op jit(solution)/shard_map/reduce_scatter | solution.py:1458
  623.5 67.7 %collective-permute-start.11 = (bf16[1,4,144,1152]{3,2,1,0:T(8,128)(2,1)}, bf16[1,4,144,1152]{3,2,1,0:T(8,128)(2,1)S(1)}, u32[]{:S(2)}, u32[]{:S(2)}) collective-permute-start(bf16[1,4,144,1152]{3,2,1,0:T(8,128)(2,1)} %get-tuple-element.152), channel_id=1, source_target_pairs={{0,4},{4,0},{1,5},{5,1},{2,6},{6,2},{3,7},{7,3},{8,12},{12,8},{9,1... | collective-permute-start | bytes 3981320 | tf_op jit(solution)/shard_map/ppermute | solution.py:1446
  707.1 23.2 %collective-permute-start.15 = (bf16[4,4,144,896]{3,2,1,0:T(8,128)(2,1)}, bf16[4,4,144,896]{3,2,1,0:T(8,128)(2,1)S(1)}, u32[]{:S(2)}, u32[]{:S(2)}) collective-permute-start(bf16[4,4,144,896]{3,2,1,0:T(8,128)(2,1)} %get-tuple-element.157), channel_id=1, source_target_pairs={{0,4},{4,0},{1,5},{5,1},{2,6},{6,2},{3,7},{7,3},{8,12},{12,8},{9,1... | collective-permute-start | bytes 12386312 | tf_op jit(solution)/shard_map/ppermute | solution.py:1446
  709.1 33.1 %collective-permute-start.3 = (bf16[256,1152]{1,0:T(8,128)(2,1)}, bf16[256,1152]{1,0:T(8,128)(2,1)}, u32[]{:S(2)}, u32[]{:S(2)}) collective-permute-start(bf16[256,1152]{1,0:T(8,128)(2,1)} %dynamic-slice_bitcast_fusion.5), channel_id=1, source_target_pairs={{0,1},{1,2},{2,3},{3,0},{4,5},{5,6},{6,7},{7,4},{8,9},{9,10},{10,1... | collective-permute-start | bytes 1769480 | tf_op jit(solution)/shard_map/ppermute | solution.py:1495
  742.1 50.5 %copy-start.2 = (bf16[1024,1152]{1,0:T(8,128)(2,1)S(1)}, bf16[1024,1152]{1,0:T(8,128)(2,1)}, u32[]{:S(2)}) copy-start(bf16[1024,1152]{1,0:T(8,128)(2,1)} %get-tuple-element.160) | copy-start | bytes 7077892
  745.0 39.5 %collective-permute-start.4 = (bf16[256,1152]{1,0:T(8,128)(2,1)}, bf16[256,1152]{1,0:T(8,128)(2,1)S(1)}, u32[]{:S(2)}, u32[]{:S(2)}) collective-permute-start(bf16[256,1152]{1,0:T(8,128)(2,1)} %get-tuple-element.195), channel_id=1, source_target_pairs={{0,2},{1,3},{2,0},{3,1},{4,6},{5,7},{6,4},{7,5},{8,10},{9,11},{10,... | collective-permute-start | bytes 1769480 | tf_op jit(solution)/shard_map/ppermute | solution.py:1495
  748.0 37.7 %collective-permute-start.5 = (bf16[256,1152]{1,0:T(8,128)(2,1)}, bf16[256,1152]{1,0:T(8,128)(2,1)S(1)}, u32[]{:S(2)}, u32[]{:S(2)}) collective-permute-start(bf16[256,1152]{1,0:T(8,128)(2,1)} %get-tuple-element.194), channel_id=1, source_target_pairs={{0,3},{1,0},{2,1},{3,2},{4,7},{5,4},{6,5},{7,6},{8,11},{9,8},{10,9... | collective-permute-start | bytes 1769480 | tf_op jit(solution)/shard_map/ppermute | solution.py:1495
  791.7 4.7 collective-permute-start.16
  792.7 20.6 %collective-permute-start.12 = (bf16[256,1152]{1,0:T(8,128)(2,1)S(1)}, bf16[256,1152]{1,0:T(8,128)(2,1)S(1)}, u32[]{:S(2)}, u32[]{:S(2)}) collective-permute-start(bf16[256,1152]{1,0:T(8,128)(2,1)S(1)} %dynamic-slice_bitcast_fusion.2), channel_id=1, source_target_pairs={{0,1},{1,2},{2,3},{3,0},{4,5},{5,6},{6,7},{7,4},{8,9},{9,10},{10,1... | collective-permute-start | bytes 1769480 | tf_op jit(solution)/shard_map/ppermute | solution.py:1495
  797.3 5.2 collective-permute-start.17
  803.1 5.4 collective-permute-start.18
  809.5 5.2 collective-permute-start.19
  812.1 3.5 collective-permute-start.20
  813.0 2.8 collective-permute-start.21
  813.5 39.8 %collective-permute-start.13 = (bf16[256,1152]{1,0:T(8,128)(2,1)S(1)}, bf16[256,1152]{1,0:T(8,128)(2,1)S(1)}, u32[]{:S(2)}, u32[]{:S(2)}) collective-permute-start(bf16[256,1152]{1,0:T(8,128)(2,1)S(1)} %get-tuple-element.192), channel_id=1, source_target_pairs={{0,2},{1,3},{2,0},{3,1},{4,6},{5,7},{6,4},{7,5},{8,10},{9,11},{10,... | collective-permute-start | bytes 1769480 | tf_op jit(solution)/shard_map/ppermute | solution.py:1495
  816.3 39.1 %collective-permute-start.14 = (bf16[256,1152]{1,0:T(8,128)(2,1)S(1)}, bf16[256,1152]{1,0:T(8,128)(2,1)S(1)}, u32[]{:S(2)}, u32[]{:S(2)}) collective-permute-start(bf16[256,1152]{1,0:T(8,128)(2,1)S(1)} %get-tuple-element.191), channel_id=1, source_target_pairs={{0,3},{1,0},{2,1},{3,2},{4,7},{5,4},{6,5},{7,6},{8,11},{9,8},{10,9... | collective-permute-start | bytes 1769480 | tf_op jit(solution)/shard_map/ppermute | solution.py:1495
  858.1 150.8 %copy-start.11 = (bf16[224,128]{1,0:T(8,128)(2,1)S(1)}, bf16[224,128]{1,0:T(8,128)(2,1)}, u32[]{:S(2)}) copy-start(bf16[224,128]{1,0:T(8,128)(2,1)} %pad.9) | copy-start | bytes 172036
  1028.2 10.8 copy-start.10
  1084.6 7.3 copy-start.1
  1084.6 6.3 copy-start.12
  (6 other events, 12.3 us)
Sparse Core Ops, SparseCore 0:
  11.5 157.8 all-gather.4
  200.0 66.2 all-gather.10
  269.8 68.4 all-gather.6
  341.5 75.8 all-gather.8
  495.1 29.0 reduce-scatter.8
  527.1 37.3 reduce-scatter.12
  567.5 52.7 reduce-scatter.10
  624.1 61.9 reduce-scatter.16
  690.0 61.9 reduce-scatter.14
  755.2 53.2 reduce-scatter.6

commit v3 on v2

--- a/solution.py
+++ b/solution.py
@@ -57,6 +57,11 @@
     )
 
 
+GATHER_AT = (1, 1, 2, 3, 3, 4, 5, 6, 7, 8, 9, 10, 11, 12, 13, 14, 15, 15, 15)
+FEED_AT = (1, 1, 1, 1, 2, 2, 2, 3, 3, 3, 4, 4, 4, 5, 5, 5, 6, 6, 6, 7, 7, 7, 7, 7, 7, 7, 7, 7)
+SETTLE_AT = (4, 7, 12, 15)
+
+
 def head_window(head, width):
     tile = jnp.minimum((head * HEAD_DIM) // LANES, width // LANES - 2)
     base = pl.multiple_of(tile * LANES, LANES)
@@ -73,30 +78,37 @@
     return jnp.where(mine, block.astype(F32), code).astype(BF)
 
 
-def attend_forward_kernel(q_ref, k_ref, v_ref, segq_ref, segk_ref, out_ref, total_ref, *, block):
-    head = pl.program_id(0)
-    width = q_ref.shape[1]
-    base, mine, lane, low = head_window(head, width)
-    window = pl.ds(base, 2 * LANES)
+def attend_head(head, refs, seg_refs, out_ref, total_ref, block):
+    (q_ref, qcol), (k_ref, kcol), (v_ref, vcol) = refs
+    segq_ref, segk_ref = seg_refs
+    base, mine, lane, low = head_window(head, out_ref.shape[1])
+    window = lambda column: pl.ds(pl.multiple_of(base + column, LANES), 2 * LANES)
     factor = HEAD_DIM ** (-0.5) * LOG2E
-    keys = with_segments(k_ref[:, window], mine, lane, segk_ref[...], 0.0, 1.0)
+    keys = with_segments(k_ref[:, window(kcol)], mine, lane, segk_ref[...], 0.0, 1.0)
     values = jnp.where(
-        mine, v_ref[:, window].astype(F32), jnp.where(lane == 0, 1.0, 0.0)
+        mine, v_ref[:, window(vcol)].astype(F32), jnp.where(lane == 0, 1.0, 0.0)
     ).astype(BF)
     values_t = values.T
-    for start in range(0, q_ref.shape[0], block):
+    for start in range(0, out_ref.shape[0], block):
         rows = pl.ds(start, block)
-        query = with_segments(q_ref[rows, window], mine, lane, segq_ref[rows, :], MASKED, 0.0)
+        query = with_segments(
+            q_ref[rows, window(qcol)], mine, lane, segq_ref[rows, :], MASKED, 0.0
+        )
         scores = dot_nt(keys, query) * factor
         top = jnp.max(scores, axis=0, keepdims=True)
         weights = jnp.exp2(scores - top).astype(BF)
         gathered = dot_nn(values_t, weights)
         total = jnp.where(low, gathered[0:1], gathered[LANES : LANES + 1])
         result = (gathered * (1.0 / total)).T
-        out_ref[rows, window] = jnp.where(
-            mine, result, out_ref[rows, window].astype(F32)
+        out_ref[rows, window(0)] = jnp.where(
+            mine, result, out_ref[rows, window(0)].astype(F32)
         ).astype(BF)
         total_ref[pl.ds(head, 1), rows] = top + jnp.log2(total)
+
+
+def attend_forward_kernel(q_ref, k_ref, v_ref, segq_ref, segk_ref, out_ref, total_ref, *, block):
+    parts = ((q_ref, 0), (k_ref, 0), (v_ref, 0))
+    attend_head(pl.program_id(0), parts, (segq_ref, segk_ref), out_ref, total_ref, block)
 
 
 def whole(shape):
@@ -133,9 +145,29 @@
 
 
 def attend_backward_kernel(
-    q_ref, k_ref, v_ref, segq_ref, segk_ref, total_ref, out_ref, grad_ref, *rest, block, columns
+    q_ref, k_ref, v_ref, segq_ref, segk_ref, total_ref, out_ref, grad_ref, *rest, block, columns,
+    carried=0
 ):
-    grads, dots = rest[:-1], rest[-1]
+    work = None
+    if carried:
+        rest = list(rest)
+        take = lambda number: [rest.pop(0) for _ in range(number)]
+        sums = take(carried)
+        grads = take(1)
+        targets = take(carried)
+        dots = rest.pop(0)
+        work = Sum(sums, targets, rest)
+        head = pl.program_id(0)
+
+        @pl.when(head == 0)
+        def _():
+            work.link.greet()
+            work.start()
+
+        for k in range(carried):
+            pl.when(head == SETTLE_AT[k])(functools.partial(work.add, k))
+    else:
+        grads, dots = rest[:-1], rest[-1]
     dq_ref, dk_ref, dv_ref = grads if len(grads) == 3 else grads * 3
     head = pl.program_id(0)
     width = q_ref.shape[1]
@@ -182,6 +214,8 @@
     every = pl.ds(0, k_ref.shape[0])
     put(dk_ref, every, base + columns[1], mine, grad_keys * HEAD_DIM ** (-0.5))
     put(dv_ref, every, base + columns[2], mine, grad_values)
+    if work is not None:
+        pl.when(head == pl.num_programs(0) - 1)(work.finish)
 
 
 def put(ref, rows, base, mine, value):
@@ -189,7 +223,9 @@
     ref[rows, window] = jnp.where(mine, value, ref[rows, window].astype(F32)).astype(BF)
 
 
-def attend_backward(parts, seg_query, seg_keys, totals, out, grad, heads):
+def attend_backward(
+    parts, seg_query, seg_keys, totals, out, grad, heads, sums=(), collective=None
+):
     (query, qcol), (keys, kcol), (values, vcol) = parts
     count, tokens = seg_query.shape[0], seg_keys.shape[0]
     width = heads * HEAD_DIM
@@ -200,7 +236,9 @@
         shapes = [(count, width), (tokens, width), (tokens, width)]
         columns = (0, 0, 0)
     return pl.pallas_call(
-        functools.partial(attend_backward_kernel, block=min(256, count), columns=columns),
+        functools.partial(
+            attend_backward_kernel, block=min(256, count), columns=columns, carried=len(sums)
+        ),
         grid=(heads,),
         in_specs=[
             pl.BlockSpec((count, width), lambda h: (0, qcol)),
@@ -211,18 +249,25 @@
             whole((heads, count)),
             whole((count, width)),
             whole((count, width)),
-        ],
-        out_specs=[whole(shape) for shape in shapes],
-        out_shape=[jax.ShapeDtypeStruct(shape, BF) for shape in shapes],
-        scratch_shapes=[pltpu.VMEM((heads, count), F32)],
-        compiler_params=pltpu.CompilerParams(vmem_limit_bytes=60 * 1024 * 1024),
+        ]
+        + [ANY] * len(sums),
+        out_specs=[whole(shape) for shape in shapes] + [ANY] * len(sums),
+        out_shape=[jax.ShapeDtypeStruct(shape, BF) for shape in shapes]
+        + [summed(total) for total in sums],
+        scratch_shapes=[pltpu.VMEM((heads, count), F32)]
+        + (Sum.scratch(sums) if sums else []),
+        compiler_params=pltpu.CompilerParams(
+            vmem_limit_bytes=60 * 1024 * 1024,
+            collective_id=collective,
+            has_side_effects=bool(sums),
+        ),
         cost_estimate=pl.CostEstimate(
             flops=heads * count * tokens * 10 * 256,
             bytes_accessed=2 * width * (4 * count + 4 * tokens),
             transcendentals=heads * count * tokens,
         ),
         name="attend_backward",
-    )(query, keys, values, seg_query, seg_keys, totals, out, grad)
+    )(query, keys, values, seg_query, seg_keys, totals, out, grad, *sums)
 
 
 class Rows:
@@ -357,7 +402,9 @@
     return spec(shape, lambda *_: (0,) * len(shape), once=True)
 
 
-def call(kernel, grid, inputs, outputs, args, name, flops, scratch=(), scalars=None):
+def call(
+    kernel, grid, inputs, outputs, args, name, flops, scratch=(), scalars=None, collective=None
+):
     moved = sum(math.prod(arg.shape) * arg.dtype.itemsize for arg in args)
     moved += sum(math.prod(shape) * jnp.dtype(kind).itemsize for shape, kind, _ in outputs)
     grid_spec = pltpu.PrefetchScalarGridSpec(
@@ -372,7 +419,11 @@
         kernel,
         grid_spec=grid_spec,
         out_shape=[jax.ShapeDtypeStruct(shape, kind) for shape, kind, _ in outputs],
-        compiler_params=pltpu.CompilerParams(vmem_limit_bytes=60 * MIB),
+        compiler_params=pltpu.CompilerParams(
+            vmem_limit_bytes=60 * MIB,
+            collective_id=collective,
+            has_side_effects=collective is not None,
+        ),
         cost_estimate=pl.CostEstimate(flops=flops, bytes_accessed=moved, transcendentals=0),
         name=name,
     )(*given)
@@ -386,44 +437,92 @@
     return [pl.ds(start, min(size, count)) for start in range(0, count, min(size, count))]
 
 
-def project_kernel(x_ref, hot_ref, shift_ref, scale_ref, w_ref, bias_ref, qkv_ref, modt_ref, low_ref):
-    @pl.when(pl.program_id(0) == 0)
+def carry(refs, bundles):
+    refs = list(refs)
+    take = lambda count: [refs.pop(0) for _ in range(count)]
+    return take, (take(len(bundles)), [take(count) for count in bundles])
+
+
+def project_kernel(
+    x_ref, hot_ref, shift_ref, scale_ref, w_ref, bias_ref, seg_ref, *refs, block, bundles
+):
+    take, given = carry(refs, bundles)
+    (goal_in,) = take(1)
+    qkv_ref, modt_ref, out_ref, total_ref = take(4)
+    targets = take(len(bundles))
+    (goal_out,) = take(1)
+    (low_ref,) = take(1)
+    gather = Gather(*given, targets, take(Gather.room(len(bundles))))
+    tokens = Rounds([goal_in], [goal_out], take(2))
+    head = pl.program_id(0)
+    width = x_ref.shape[1]
+
+    @pl.when(head == 0)
     def _():
+        gather.link.greet()
+        gather.start()
+        gather.start_local()
+        tokens.start()
         for rows in chunks(x_ref.shape[0]):
             normed, _ = norm_stats(x_ref[rows, :].astype(F32))
             hot = hot_ref[rows, :]
             low = normed * (1.0 + dot_nn(hot, scale_ref[...])) + dot_nn(hot, shift_ref[...])
             low_ref[rows, :] = low.astype(BF)
             modt_ref[:, rows] = low.astype(BF).T
-
-    weight = square(w_ref[...])
-    for rows in chunks(x_ref.shape[0]):
-        qkv_ref[rows, :] = (dot_nn(low_ref[rows, :], weight) + bias_ref[...]).astype(BF)
-
-
-def project(x, hot, mod, weights, bias):
+        for j in range(3):
+            columns = pl.ds(j * width, width)
+            weight = square(w_ref[:, j])
+            for rows in chunks(x_ref.shape[0]):
+                qkv_ref[rows, columns] = (
+                    dot_nn(low_ref[rows, :], weight) + bias_ref[:, columns]
+                ).astype(BF)
+
+    for index, step in enumerate(gather.steps()):
+        pl.when(head == GATHER_AT[index])(step)
+    parts = ((qkv_ref, 0), (qkv_ref, width), (qkv_ref, 2 * width))
+    attend_head(head, parts, (seg_ref, seg_ref), out_ref, total_ref, block)
+
+    @pl.when(head == pl.num_programs(0) - 1)
+    def _():
+        gather.finish()
+        tokens.finish()
+
+
+def project(x, hot, mod, weights, bias, seg, heads, slices, shards, goals, collective):
     tokens, width = x.shape
     seq, _, per, _ = weights.shape
-    part = lambda index: spec((mod.shape[0], width), lambda j: (0, index), once=True)
+    part = lambda index: spec((mod.shape[0], width), lambda h: (0, index), once=True)
+    flat = list(slices) + [array for shard in shards for array in shard]
     return call(
-        project_kernel,
-        (3,),
+        functools.partial(
+            project_kernel, block=min(256, tokens), bundles=[len(shard) for shard in shards]
+        ),
+        (heads,),
         [
             fixed((tokens, width)),
             fixed(hot.shape),
             part(0),
             part(1),
-            spec((seq, 1, per, width), lambda j: (0, j, 0, 0)),
-            spec((1, width), lambda j: (0, j)),
-        ],
+            spec((seq, 3, per, width), lambda h: (0, 0, 0, 0), once=True),
+            fixed((1, 3 * width)),
+            fixed(seg.shape),
+        ]
+        + [ANY] * (len(flat) + 1),
         [
-            ((tokens, 3 * width), BF, spec((tokens, width), lambda j: (0, j))),
+            ((tokens, 3 * width), BF, fixed((tokens, 3 * width))),
             ((width, tokens), BF, fixed((width, tokens))),
-        ],
-        [x, hot, mod, mod, weights, bias],
+            ((tokens, width), BF, fixed((tokens, width))),
+            ((heads, tokens), F32, fixed((heads, tokens))),
+        ]
+        + [(shape.shape, BF, ANY) for shape in gathered(slices, shards)]
+        + [(goals.shape, BF, ANY)],
+        [x, hot, mod, mod, weights, bias, seg] + flat + [goals],
         "project",
-        6 * tokens * width * width,
-        [pltpu.VMEM((tokens, width), BF)],
+        6 * tokens * width * width + heads * tokens * tokens * 4 * 256,
+        [pltpu.VMEM((tokens, width), BF)]
+        + Gather.scratch(gathered(slices, shards))
+        + Rounds.scratch(1),
+        collective=collective,
     )
 
 
@@ -489,44 +588,56 @@
 
 
 def feed_kernel(
-    low_ref, w_in_ref, b_in_ref, w_out_ref, b_out_ref, mid_ref, hot_ref, gate_ref,
-    actt_ref, slope_ref, res_ref, rest_ref, branch_ref, total,
+    low_ref, w_in_ref, b_in_ref, w_out_ref, b_out_ref, mid_ref, hot_ref, gate_ref, *refs, bundles
 ):
+    take, given = carry(refs, bundles)
+    actt_ref, slope_ref, res_ref, rest_ref, branch_ref = take(5)
+    targets = take(len(bundles))
+    (total,) = take(1)
+    gather = Gather(*given, targets, take(Gather.room(len(bundles))))
+    steps = gather.steps()
     step = pl.program_id(0)
+
+    @pl.when(step == 0)
+    def _():
+        gather.link.greet()
+        gather.start()
+        gather.start_local()
+        total[...] = jnp.zeros_like(total)
+
     w_in, w_out = square(w_in_ref[...]), w_out_ref[...]
-    for rows in chunks(low_ref.shape[0]):
+    pieces = chunks(low_ref.shape[0])
+    for number, rows in enumerate(pieces):
+        if number % 2 == 0:
+            for index, action in enumerate(steps):
+                if FEED_AT[index] % 2 == number // 2:
+                    pl.when(step == FEED_AT[index] // 2)(action)
         hmid = dot_nn(low_ref[rows, :], w_in) + b_in_ref[...]
         act, slope = gelu_pair(hmid)
         act = act.astype(BF)
         slope_ref[rows, :] = slope.astype(BF)
         actt_ref[:, rows] = act.T
-        part = dot_nn(act, w_out)
-
-        @pl.when(step == 0)
-        def _():
-            total[rows, :] = part
-
-        @pl.when(step > 0)
-        def _():
-            total[rows, :] += part
+        total[rows, :] += dot_nn(act, w_out)
 
     @pl.when(step == pl.num_programs(0) - 1)
     def _():
-        for rows in chunks(low_ref.shape[0]):
+        for rows in pieces:
             branch = total[rows, :] + b_out_ref[...]
             result = mid_ref[rows, :] + dot_nn(hot_ref[rows, :], gate_ref[...]) * branch
             result = result.astype(BF)
             res_ref[rows, :] = result
             rest_ref[:, rows] = result.T
             branch_ref[rows, :] = branch.astype(BF)
-
-
-def feed(low, w_in, b_in, w_out, b_out, mid, hot, mod):
+        gather.finish()
+
+
+def feed(low, w_in, b_in, w_out, b_out, mid, hot, mod, slices, shards, collective):
     tokens, width = low.shape
     seq, blocks, per, cut = w_in.shape
     hidden = blocks * cut
+    flat = list(slices) + [array for shard in shards for array in shard]
     return call(
-        feed_kernel,
+        functools.partial(feed_kernel, bundles=[len(shard) for shard in shards]),
         (blocks,),
         [
             fixed((tokens, width)),
@@ -537,18 +648,21 @@
             fixed((tokens, width)),
             fixed(hot.shape),
             spec((mod.shape[0], width), lambda j: (0, 5), once=True),
-        ],
+        ]
+        + [ANY] * len(flat),
         [
             ((hidden, tokens), BF, spec((cut, tokens), lambda j: (j, 0))),
             ((tokens, hidden), BF, spec((tokens, cut), lambda j: (0, j))),
             ((tokens, width), BF, fixed((tokens, width))),
             ((width, tokens), BF, fixed((width, tokens))),
             ((tokens, width), BF, fixed((tokens, width))),
-        ],
-        [low, w_in, b_in, w_out, b_out, mid, hot, mod],
+        ]
+        + [(shape.shape, BF, ANY) for shape in gathered(slices, shards)],
+        [low, w_in, b_in, w_out, b_out, mid, hot, mod] + flat,
         "feed",
         4 * tokens * width * hidden,
-        [pltpu.VMEM((tokens, width), F32)],
+        [pltpu.VMEM((tokens, width), F32)] + Gather.scratch(gathered(slices, shards)),
+        collective=collective,
     )
 
 
@@ -558,9 +672,17 @@
 
 
 def align_kernel(
-    res_ref, w_in_ref, b_in_ref, w_mid_ref, b_mid_ref, w_out_ref, b_out_ref, goal_ref,
-    act1t_ref, act2t_ref, gfeat_ref, gh2_ref, gh1_ref, gout_ref, act1_ref, slope1_ref,
+    res_ref, w_in_ref, b_in_ref, w_mid_ref, b_mid_ref, w_out_ref, b_out_ref, goal_ref, rows_ref,
+    act1t_ref, act2t_ref, gfeat_ref, gh2_ref, gh1_ref, gout_ref, back_ref, act1_ref, slope1_ref,
+    *sems,
 ):
+    tokens = Rounds([rows_ref], [back_ref], sems)
+
+    @pl.when(pl.program_id(0) == 0)
+    def _():
+        tokens.link.greet()
+        tokens.start()
+
     blocks, cut = w_in_ref.shape[1], w_in_ref.shape[3]
     res = res_ref[...]
     for j in range(blocks):
@@ -593,9 +715,10 @@
         part = dot_nt(gh1_ref[:, pl.ds(j * cut, cut)], square(w_in_ref[:, j]))
         total = part if total is None else total + part
     gout_ref[...] = total
-
-
-def align(res, w_in, b_in, w_mid, b_mid, w_out, b_out, goals):
+    pl.when(pl.program_id(0) == pl.num_programs(0) - 1)(tokens.finish)
+
+
+def align(res, w_in, b_in, w_mid, b_mid, w_out, b_out, goals, collective):
     tokens, width = res.shape
     inner, goal_width = w_out.shape
     size = min(256, tokens)
@@ -613,6 +736,7 @@
             fixed(w_out.shape),
             fixed((1, goal_width)),
             rows(goal_width),
+            ANY,
         ],
         [
             ((inner, tokens), BF, turned(inner)),
@@ -621,11 +745,13 @@
             ((tokens, inner), BF, rows(inner)),
             ((tokens, inner), BF, rows(inner)),
             ((tokens, width), F32, rows(width)),
+            ((SEQ, tokens // SEQ, width), BF, ANY),
         ],
-        [res, w_in, b_in, w_mid, b_mid, w_out, b_out, goals],
+        [res, w_in, b_in, w_mid, b_mid, w_out, b_out, goals, res.reshape(SEQ, -1, width)],
         "align",
         4 * tokens * inner * (width + inner + goal_width),
-        [pltpu.VMEM((size, inner), BF), pltpu.VMEM((size, inner), F32)],
+        [pltpu.VMEM((size, inner), BF), pltpu.VMEM((size, inner), F32)] + Rounds.scratch(1),
+        collective=collective,
     )
 
 
@@ -644,20 +770,13 @@
             part = dot_nn(hott_ref[:, rows], (gout * branch_ref[rows, :].astype(F32)).astype(BF))
             sums = part if sums is None else sums + part
         ggate_ref[...] = sums
+        gmod_ref[...] = jnp.zeros_like(gmod_ref)
 
     w_out, w_in = w_out_ref[...], square(w_in_ref[...])
     for rows in chunks(gout_ref.shape[0]):
         ghmid = (dot_nt(gmlp_ref[rows, :], w_out) * slope_ref[rows, :].astype(F32)).astype(BF)
         ghmid_ref[rows, :] = ghmid
-        part = dot_nt(ghmid, w_in)
-
-        @pl.when(step == 0)
-        def _():
-            gmod_ref[rows, :] = part
-
-        @pl.when(step > 0)
-        def _():
-            gmod_ref[rows, :] += part
+        gmod_ref[rows, :] += dot_nt(ghmid, w_in)
 
 
 def feed_back(gout, branch, hot, hott, mod, w_out, slope, w_in):
@@ -754,9 +873,19 @@
 
 
 def project_back_kernel(
-    gqkv_ref, x_ref, gmid_ref, hot_ref, hott_ref, scale_ref, w_ref,
-    gin_ref, gshift_ref, gscale_ref,
+    gqkv_ref, x_ref, gmid_ref, hot_ref, hott_ref, scale_ref, w_ref, *refs, carried
 ):
+    refs = list(refs)
+    take = lambda number: [refs.pop(0) for _ in range(number)]
+    sums = take(carried)
+    gin_ref, gshift_ref, gscale_ref = take(3)
+    work = Sum(sums, take(carried), refs)
+
+    @pl.when(pl.program_id(0) == 0)
+    def _():
+        work.link.greet()
+        work.start()
+
     width = x_ref.shape[1]
     hott = hott_ref[...]
     gmod = None
@@ -771,15 +900,21 @@
     add_rows(gshift_ref, dot_nn(hott, gmod.astype(BF)))
     add_rows(gscale_ref, dot_nn(hott, (gmod * normed).astype(BF)))
 
-
-def project_back(gqkv, x, gmid, hot, hott, mod, weights):
+    @pl.when(pl.program_id(0) == pl.num_programs(0) - 1)
+    def _():
+        for k in range(carried):
+            work.add(k)
+        work.finish()
+
+
+def project_back(gqkv, x, gmid, hot, hott, mod, weights, carried, collective):
     tokens, width = x.shape
     seq, _, per, _ = weights.shape
     size = min(256, tokens)
     rows = spec((size, width), lambda i: (i, 0))
     sums = ((hott.shape[0], width), F32, fixed((hott.shape[0], width)))
     return call(
-        project_back_kernel,
+        functools.partial(project_back_kernel, carried=len(carried)),
         (tokens // size,),
         [
             spec((size, 3 * width), lambda i: (i, 0)),
@@ -789,11 +924,15 @@
             spec((hott.shape[0], size), lambda i: (0, i)),
             spec((mod.shape[0], width), lambda i: (0, 1), once=True),
             spec((seq, 3, per, width), lambda i: (0, 0, 0, 0), once=True),
-        ],
-        [((tokens, width), BF, rows), sums, sums],
-        [gqkv, x, gmid, hot, hott, mod, weights],
+        ]
+        + [ANY] * len(carried),
+        [((tokens, width), BF, rows), sums, sums]
+        + [(total.shape[1:], total.dtype, ANY) for total in carried],
+        [gqkv, x, gmid, hot, hott, mod, weights] + list(carried),
         "project_back",
         6 * tokens * width * width,
+        Sum.scratch(carried),
+        collective=collective,
     )
 
 
@@ -896,12 +1035,24 @@
     def __init__(self, slices, shards, targets, sems):
         self.link = Link()
         self.slices, self.shards, self.targets = slices, shards, targets
-        self.z_sems, self.p_sems, self.c_sems, self.local_sems = sems
+        self.z_sems, self.p_sems, self.c_sems, self.local_sems, self.out_sems = sems[:5]
+        self.bufs = sems[5:]
 
     @staticmethod
-    def scratch(count):
+    def scratch(targets):
         dma = pltpu.SemaphoreType.DMA
-        return [dma((2, count, 3)), dma((2, count, 3, 3)), dma((2, count, 3)), dma((count, 4))]
+        count = len(targets)
+        return [
+            dma((2, count, 3)),
+            dma((2, count, 3, 6)),
+            dma((2, count, 3)),
+            dma((count, 4)),
+            dma((count,)),
+        ] + [pltpu.VMEM(target.shape[1:], BF) for target in targets]
+
+    @staticmethod
+    def room(count):
+        return 5 + count
 
     def rows(self, target):
         half = target.shape[2] // 2
@@ -912,13 +1063,29 @@
             width = target.shape[3]
             block = 0
             for array in shard:
-                for start in range(0, array.shape[1], width):
+                if len(array.shape) == 3:
+                    parts = [array.at[index] for index in range(array.shape[0])]
+                else:
+                    parts = [
+                        array.at[:, pl.ds(start, width)]
+                        for start in range(0, array.shape[1], width)
+                    ]
+                for part in parts:
                     yield pltpu.make_async_copy(
-                        array.at[:, pl.ds(start, width)],
-                        target.at[self.link.z, block],
-                        self.local_sems.at[k, block],
+                        part, self.bufs[k].at[block], self.local_sems.at[k, block]
                     )
                     block += 1
+
+    def stored(self, k):
+        return pltpu.make_async_copy(
+            self.bufs[k], self.targets[k].at[self.link.z], self.out_sems.at[k]
+        )
+
+    def store(self):
+        for copy in self.locals():
+            copy.wait()
+        for k in range(len(self.targets)):
+            self.stored(k).start()
 
     def along(self, k, shift, incoming):
         link, target = self.link, self.targets[k]
@@ -931,16 +1098,25 @@
             link.ahead(shift),
         )
 
-    def across(self, k, shift, bit, incoming):
+    def across(self, k, shift, index, incoming):
         link, target = self.link, self.targets[k]
-        plane = link.across(bit)
-        place = (link.behind(shift), plane if incoming else link.p, self.rows(target))
+        half = target.shape[2] // 2
+        first = -(-half // 32) * 16
+        start, size = ((0, first), (first, half - first))[index % 2]
+        peer = (1, 1, 2, 2, 2, 1)[index]
+        plane = link.p
+        if incoming:
+            plane = link.across(3 if index >= 4 else peer)
+        elif index >= 4:
+            plane = link.across(3 - peer)
+        rows = pl.ds(pl.multiple_of(link.c * half + start, 16), size)
+        place = target.at[link.behind(shift), plane, rows, :]
         return link.copy(
-            target.at[place],
-            target.at[place],
-            (self.p_sems.at[0, k, shift - 1, bit - 1], self.p_sems.at[1, k, shift - 1, bit - 1]),
+            place,
+            place,
+            (self.p_sems.at[0, k, shift - 1, index], self.p_sems.at[1, k, shift - 1, index]),
             "plane",
-            plane,
+            link.across(peer),
         )
 
     def beside(self, k, shift, incoming):
@@ -966,14 +1142,28 @@
         for copy in self.locals():
             copy.start()
 
+    def steps(self):
+        return [self.store] + [
+            functools.partial(stage, k, shift)
+            for k in range(len(self.targets))
+            for stage in (self.spread, self.relay, self.pair)
+            for shift in (1, 3, 2)
+        ]
+
     def spread(self, k, shift):
         self.along(k, shift, True).wait_recv()
-        for bit in range(1, PLANES):
-            self.across(k, shift, bit, False).start()
+        for index in (0, 3, 1, 2):
+            self.across(k, shift, index, False).start()
+
+    def relay(self, k, shift):
+        self.across(k, shift, 0, True).wait_recv()
+        self.across(k, shift, 4, False).start()
+        self.across(k, shift, 3, True).wait_recv()
+        self.across(k, shift, 5, False).start()
 
     def pair(self, k, shift):
-        for bit in range(1, PLANES):
-            self.across(k, shift, bit, True).wait_recv()
+        for index in (1, 2, 4, 5):
+            self.across(k, shift, index, True).wait_recv()
         self.beside(k, shift, False).start()
 
     def finish(self):
@@ -982,10 +1172,9 @@
                 self.beside(k, shift, True).wait_recv()
                 self.along(k, shift, False).wait_send()
                 self.beside(k, shift, False).wait_send()
-                for bit in range(1, PLANES):
-                    self.across(k, shift, bit, False).wait_send()
-        for copy in self.locals():
-            copy.wait()
+                for index in range(6):
+                    self.across(k, shift, index, False).wait_send()
+            self.stored(k).wait()
 
 
 class Rounds:
@@ -1028,45 +1217,93 @@
             self.local(k).wait()
 
 
-class Finish:
-    def __init__(self, sources, targets, refs):
+class Sum:
+    def __init__(self, sources, results, refs):
         self.link = Link()
-        self.sources, self.targets = sources, targets
-        count = len(sources)
-        self.bufs = refs[:count]
-        self.z_sems, self.p_sems, self.c_sems, self.local_sems = refs[count:]
+        self.sources, self.results = sources, results
+        self.bufs = refs[: len(sources)]
+        self.sems, self.local_sems = refs[len(sources) :]
 
     @staticmethod
-    def scratch(shapes):
+    def scratch(sources):
         dma = pltpu.SemaphoreType.DMA
-        count = len(shapes)
-        bufs = [
-            pltpu.VMEM((9 if shared else 5,) + tuple(shape), BF) for shape, shared in shapes
-        ]
-        return bufs + [dma((2, count, 3)), dma((2, count, 3)), dma((2, count, 4)), dma((count, 2))]
-
-    def shared(self, k):
-        return len(self.targets[k].shape) == 3
+        bufs = [pltpu.VMEM((5,) + source.shape[1:], source.dtype) for source in sources]
+        return bufs + [dma((2, len(sources), 3)), dma((len(sources), 2))]
 
     def along(self, k, shift):
         link = self.link
         return link.copy(
             self.sources[k].at[link.ahead(shift)],
             self.bufs[k].at[shift - 1],
-            (self.z_sems.at[0, k, shift - 1], self.z_sems.at[1, k, shift - 1]),
+            (self.sems.at[0, k, shift - 1], self.sems.at[1, k, shift - 1]),
             "seq",
             link.ahead(shift),
         )
+
+    def mine(self, k):
+        return pltpu.make_async_copy(
+            self.sources[k].at[self.link.z], self.bufs[k].at[3], self.local_sems.at[k, 0]
+        )
+
+    def stored(self, k):
+        return pltpu.make_async_copy(
+            self.bufs[k].at[4], self.results[k], self.local_sems.at[k, 1]
+        )
+
+    def start(self):
+        for k in range(len(self.sources)):
+            for shift in (2, 1, 3):
+                self.along(k, shift).start()
+            self.mine(k).start()
+
+    def add(self, k):
+        for shift in range(1, SEQ):
+            self.along(k, shift).wait_recv()
+        self.mine(k).wait()
+        buf = self.bufs[k]
+        total = buf[0].astype(F32) + buf[1].astype(F32) + buf[2].astype(F32) + buf[3].astype(F32)
+        buf[4] = total.astype(buf.dtype)
+        self.stored(k).start()
+
+    def finish(self):
+        for k in range(len(self.sources)):
+            for shift in range(1, SEQ):
+                self.along(k, shift).wait_send()
+            self.stored(k).wait()
+
+
+class Share:
+    def __init__(self, sources, targets, refs):
+        self.link = Link()
+        self.sources, self.targets = sources, targets
+        self.bufs = refs[: len(sources)]
+        self.p_sems, self.c_sems, self.local_sems = refs[len(sources) :]
+
+    @staticmethod
+    def scratch(sources, shared):
+        dma = pltpu.SemaphoreType.DMA
+        count = len(sources)
+        bufs = [
+            pltpu.VMEM((5 if one else 1,) + source.shape[-2:], source.dtype)
+            for source, one in zip(sources, shared)
+        ]
+        return bufs + [dma((2, count, 3)), dma((2, count, 4)), dma((count, 2))]
+
+    def shared(self, k):
+        return len(self.targets[k].shape) == 3
+
+    def loaded(self, k):
+        return pltpu.make_async_copy(self.sources[k], self.bufs[k].at[0], self.local_sems.at[k, 0])
 
     def across(self, k, bit, incoming):
         link = self.link
         plane = link.across(bit)
         if self.shared(k):
-            target = self.bufs[k].at[4 + bit]
+            target = self.bufs[k].at[bit]
         else:
             target = self.targets[k].at[plane if incoming else link.p, link.c]
         return link.copy(
-            self.bufs[k].at[4],
+            self.bufs[k].at[0],
             target,
             (self.p_sems.at[0, k, bit - 1], self.p_sems.at[1, k, bit - 1]),
             "plane",
@@ -1077,11 +1314,11 @@
         link = self.link
         core = 1 - link.c if incoming else link.c
         if self.shared(k):
-            source, target = self.bufs[k].at[8], self.targets[k].at[core]
+            source, target = self.bufs[k].at[4], self.targets[k].at[core]
         else:
             plane = link.across(bit)
             target = self.targets[k].at[plane, core]
-            source = self.bufs[k].at[4] if bit == 0 else self.targets[k].at[plane, link.c]
+            source = self.bufs[k].at[0] if bit == 0 else self.targets[k].at[plane, link.c]
         return link.copy(
             source,
             target,
@@ -1090,32 +1327,15 @@
             1 - link.c,
         )
 
-    def mine(self, k):
-        return pltpu.make_async_copy(
-            self.sources[k].at[self.link.z], self.bufs[k].at[3], self.local_sems.at[k, 0]
-        )
-
     def own(self, k):
         link = self.link
         if self.shared(k):
-            source, target = self.bufs[k].at[8], self.targets[k].at[link.c]
+            source, target = self.bufs[k].at[4], self.targets[k].at[link.c]
         else:
-            source, target = self.bufs[k].at[4], self.targets[k].at[link.p, link.c]
+            source, target = self.bufs[k].at[0], self.targets[k].at[link.p, link.c]
         return pltpu.make_async_copy(source, target, self.local_sems.at[k, 1])
 
-    def start(self):
-        for k in range(len(self.sources)):
-            for shift in (2, 1, 3):
-                self.along(k, shift).start()
-            self.mine(k).start()
-
-    def add(self, k):
-        for shift in range(1, SEQ):
-            self.along(k, shift).wait_recv()
-        self.mine(k).wait()
-        buf = self.bufs[k]
-        total = buf[0].astype(F32) + buf[1].astype(F32) + buf[2].astype(F32) + buf[3].astype(F32)
-        buf[4] = total.astype(BF)
+    def send(self, k):
         for bit in range(1, PLANES):
             self.across(k, bit, False).start()
         if not self.shared(k):
@@ -1129,19 +1349,18 @@
                 self.beside(k, bit, False).start()
         if self.shared(k):
             buf = self.bufs[k]
-            total = buf[4].astype(F32) + buf[5].astype(F32) + buf[6].astype(F32) + buf[7].astype(F32)
-            buf[8] = total.astype(BF)
+            total = buf[0].astype(F32) + buf[1].astype(F32) + buf[2].astype(F32) + buf[3].astype(F32)
+            buf[4] = total.astype(buf.dtype)
             self.own(k).start()
             self.beside(k, 0, False).start()
 
     def finish(self):
-        for k in range(len(self.sources)):
+        for k in range(len(self.targets)):
             for bit in range(1 if self.shared(k) else PLANES):
                 self.beside(k, bit, True).wait_recv()
                 self.beside(k, bit, False).wait_send()
-            for step in range(1, SEQ):
-                self.along(k, step).wait_send()
-                self.across(k, step, False).wait_send()
+            for bit in range(1, PLANES):
+                self.across(k, bit, False).wait_send()
             self.own(k).wait()
 
 
@@ -1153,29 +1372,33 @@
     sources = take(rounds)
     targets = take(len(bundles))
     arrived = take(rounds)
-    gather = Gather(slices, shards, targets, take(4))
+    gather = Gather(slices, shards, targets, take(Gather.room(len(bundles))))
     tokens = Rounds(sources, arrived, take(2))
     gather.link.greet()
     gather.start()
     tokens.start()
     gather.start_local()
-    for k in range(len(bundles)):
-        for shift in (1, 3, 2):
-            gather.spread(k, shift)
-        for shift in (1, 3, 2):
-            gather.pair(k, shift)
+    for step in gather.steps():
+        step()
     tokens.finish()
     gather.finish()
 
 
+def gathered(slices, shards):
+    shapes = []
+    for piece, shard in zip(slices, shards):
+        cut = piece.shape[1]
+        if shard[0].ndim == 3:
+            blocks, per = shard[0].shape[:2]
+        else:
+            blocks, per = sum(array.shape[1] for array in shard) // cut, shard[0].shape[0]
+        shapes.append(jax.ShapeDtypeStruct((SEQ, blocks, per, cut), BF))
+    return shapes
+
+
 def bring(slices, shards, sources, collective):
-    per = [shard[0].shape[0] for shard in shards]
-    cut = [piece.shape[1] for piece in slices]
-    blocks = [sum(a.shape[1] for a in shard) // n for shard, n in zip(shards, cut)]
     flat = [array for shard in shards for array in shard]
-    shapes = [
-        jax.ShapeDtypeStruct((SEQ, b, r, n), BF) for b, r, n in zip(blocks, per, cut)
-    ] + [jax.ShapeDtypeStruct(array.shape, array.dtype) for array in sources]
+    shapes = gathered(slices, shards) + [jax.ShapeDtypeStruct(array.shape, array.dtype) for array in sources]
     args = list(slices) + flat + list(sources)
     return pl.pallas_call(
         functools.partial(
@@ -1184,7 +1407,7 @@
         in_specs=[ANY] * len(args),
         out_specs=[ANY] * len(shapes),
         out_shape=shapes,
-        scratch_shapes=Gather.scratch(len(slices)) + Rounds.scratch(len(sources)),
+        scratch_shapes=Gather.scratch(gathered(slices, shards)) + Rounds.scratch(len(sources)),
         compiler_params=pltpu.CompilerParams(
             collective_id=collective, has_side_effects=True, vmem_limit_bytes=60 * MIB
         ),
@@ -1193,41 +1416,71 @@
     )(*args)
 
 
-def settle_kernel(*refs, count, rounds):
+def settle_kernel(*refs, sums, shares, rounds, through):
     refs = list(refs)
     take = lambda number: [refs.pop(0) for _ in range(number)]
-    sums, sources = take(count), take(rounds)
-    targets, arrived = take(count), take(rounds)
-    work = Finish(sums, targets, take(count + 4))
-    tokens = Rounds(sources, arrived, take(2)) if rounds else None
-    work.link.greet()
-    work.start()
+    sum_in, share_in, round_in = take(sums), take(shares), take(rounds)
+    sum_out, share_out, round_out = take(sums), take(shares + sums * through), take(rounds)
+    add = Sum(sum_in, sum_out, take(sums + 2))
+    share = Share(share_in + sum_in * through, share_out, take(len(share_out) + 3))
+    tokens = Rounds(round_in, round_out, take(2)) if rounds else None
+    add.link.greet()
+    add.start()
     if rounds:
         tokens.start()
-    for k in range(count):
-        work.add(k)
-    for k in range(count):
-        work.pass_on(k)
-    work.finish()
+    for k in range(shares):
+        share.loaded(k).start()
+    for k in range(shares):
+        share.loaded(k).wait()
+        share.send(k)
+    for k in range(shares):
+        share.pass_on(k)
+    for k in range(sums):
+        add.add(k)
+        if through:
+            share.bufs[shares + k][0] = add.bufs[k][4]
+            share.send(shares + k)
+    if through:
+        for k in range(sums):
+            share.pass_on(shares + k)
+    add.finish()
+    share.finish()
     if rounds:
         tokens.finish()
 
 
-def settle(sums, shared, sources, collective):
-    shapes = [
-        jax.ShapeDtypeStruct(((2,) if one else (PLANES, 2)) + total.shape[1:], BF)
-        for total, one in zip(sums, shared)
-    ] + [jax.ShapeDtypeStruct(array.shape, array.dtype) for array in sources]
-    args = list(sums) + list(sources)
-    scratch = Finish.scratch([(total.shape[1:], one) for total, one in zip(sums, shared)])
-    if sources:
-        scratch = scratch + Rounds.scratch(len(sources))
+def summed(array):
+    return jax.ShapeDtypeStruct(array.shape[1:], array.dtype)
+
+
+def shared_out(array, shared):
+    return jax.ShapeDtypeStruct(
+        ((2,) if shared else (PLANES, 2)) + array.shape[-2:], array.dtype
+    )
+
+
+def settle(sums, shares, rounds, shared, collective, through=False):
+    args = list(sums) + list(shares) + list(rounds)
+    given = list(shares) + (list(sums) if through else [])
+    shapes = (
+        [summed(array) for array in sums]
+        + [shared_out(array, one) for array, one in zip(given, shared)]
+        + [jax.ShapeDtypeStruct(array.shape, array.dtype) for array in rounds]
+    )
     return pl.pallas_call(
-        functools.partial(settle_kernel, count=len(sums), rounds=len(sources)),
+        functools.partial(
+            settle_kernel,
+            sums=len(sums),
+            shares=len(shares),
+            rounds=len(rounds),
+            through=int(through),
+        ),
         in_specs=[ANY] * len(args),
         out_specs=[ANY] * len(shapes),
         out_shape=shapes,
-        scratch_shapes=scratch,
+        scratch_shapes=Sum.scratch(sums)
+        + Share.scratch(given, shared)
+        + (Rounds.scratch(len(rounds)) if rounds else []),
         compiler_params=pltpu.CompilerParams(
             collective_id=collective, has_side_effects=True, vmem_limit_bytes=60 * MIB
         ),
@@ -1471,51 +1724,27 @@
     return full.reshape(lax.axis_size("plane"), 2, own.shape[0], own.shape[1])
 
 
-def sum_vectors(packed):
-    bit = 1
-    total = packed + swap_cores(packed)
-    while bit < lax.axis_size("plane"):
-        total = total + swap_planes(total, bit)
-        bit *= 2
-    seq = lax.axis_size("seq")
-    here = lax.axis_index("seq")
-    own = lax.dynamic_index_in_dim(total, here, 0, keepdims=False)
-    for shift in range(1, seq):
-        piece = lax.dynamic_index_in_dim(total, (here + shift) % seq, 0, keepdims=False)
-        own = own + lax.ppermute(piece, "seq", [(z, (z + shift) % seq) for z in range(seq)])
-    return own
-
-
-def exchange(array):
-    seq = lax.axis_size("seq")
-    here = lax.axis_index("seq")
-    result = array
-    for shift in range(1, seq):
-        piece = lax.dynamic_index_in_dim(array, (here + shift) % seq, 0, keepdims=False)
-        piece = lax.ppermute(piece, "seq", [(z, (z + shift) % seq) for z in range(seq)])
-        result = lax.dynamic_update_index_in_dim(result, piece, (here + seq - shift) % seq, 0)
-    return result
-
-
-def unpack_kernel(full_ref, out_ref):
-    out_ref[...] = full_ref[0, 0].astype(F32)
-
-
-def unpack(full, columns=None):
-    planes, _, count, cut = full.shape
-    if columns is None:
-        shape, place = (planes * 2 * count, cut), (lambda p, c: (2 * p + c, 0))
-    else:
-        shape, place = (2 * count, columns), (lambda p, c: (c, p))
+def unpack_kernel(*refs):
+    count = len(refs) // 2
+    for full_ref, out_ref in zip(refs[:count], refs[count:]):
+        out_ref[...] = square(full_ref[...]).astype(F32)
+
+
+def unpack(*fulls):
+    planes = fulls[0][0].shape[0]
+    inputs, outputs = [], []
+    for full, columns in fulls:
+        _, _, count, cut = full.shape
+        inputs.append(spec((1, 2, count, cut), lambda p: (p, 0, 0, 0)))
+        if columns is None:
+            outputs.append(
+                ((planes * 2 * count, cut), F32, spec((2 * count, cut), lambda p: (p, 0)))
+            )
+        else:
+            outputs.append(((2 * count, columns), F32, spec((2 * count, cut), lambda p: (0, p))))
     return call(
-        unpack_kernel,
-        (planes, 2),
-        [spec((1, 1, count, cut), lambda p, c: (p, c, 0, 0))],
-        [(shape, F32, spec((count, cut), place))],
-        [full],
-        "unpack",
-        0,
-    )[0]
+        unpack_kernel, (planes,), inputs, outputs, [full for full, _ in fulls], "unpack", 0
+    )
 
 
 def local_row(
@@ -1540,16 +1769,18 @@
 
     slice1, _ = own_slice([qkv_weight, attn_out_weight], width)
     slice2, _ = own_slice([mlp_in_weight], width)
-    third = gather_slices(own_slice([mlp_out_weight], width))
-    w1, w2, x, seg_own = bring(
-        [slice1, slice2],
-        [[qkv_weight, attn_out_weight], [mlp_in_weight]],
+    slice3, _ = own_slice([mlp_out_weight], width)
+    slice4, _ = own_slice([proj_in_weight], inner // planes)
+    slice5, _ = own_slice([proj_mid_weight], inner)
+    slice6, _ = own_slice([proj_out_weight], goal_width)
+    w1, x, seg_own = bring(
+        [slice1],
+        [[qkv_weight, attn_out_weight]],
         [block_input, segment_ids.reshape(rows, -1, LANES)],
         0,
     )
     x = x.reshape(tokens, width)
     seg_own = seg_own.reshape(tokens)
-    goals = exchange(tie(targets, x)).reshape(tokens, goal_width)
     mod_row = lax.dynamic_index_in_dim(modulation, lax.axis_index("seq"), 0, keepdims=False)
     mod = jnp.pad(mod_row, ((0, 16 - mod_row.shape[0]), (0, 0)))
     hot = (seg_own[:, None] == jnp.arange(16, dtype=jnp.int32)[None, :]).astype(BF)
@@ -1562,30 +1793,32 @@
     full_bias = jnp.concatenate(
         [bias_float[:width], jnp.zeros((width,), F32), bias_float[width:]]
     )
-    qkv, mod1t = project(x, hot, mod, w1, full_bias[None, :])
-    fourth = gather_slices(own_slice([tie(proj_in_weight, x)], inner // planes))
-    fifth = gather_slices(own_slice([tie(proj_mid_weight, x)], inner))
-    sixth = gather_slices(own_slice([tie(proj_out_weight, x)], goal_width))
+    by_rows = lambda weight: weight.reshape(planes, -1, weight.shape[1])
+    qkv, mod1t, attended, totals, w2, w3, goals = project(
+        x, hot, mod, w1, full_bias[None, :], seg_column, heads,
+        [slice2, slice3], [[mlp_in_weight], [by_rows(mlp_out_weight)]], targets, 3,
+    )
+    goals = goals.reshape(tokens, goal_width)
     parts = ((qkv, 0), (qkv, 1), (qkv, 2))
-    attended, totals = attend_forward(parts, seg_column, seg_column, heads)
     branch, mid, low2, mod2t, attt = merge(attended, x, hot, mod, w1, vector(attn_out_bias))
-    w3 = third.reshape(hidden, width)
-    actt, slope, out_low, outt, mlp_branch = feed(
-        low2, w2, vector(mlp_in_bias), w3, vector(mlp_out_bias), mid, hot, mod
-    )
-    w4 = fourth.reshape(seq, planes, per, inner // planes)
-    w5, w6 = fifth.reshape(inner, inner), sixth.reshape(inner, goal_width)
-    act1t, act2t, gfeat, gh2, gh1, gout = align(
-        out_low, w4, vector(proj_in_bias), w5, vector(proj_mid_bias), w6, vector(proj_out_bias), goals
-    )
-    block_out = exchange(tie(out_low, gout).reshape(block_input.shape))
-
+    w3 = w3.reshape(hidden, width)
+    actt, slope, out_low, outt, mlp_branch, w4, w5, w6 = feed(
+        low2, w2, vector(mlp_in_bias), w3, vector(mlp_out_bias), mid, hot, mod,
+        [slice4, slice5, slice6],
+        [[proj_in_weight], [by_rows(proj_mid_weight)], [by_rows(proj_out_weight)]],
+        5,
+    )
+    w5, w6 = w5.reshape(inner, inner), w6.reshape(inner, goal_width)
+    act1t, act2t, gfeat, gh2, gh1, gout, block_out = align(
+        out_low, w4, vector(proj_in_bias), w5, vector(proj_mid_bias), w6, vector(proj_out_bias),
+        goals, 7,
+    )
     half = functools.partial(weight_half, where, seq=seq, planes=planes)
-    other6, sum6 = half(act2t, tie(gfeat, gout), by_columns=False)
+    other6, column6 = half(act2t, tie(gfeat, gout), by_columns=False)
     got6 = swap_cores(other6)
-    other5, sum5 = half(act1t, tie(gh2, other6), by_columns=True)
+    other5, column5 = half(act1t, tie(gh2, other6), by_columns=True)
     got5 = swap_cores(other5)
-    other4, sum4 = half(outt, tie(gh1, other5), by_columns=True)
+    other4, column4 = half(outt, tie(gh1, other5), by_columns=True)
     got4 = swap_cores(other4)
     (own6,) = half(act2t, tie(gfeat, other4), by_columns=False, got=got6)
     (own5,) = half(act1t, tie(gh2, own6), by_columns=True, got=got5)
@@ -1596,30 +1829,32 @@
     gmlp, ghmid, gmod2, ggate2 = feed_back(
         tie(gout, own4), mlp_branch, hot, hott, mod, w3, slope, w2
     )
-    other3, sum3 = half(actt, tie(gmlp, gmod2), by_columns=False)
+    other3, column3 = half(actt, tie(gmlp, gmod2), by_columns=False)
     got3 = swap_cores(other3)
-    other2, sum2 = half(mod2t, tie(ghmid, other3), by_columns=True)
+    other2, column2 = half(mod2t, tie(ghmid, other3), by_columns=True)
     got2 = swap_cores(other2)
     (own3,) = half(actt, tie(gmlp, other2), by_columns=False, got=got3)
     plane3 = scatter_planes(own3)
-    (own2,) = half(mod2t, tie(ghmid, own3), by_columns=True, got=got2)
+    gmid, gbranch, gatt, gshift2, gscale2, ggate1 = merge_back(
+        gout, tie(gmod2, own3), mid, branch, hot, hott, mod, w1
+    )
+    half1 = functools.partial(weight_half, where, seq=seq, planes=1)
+    other0, column0 = half1(attt, tie(gbranch, gatt), by_columns=True)
+    got0 = swap_cores(other0)
+    (own2,) = half(mod2t, tie(ghmid, other0), by_columns=True, got=got2)
     plane2 = scatter_planes(own2)
-    gmid, gbranch, gatt, gshift2, gscale2, ggate1 = merge_back(
-        gout, tie(gmod2, own2), mid, branch, hot, hott, mod, w1
-    )
-    half1 = functools.partial(weight_half, where, seq=seq, planes=1)
-    other0, sum0 = half1(attt, tie(gbranch, gatt), by_columns=True)
-    got0 = swap_cores(other0)
-    (gqkv,) = attend_backward(parts, seg_column, seg_column, totals, attended, tie(gatt, other0), heads)
-    (own0,) = half1(attt, tie(gbranch, gqkv), by_columns=True, got=got0)
-    other1, sum1 = half(mod1t, tie(gqkv, own0), by_columns=True)
+    (own0,) = half1(attt, tie(gbranch, own2), by_columns=True, got=got0)
+    gqkv, sum6, sum4, sum5, own_attn = attend_backward(
+        parts, seg_column, seg_column, totals, attended, tie(gatt, own0), heads,
+        [plane6, plane4, plane5, own0[0]], 4,
+    )
+    other1, column1 = half(mod1t, tie(gqkv, other0), by_columns=True)
     got1 = swap_cores(other1)
-    gin, gshift1, gscale1 = project_back(
-        tie(gqkv, other1), x, gmid, hot, hott, mod, w1
+    gin, gshift1, gscale1, sum3 = project_back(
+        tie(gqkv, other1), x, gmid, hot, hott, mod, w1, [plane3], 6
     )
     (own1,) = half(mod1t, tie(gqkv, gin), by_columns=True, got=got1)
     plane1 = scatter_planes(own1)
-    grad_input = exchange(gin.reshape(block_input.shape)).astype(F32)
 
     segs = modulation.shape[1]
     grad_mod = jnp.concatenate(
@@ -1627,21 +1862,32 @@
     )[:segs].astype(BF)
     grad_mod = jnp.pad(grad_mod.reshape(-1, LANES), ((0, 8), (0, 0)))
     grad_mod = jnp.broadcast_to(grad_mod[None], (rows,) + grad_mod.shape)
-    full6, full5, full4, full3, full2, full0 = settle(
-        [plane6, plane5, plane4, plane3, plane2, tie(own0[0], own1)],
-        [False] * 5 + [True],
-        [],
-        1,
-    )
-    full1, all_mod = settle([plane1], [False], [tie(grad_mod, full0)], 2)
-    grad_modulation = all_mod[:, :-8].reshape(rows, segs, 6 * width).astype(F32)
-
-    columns1 = sum1[0]
+    columns1 = column1[0]
     biases = [
         jnp.concatenate([columns1[:width], columns1[2 * width : 3 * width]]),
-        sum0[0], sum2[0], sum3[0], sum4[0], sum5[0], sum6[0],
+        column0[0], column2[0], column3[0], column4[0], column5[0], column6[0],
     ]
-    packed = sum_vectors(jnp.concatenate([bias.reshape(seq, -1) for bias in biases], axis=1))
+    packed = jnp.concatenate([bias.reshape(seq, -1) for bias in biases], axis=1)
+    count = -(-packed.shape[1] // (8 * LANES)) * 8 * LANES
+    packed = jnp.pad(packed, ((0, 0), (0, count - packed.shape[1]))).reshape(seq, -1, LANES)
+    sum2, full6, full5, full4, full3, full0, grad_input = settle(
+        [plane2],
+        [sum6, sum5, sum4, sum3, tie(own_attn, own1)],
+        [gin.reshape(block_input.shape)],
+        [False] * 4 + [True],
+        1,
+    )
+    _, _, full2, full1, all_bias, all_mod = settle(
+        [tie(plane1, sum2), packed], [sum2], [grad_mod], [False, False, True], 2, True
+    )
+    grad_input = grad_input.astype(F32)
+    grad3, grad4, grad5, grad6 = unpack(
+        (full3, None), (full4, inner), (full5, inner), (full6, None)
+    )
+    grad2, grad1 = unpack((full2, hidden), (full1, 3 * width))
+    grad_modulation = all_mod[:, :-8].reshape(rows, segs, 6 * width).astype(F32)
+
+    packed = (all_bias[0] + all_bias[1]).reshape(-1)
     shares = []
     start = 0
     for bias in biases:
@@ -1653,19 +1899,19 @@
         block_out,
         grad_input,
         grad_modulation,
-        unpack(full1, 3 * width),
+        grad1,
         shares[0],
         full0.reshape(per, width).astype(F32),
         shares[1],
-        unpack(full2, hidden),
+        grad2,
         shares[2],
-        unpack(full3),
+        grad3,
         shares[3],
-        unpack(full4, inner),
+        grad4,
         shares[4],
-        unpack(full5, inner),
+        grad5,
         shares[5],
-        unpack(full6),
+        grad6,
         shares[6],
     )
 

time: 1110 us -> 885 us (0.80)
  waiting for transfers between devices: 155 us -> 3.71 us
  Pallas kernels: 848 us -> 803 us
  starting transfers between devices: 17.5 us -> 3.35 us
  local copies, waits for them, and re-layouts: 47.4 us -> 33.5 us
    pallas_call x27 -> x23, Pallas kernels: 355 us -> 502 us  [call(): pl.pallas_call(kernel, grid_spec=grid_spec, out_shape=[jax.ShapeDtypeStru...]
    pallas_call x3 -> x2, Pallas kernels: 242 us -> 128 us  [settle(): pl.pallas_call(functools.partial(settle_kernel, sums=len(sums), shares=le...]
    pallas_call x1, Pallas kernels: 183 us -> 83.8 us  [bring(): pl.pallas_call(functools.partial(bring_kernel, bundles=[len(shard) for sh...]
    all_gather x4 -> x0, waiting for transfers between devices: 79.4 us -> none  [gather_slices(): return lax.all_gather(own, EVERY, axis=0, tiled=True).reshape(shape)]
    ppermute x14 -> x0, waiting for transfers between devices: 74.9 us -> none  [the longest x9 70.6 us: exchange(): lax.ppermute(piece, 'seq', [(z, (z + shift) % seq) for z in range(seq)])]
    pallas_call x1, Pallas kernels: 67.1 us -> 88.6 us  [attend_backward(): pl.pallas_call(functools.partial(attend_backward_kernel, block=min(256, c...]
    ppermute x14 -> x0, starting transfers between devices: 14.3 us -> none  [the longest x9 8.39 us: exchange(): lax.ppermute(piece, 'seq', [(z, (z + shift) % seq) for z in range(seq)])]
  transfers between devices with their start and end apart: 32 -> 13, of which waited for: 10 -> 1; matrix products, arithmetic and copies ran while one was open for 5% -> 2% of each run, Pallas kernels for 67% -> 44%
where the time goes in v3:
time: 885 us; the launch traced here: 872 us
  Pallas kernels  803 us (91%)
  local copies, waits for them, and re-layouts  33.5 us (4%)
  between operations  15 us (2%)
  other arithmetic  13.3 us (2%)
    pallas_call x23, Pallas kernels, call(): pl.pallas_call(kernel, grid_spec=grid_spec, out_shape=[jax.ShapeDtypeStru...  502 us
    pallas_call x2, Pallas kernels, settle(): pl.pallas_call(functools.partial(settle_kernel, sums=len(sums), shares=le...  128 us
    pallas_call x1, Pallas kernels, attend_backward(): pl.pallas_call(functools.partial(attend_backward_kernel, block=min(256, c...  88.6 us
    pallas_call x1, Pallas kernels, bring(): pl.pallas_call(functools.partial(bring_kernel, bundles=[len(shard) for sh...  83.8 us
  transfers between devices with their start and end apart: 13, of which 1 were waited for; matrix products, arithmetic and copies ran while one was open for 2% of the time, Pallas kernels for 44%

profile of v3, /device:TPU:9, one launch (start us, length us, event | category | flops | bytes accessed | tf_op | source)
XLA Modules:
  0.0 872.2 jit_solution(5671954478151216512)
XLA Ops:
  7.3 1.3 reshape.167.refs_4_
  8.6 2.0 dynamic-slice_select_fusion.refs_0_
  10.7 83.8 %bring.1 = (bf16[4,4,288,1152]{3,2,1,0:T(8,128)(2,1)}, bf16[4,256,1152]{2,1,0:T(8,128)(2,1)}, s32[4,2,128]{2,1,0:T(2,128)}) custom-call(bf16[144,1152]{1,0:T(8,128)(2,1)} %dynamic-slice_select_fusion.refs_0_, bf16[288,3456]{1,0:T(8,128)(2,1)} %refs_1_.1, bf16[288,1152]{1,0:T(8,128)(2,1)} %refs_2_.2, bf16[4,256,1152]{2,1,0:T(8,128)(2,1)} %refs_3_.2, ...), custom_call_target="tpu_custom_call" | custom-call | bytes 300000000 | tf_op jit(solution)/shard_map/bring/pallas_call | solution.py:1403
  94.5 1.6 fusion.hot_ref
  96.1 1.7 copy.35.seg_ref.segq_ref.segk_ref
  99.0 1.7 constant_dynamic-slice_fusion.1.refs_1_
  100.7 1.5 constant_dynamic-slice_fusion.refs_2_
  105.2 1.9 dynamic_slice.29.refs_0_
  107.1 1.8 constant_dynamic-slice_fusion.2.refs_1_
  109.7 111.2 %project.1 = (bf16[1024,3456]{1,0:T(8,128)(2,1)}, bf16[1152,1024]{1,0:T(8,128)(2,1)}, bf16[1024,1152]{1,0:T(8,128)(2,1)}, f32[16,1024]{1,0:T(8,128)}, bf16[4,4,2...) custom-call(bf16[1024,1152]{1,0:T(8,128)(2,1)} %bitcast.63, ...), custom_call_target="tpu_custom_call" | custom-call | flops 25333596160 | bytes 55682560 | tf_op jit(solution)/shard_map/project/pallas_call | solution.py:418
  220.8 10.8 %merge.1 = (bf16[1024,1152]{1,0:T(8,128)(2,1)}, f32[1024,1152]{1,0:T(8,128)}, bf16[1024,1152]{1,0:T(8,128)(2,1)}, bf16[1152,1024]{1,0:T(8,128)(2,1)}, bf16[1152,1024]{1,0:T(8,128)(2,1)}) custom-call(bf16[1024,1152]{1,0:T(8,128)(2,1)} %get-tuple-element.120.out_ref, bf16[1024,1152]{1,0:T(8,128)(2,1)} %bitcast.64, bf16[1024,16]{1,0:T(8,128)(2,1)} %fusion.hot_ref, ...), custom_call_target="tpu_custom_call" | custom-call | flops 2717908992 | bytes 30192128 | tf_op jit(solution)/shard_map/merge/pallas_call | solution.py:418
  231.6 1.7 dynamic_slice.31.refs_0_
  233.3 88.9 %feed.1 = (bf16[4608,1024]{1,0:T(8,128)(2,1)}, bf16[1024,4608]{1,0:T(8,128)(2,1)}, bf16[1024,1152]{1,0:T(8,128)(2,1)}, bf16[1152,1024]{1,0:T(8,128)(2,1)}, bf16[...) custom-call(bf16[1024,1152]{1,0:T(8,128)(2,1)} %get-tuple-element.12, ...), custom_call_target="tpu_custom_call" | custom-call | flops 21743271936 | bytes 75364864 | tf_op jit(solution)/shard_map/feed/pallas_call | solution.py:418
  322.2 69.8 %align.1 = (bf16[2048,1024]{1,0:T(8,128)(2,1)}, bf16[2048,1024]{1,0:T(8,128)(2,1)}, bf16[1024,768]{1,0:T(8,128)(2,1)}, bf16[1024,2048]{1,0:T(8,128)(2,1)}, bf16[...) custom-call(bf16[1024,1152]{1,0:T(8,128)(2,1)} %get-tuple-element.125.res_ref, ...), custom_call_target="tpu_custom_call" | custom-call | flops 33285996544 | bytes 47991808 | tf_op jit(solution)/shard_map/align/pallas_call | solution.py:418
  392.1 5.6 weight_other.7
  397.7 1.5 collective-permute-start
  399.2 8.4 weight_other.8
  407.6 6.4 weight_other.9
  414.0 1.1 copy-done.4
  415.2 5.6 weight_own.7
  421.4 9.5 %weight_own.8 = bf16[4,4,256,512]{3,2,1,0:T(8,128)(2,1)} custom-call(s32[1]{0:T(128)} %bitcast.14.where_ref, bf16[4,2,256,1024]{3,2,1,0:T(8,128)(2,1)} %bitcast.60, bf16[1024,2048]{1,0:T(8,128)(2,1)} %get-tuple-element.146.right_ref, bf16[4,4,256,512]{3,2,1,0:T(8,128)(2,1)} %collective-permute-done.1.refs_0_), custom_call_target="tpu_custom_call" | custom-call | flops 4294967296 | bytes 16777216 | tf_op jit(solution)/shard_map/weight_own/pallas_call | solution.py:418
  430.9 1.4 copy-done.3
  432.3 6.8 weight_own.9
  440.6 37.3 %feed_back.1 = (bf16[1024,1152]{1,0:T(8,128)(2,1)}, bf16[1024,4608]{1,0:T(8,128)(2,1)}, f32[1024,1152]{1,0:T(8,128)}, f32[16,1152]{1,0:T(8,128)}) custom-call(f32[1024,1152]{1,0:T(8,128)} %get-tuple-element.148.gout_ref, bf16[1024,1152]{1,0:T(8,128)(2,1)} %get-tuple-element.149.branch_ref, bf16[1024,16]{1,0:T(8,128)(2,1)} %fusion.hot_ref, ...), custom_call_target="tpu_custom_call" | custom-call | flops 21743271936 | bytes 54624256 | tf_op jit(solution)/shard_map/feed_back/pallas_call | solution.py:418
  477.9 11.2 %weight_other.10 = (bf16[4,4,144,1152]{3,2,1,0:T(8,128)(2,1)}, f32[16,1152]{1,0:T(8,128)}) custom-call(s32[1]{0:T(128)} %bitcast.14.where_ref, bf16[4,4,2,144,1024]{4,3,2,1,0:T(8,128)(2,1)} %bitcast.55, bf16[1024,1152]{1,0:T(8,128)(2,1)} %get-tuple-element.160.right_ref), custom_call_target="tpu_custom_call" | custom-call | flops 5435817984 | bytes 17178624 | tf_op jit(solution)/shard_map/weight_other/pallas_call | solution.py:418
  489.1 11.3 %weight_other.11 = (bf16[4,4,144,1152]{3,2,1,0:T(8,128)(2,1)}, f32[16,4608]{1,0:T(8,128)}) custom-call(s32[1]{0:T(128)} %bitcast.14.where_ref, bf16[4,2,144,1024]{3,2,1,0:T(8,128)(2,1)} %bitcast.66, bf16[1024,4608]{1,0:T(8,128)(2,1)} %get-tuple-element.167.right_ref), custom_call_target="tpu_custom_call" | custom-call | flops 5435817984 | bytes 17399808 | tf_op jit(solution)/shard_map/weight_other/pallas_call | solution.py:418
  500.4 11.6 %weight_own.10 = bf16[4,4,144,1152]{3,2,1,0:T(8,128)(2,1)} custom-call(s32[1]{0:T(128)} %bitcast.14.where_ref, bf16[4,4,2,144,1024]{4,3,2,1,0:T(8,128)(2,1)} %bitcast.56, bf16[1024,1152]{1,0:T(8,128)(2,1)} %get-tuple-element.160.right_ref, bf16[4,4,144,1152]{3,2,1,0:T(8,128)(2,1)} %collective-permute-done.3.refs_0_), custom_call_target="tpu_custom_call" | custom-call | flops 5435817984 | bytes 22413312 | tf_op jit(solution)/shard_map/weight_own/pallas_call | solution.py:418
  512.5 15.4 %merge_back.1 = (f32[1024,1152]{1,0:T(8,128)}, bf16[1024,1152]{1,0:T(8,128)(2,1)}, bf16[1024,1152]{1,0:T(8,128)(2,1)}, f32[16,1152]{1,0:T(8,128)}, f32[16,1152]{1,0:T(8,128)}, /*index=5*/f32[16,1152]{1,0:T(8,128)}) custom-call(f32[1024,1152]{1,0:T(8,128)} %get-tuple-element.148.gout_ref, f32[1024,1152]{1,0:T(8,128)} %get-tuple-element.161.gmod_ref, ...), custom_call_target="tpu_custom_call" | custom-call | flops 2717908992 | bytes 37298176 | tf_op jit(solution)/shard_map/merge_back/pallas_call | solution.py:418
  527.9 5.1 weight_other.12
  533.0 11.4 %weight_own.11 = bf16[4,4,144,1152]{3,2,1,0:T(8,128)(2,1)} custom-call(s32[1]{0:T(128)} %bitcast.14.where_ref, bf16[4,2,144,1024]{3,2,1,0:T(8,128)(2,1)} %bitcast.67, bf16[1024,4608]{1,0:T(8,128)(2,1)} %get-tuple-element.167.right_ref, bf16[4,4,144,1152]{3,2,1,0:T(8,128)(2,1)} %collective-permute-done.4.refs_0_), custom_call_target="tpu_custom_call" | custom-call | flops 5435817984 | bytes 22413312 | tf_op jit(solution)/shard_map/weight_own/pallas_call | solution.py:418
  544.4 1.2 copy-done.21
  545.8 2.9 collective-permute-done.5.refs_0_
  548.7 1.1 copy-done.5
  549.8 5.1 weight_own.12
  554.9 88.6 %attend_backward.1 = (bf16[1024,3584]{1,0:T(8,128)(2,1)}, bf16[64,768]{1,0:T(8,128)(2,1)}, bf16[144,512]{1,0:T(8,128)(2,1)}, bf16[256,512]{1,0:T(8,128)(2,1)}, bf16[144,1152]{1,0:T(8,128)(2,1)}) custom-call(bf16[1024,3456]{1,0:T(8,128)(2,1)} %get-tuple-element.168.q_ref.k_ref.v_ref, bf16[1024,3456]{1,0:T(8,128)(2,1)} %get-tuple-element.168.q_ref.k_ref.v_ref, ...), custom_call_target="tpu_custom_call" | custom-call | flops 42949672960 | bytes 18874368 | tf_op jit(solution)/shard_map/attend_backward/pallas_call | solution.py:238
  643.5 9.3 %weight_other.13 = (bf16[4,4,144,896]{3,2,1,0:T(8,128)(2,1)}, f32[16,3584]{1,0:T(8,128)}) custom-call(s32[1]{0:T(128)} %bitcast.14.where_ref, bf16[4,2,144,1024]{3,2,1,0:T(8,128)(2,1)} %bitcast.69, bf16[1024,3584]{1,0:T(8,128)(2,1)} %get-tuple-element.184.right_ref.gqkv_ref), custom_call_target="tpu_custom_call" | custom-call | flops 4227858432 | bytes 14057472 | tf_op jit(solution)/shard_map/weight_other/pallas_call | solution.py:418
  653.3 37.3 %project_back.1 = (bf16[1024,1152]{1,0:T(8,128)(2,1)}, f32[16,1152]{1,0:T(8,128)}, f32[16,1152]{1,0:T(8,128)}, bf16[144,1152]{1,0:T(8,128)(2,1)}) custom-call(bf16[1024,3584]{1,0:T(8,128)(2,1)} %get-tuple-element.184.right_ref.gqkv_ref, bf16[1024,1152]{1,0:T(8,128)(2,1)} %bitcast.65, f32[1024,1152]{1,0:T(8,128)} %get-tuple-element.180.gmid_ref, ...), custom_call_target="tpu_custom_call" | custom-call | flops 8153726976 | bytes 29487104 | tf_op jit(solution)/shard_map/project_back/pallas_call | solution.py:418
  690.7 9.9 %weight_own.13 = bf16[4,4,144,896]{3,2,1,0:T(8,128)(2,1)} custom-call(s32[1]{0:T(128)} %bitcast.14.where_ref, bf16[4,2,144,1024]{3,2,1,0:T(8,128)(2,1)} %bitcast.70, bf16[1024,3584]{1,0:T(8,128)(2,1)} %get-tuple-element.184.right_ref.gqkv_ref, bf16[4,4,144,896]{3,2,1,0:T(8,128)(2,1)} %collective-permute-done.6.refs_0_), custom_call_target="tpu_custom_call" | custom-call | flops 4227858432 | bytes 17956864 | tf_op jit(solution)/shard_map/weight_own/pallas_call | solution.py:418
  700.7 1.0 slice_reduce_fusion.2
  703.4 1.0 slice_reduce_fusion
  708.1 83.8 %settle.2 = (bf16[144,1152]{1,0:T(8,128)(2,1)}, bf16[4,2,64,768]{3,2,1,0:T(8,128)(2,1)}, bf16[4,2,256,512]{3,2,1,0:T(8,128)(2,1)}, bf16[4,2,144,512]{3,2,1,0:T(8...) custom-call(bf16[4,144,1152]{2,1,0:T(8,128)(2,1)} %bitcast.75, ...), custom_call_target="tpu_custom_call" | custom-call | bytes 200000000 | tf_op jit(solution)/shard_map/settle/pallas_call | solution.py:1470
  791.9 4.2 convert_element_type.40
  796.1 8.0 unpack.3
  804.1 1.2 bitcast_convert_fusion
  806.0 44.6 %settle.3 = (bf16[144,896]{1,0:T(8,128)(2,1)}, f32[32,128]{1,0:T(8,128)}, bf16[4,2,144,1152]{3,2,1,0:T(8,128)(2,1)}, bf16[4,2,144,896]{3,2,1,0:T(8,128)(2,1)}, f...) custom-call(bf16[4,144,896]{2,1,0:T(8,128)(2,1)} %bitcast.77, f32[4,32,128]{2,1,0:T(8,128)} %bitcast.78, ...), custom_call_target="tpu_custom_call" | custom-call | bytes 200000000 | tf_op jit(solution)/shard_map/settle/pallas_call | solution.py:1470
  854.5 1.0 slice_convert_fusion
  857.0 6.5 unpack.2
  863.5 1.4 copy.47
  (118 shorter events, 19.9 us)
Async XLA Ops:
  7.2 101.7 %copy-start = (bf16[4,4,6912]{2,1,0:T(4,128)(2,1)S(1)}, bf16[4,4,6912]{2,1,0:T(4,128)(2,1)}, u32[]{:S(2)}) copy-start(bf16[4,4,6912]{2,1,0:T(4,128)(2,1)} %param.19) | copy-start | bytes 663556
  7.2 547.7 %reduce-scatter.9.cloned.1.call-start = ((), (), s32[]{:S(2)}) async-start(), calls=%async_computation.7 | async-start | bytes 1966080 | tf_op jit(solution)/shard_map/reduce_scatter | solution.py:1711
  10.6 87.1 %copy-start.13 = (bf16[2304]{0:T(1024)(128)(2,1)S(1)}, bf16[2304]{0:T(1024)(128)(2,1)}, u32[]{:S(2)}) copy-start(bf16[2304]{0:T(1024)(128)(2,1)} %param.22) | copy-start | bytes 13828
  10.7 87.8 %copy-start.18 = (bf16[1152]{0:T(1024)(128)(2,1)S(1)}, bf16[1152]{0:T(1024)(128)(2,1)}, u32[]{:S(2)}) copy-start(bf16[1152]{0:T(1024)(128)(2,1)} %param.24) | copy-start | bytes 6916
  10.7 91.6 %copy-start.15 = (bf16[4608]{0:T(1024)(128)(2,1)S(1)}, bf16[4608]{0:T(1024)(128)(2,1)}, u32[]{:S(2)}) copy-start(bf16[4608]{0:T(1024)(128)(2,1)} %param.26) | copy-start | bytes 27652
  10.7 92.2 %copy-start.19 = (bf16[1152]{0:T(1024)(128)(2,1)S(1)}, bf16[1152]{0:T(1024)(128)(2,1)}, u32[]{:S(2)}) copy-start(bf16[1152]{0:T(1024)(128)(2,1)} %param.28) | copy-start | bytes 6916
  10.7 92.8 %copy-start.16 = (bf16[2048]{0:T(1024)(128)(2,1)S(1)}, bf16[2048]{0:T(1024)(128)(2,1)}, u32[]{:S(2)}) copy-start(bf16[2048]{0:T(1024)(128)(2,1)} %param.32) | copy-start | bytes 12292
  10.7 93.4 %copy-start.17 = (bf16[2048]{0:T(1024)(128)(2,1)S(1)}, bf16[2048]{0:T(1024)(128)(2,1)}, u32[]{:S(2)}) copy-start(bf16[2048]{0:T(1024)(128)(2,1)} %param.30) | copy-start | bytes 12292
  10.7 94.0 %copy-start.20 = (bf16[768]{0:T(1024)(128)(2,1)S(1)}, bf16[768]{0:T(1024)(128)(2,1)}, u32[]{:S(2)}) copy-start(bf16[768]{0:T(1024)(128)(2,1)} %param.34) | copy-start | bytes 4612
  397.7 16.3 %collective-permute-start = (bf16[4,4,64,768]{3,2,1,0:T(8,128)(2,1)}, bf16[4,4,64,768]{3,2,1,0:T(8,128)(2,1)S(1)}, u32[]{:S(2)}, u32[]{:S(2)}) collective-permute-start(bf16[4,4,64,768]{3,2,1,0:T(8,128)(2,1)} %get-tuple-element.140), channel_id=1, source_target_pairs={{0,4},{4,0},{1,5},{5,1},{2,6},{6,2},{3,7},{7,3},{8,12},{12,8},{9,1... | collective-permute-start | bytes 4718600 | tf_op jit(solution)/shard_map/ppermute | solution.py:1699
  407.6 13.8 %collective-permute-start.1 = (bf16[4,4,256,512]{3,2,1,0:T(8,128)(2,1)}, bf16[4,4,256,512]{3,2,1,0:T(8,128)(2,1)}, u32[]{:S(2)}, u32[]{:S(2)}) collective-permute-start(bf16[4,4,256,512]{3,2,1,0:T(8,128)(2,1)} %get-tuple-element.142), channel_id=1, source_target_pairs={{0,4},{4,0},{1,5},{5,1},{2,6},{6,2},{3,7},{7,3},{8,12},{12,8},{9,1... | collective-permute-start | bytes 12582920 | tf_op jit(solution)/shard_map/ppermute | solution.py:1699
  414.0 1.1 copy-start.4
  420.8 134.1 %reduce-scatter.11.cloned.1.call-start = ((), (), s32[]{:S(2)}) async-start(), calls=%async_computation.8 | async-start | bytes 2949120 | tf_op jit(solution)/shard_map/reduce_scatter | solution.py:1711
  420.9 10.1 %collective-permute-start.2 = (bf16[4,4,144,512]{3,2,1,0:T(8,128)(2,1)}, bf16[4,4,144,512]{3,2,1,0:T(8,128)(2,1)S(1)}, u32[]{:S(2)}, u32[]{:S(2)}) collective-permute-start(bf16[4,4,144,512]{3,2,1,0:T(8,128)(2,1)} %get-tuple-element.144), channel_id=1, source_target_pairs={{0,4},{4,0},{1,5},{5,1},{2,6},{6,2},{3,7},{7,3},{8,12},{12,8},{9,1... | collective-permute-start | bytes 7077896 | tf_op jit(solution)/shard_map/ppermute | solution.py:1699
  430.9 1.4 copy-start.3
  439.2 0.8 copy-start.14
  439.2 115.7 %reduce-scatter.13.cloned.1.call-start = ((), (), s32[]{:S(2)}) async-start(), calls=%async_computation.9 | async-start | bytes 5242880 | tf_op jit(solution)/shard_map/reduce_scatter | solution.py:1711
  439.9 213.4 %reduce-scatter.15.cloned.1.call-start = ((), (), s32[]{:S(2)}) async-start(), calls=%async_computation.10 | async-start | bytes 6635520 | tf_op jit(solution)/shard_map/reduce_scatter | solution.py:1711
  489.1 11.3 %collective-permute-start.3 = (bf16[4,4,144,1152]{3,2,1,0:T(8,128)(2,1)}, bf16[4,4,144,1152]{3,2,1,0:T(8,128)(2,1)}, u32[]{:S(2)}, u32[]{:S(2)}) collective-permute-start(bf16[4,4,144,1152]{3,2,1,0:T(8,128)(2,1)} %get-tuple-element.157), channel_id=1, source_target_pairs={{0,4},{4,0},{1,5},{5,1},{2,6},{6,2},{3,7},{7,3},{8,12},{12,8},{9,1... | collective-permute-start | bytes 15925256 | tf_op jit(solution)/shard_map/ppermute | solution.py:1699
  512.1 196.0 %reduce-scatter.7.cloned.1.call-start = ((), (), s32[]{:S(2)}) async-start(), calls=%async_computation.6 | async-start | bytes 6635520 | tf_op jit(solution)/shard_map/reduce_scatter | solution.py:1711
  512.1 20.9 %collective-permute-start.4 = (bf16[4,4,144,1152]{3,2,1,0:T(8,128)(2,1)}, bf16[4,4,144,1152]{3,2,1,0:T(8,128)(2,1)}, u32[]{:S(2)}, u32[]{:S(2)}) collective-permute-start(bf16[4,4,144,1152]{3,2,1,0:T(8,128)(2,1)} %get-tuple-element.159), channel_id=1, source_target_pairs={{0,4},{4,0},{1,5},{5,1},{2,6},{6,2},{3,7},{7,3},{8,12},{12,8},{9,1... | collective-permute-start | bytes 15925256 | tf_op jit(solution)/shard_map/ppermute | solution.py:1699
  544.4 1.3 copy-start.21
  544.4 260.9 %reduce-scatter.17.cloned.1.call-start = ((), (), s32[]{:S(2)}) async-start(), calls=%async_computation.11 | async-start | bytes 5160960 | tf_op jit(solution)/shard_map/reduce_scatter | solution.py:1711
  545.7 3.1 collective-permute-start.5
  548.7 1.1 copy-start.5
  652.8 37.9 %collective-permute-start.6 = (bf16[4,4,144,896]{3,2,1,0:T(8,128)(2,1)}, bf16[4,4,144,896]{3,2,1,0:T(8,128)(2,1)}, u32[]{:S(2)}, u32[]{:S(2)}) collective-permute-start(bf16[4,4,144,896]{3,2,1,0:T(8,128)(2,1)} %get-tuple-element.178), channel_id=1, source_target_pairs={{0,4},{4,0},{1,5},{5,1},{2,6},{6,2},{3,7},{7,3},{8,12},{12,8},{9,1... | collective-permute-start | bytes 12386312 | tf_op jit(solution)/shard_map/ppermute | solution.py:1699
  700.6 7.3 copy-start.12
  700.6 7.3 copy-start.11
  700.6 7.3 copy-start.10
  700.6 7.3 copy-start.9
  700.6 7.3 copy-start.8
  700.6 7.3 copy-start.7
  796.1 8.0 copy-start.6
  857.0 6.5 copy-start.2
  863.5 1.4 copy-start.1
Sparse Core Ops, SparseCore 0:
  420.9 28.9 reduce-scatter.8
  453.0 37.3 reduce-scatter.10
  493.9 52.6 reduce-scatter.12
  550.4 61.9 reduce-scatter.14
  616.1 61.9 reduce-scatter.6
  700.8 93.7 reduce-scatter.16

commit v4 on v3

--- a/solution.py
+++ b/solution.py
@@ -57,8 +57,9 @@
     )
 
 
-GATHER_AT = (1, 1, 2, 3, 3, 4, 5, 6, 7, 8, 9, 10, 11, 12, 13, 14, 15, 15, 15)
-FEED_AT = (1, 1, 1, 1, 2, 2, 2, 3, 3, 3, 4, 4, 4, 5, 5, 5, 6, 6, 6, 7, 7, 7, 7, 7, 7, 7, 7, 7)
+GATHER_AT = (7, 7, 7, 16, 17, 17, 11, 11, 11, 18, 18, 18, 14, 14, 14, 18, 18, 18)
+SECOND_AT, THIRD_AT = 6, 15
+FEED_AT = (1, 1, 4, 5, 5, 8, 7, 7, 8, 3, 3, 6, 7, 7, 8, 8, 8, 8, 5, 5, 7, 8, 8, 8, 8, 8, 8)
 SETTLE_AT = (4, 7, 12, 15)
 
 
@@ -440,7 +441,7 @@
 def carry(refs, bundles):
     refs = list(refs)
     take = lambda count: [refs.pop(0) for _ in range(count)]
-    return take, (take(len(bundles)), [take(count) for count in bundles])
+    return take, [take(count) for count in bundles]
 
 
 def project_kernel(
@@ -452,23 +453,32 @@
     targets = take(len(bundles))
     (goal_out,) = take(1)
     (low_ref,) = take(1)
-    gather = Gather(*given, targets, take(Gather.room(len(bundles))))
+    gather = Gather(given, targets, take(Gather.room(len(bundles))))
     tokens = Rounds([goal_in], [goal_out], take(2))
     head = pl.program_id(0)
     width = x_ref.shape[1]
+    steps = gather.steps()
+
+    def point(number):
+        if number == SECOND_AT:
+            gather.issue(1)
+        if number == THIRD_AT:
+            tokens.start()
+        for step, when in zip(steps, GATHER_AT):
+            if when == number:
+                step()
 
     @pl.when(head == 0)
     def _():
         gather.link.greet()
         gather.start()
-        gather.start_local()
-        tokens.start()
         for rows in chunks(x_ref.shape[0]):
             normed, _ = norm_stats(x_ref[rows, :].astype(F32))
             hot = hot_ref[rows, :]
             low = normed * (1.0 + dot_nn(hot, scale_ref[...])) + dot_nn(hot, shift_ref[...])
             low_ref[rows, :] = low.astype(BF)
             modt_ref[:, rows] = low.astype(BF).T
+        point(0)
         for j in range(3):
             columns = pl.ds(j * width, width)
             weight = square(w_ref[:, j])
@@ -476,9 +486,11 @@
                 qkv_ref[rows, columns] = (
                     dot_nn(low_ref[rows, :], weight) + bias_ref[:, columns]
                 ).astype(BF)
-
-    for index, step in enumerate(gather.steps()):
-        pl.when(head == GATHER_AT[index])(step)
+            point(j + 1)
+
+    for number in range(4, max(GATHER_AT) + 1):
+        if number in GATHER_AT + (SECOND_AT, THIRD_AT):
+            pl.when(head == number - 3)(functools.partial(point, number))
     parts = ((qkv_ref, 0), (qkv_ref, width), (qkv_ref, 2 * width))
     attend_head(head, parts, (seg_ref, seg_ref), out_ref, total_ref, block)
 
@@ -488,11 +500,11 @@
         tokens.finish()
 
 
-def project(x, hot, mod, weights, bias, seg, heads, slices, shards, goals, collective):
+def project(x, hot, mod, weights, bias, seg, heads, cuts, shards, goals, collective):
     tokens, width = x.shape
     seq, _, per, _ = weights.shape
     part = lambda index: spec((mod.shape[0], width), lambda h: (0, index), once=True)
-    flat = list(slices) + [array for shard in shards for array in shard]
+    flat = [array for shard in shards for array in shard]
     return call(
         functools.partial(
             project_kernel, block=min(256, tokens), bundles=[len(shard) for shard in shards]
@@ -514,13 +526,13 @@
             ((tokens, width), BF, fixed((tokens, width))),
             ((heads, tokens), F32, fixed((heads, tokens))),
         ]
-        + [(shape.shape, BF, ANY) for shape in gathered(slices, shards)]
+        + [(shape.shape, BF, ANY) for shape in gathered(cuts, shards)]
         + [(goals.shape, BF, ANY)],
         [x, hot, mod, mod, weights, bias, seg] + flat + [goals],
         "project",
         6 * tokens * width * width + heads * tokens * tokens * 4 * 256,
         [pltpu.VMEM((tokens, width), BF)]
-        + Gather.scratch(gathered(slices, shards))
+        + Gather.scratch(gathered(cuts, shards))
         + Rounds.scratch(1),
         collective=collective,
     )
@@ -594,15 +606,15 @@
     actt_ref, slope_ref, res_ref, rest_ref, branch_ref = take(5)
     targets = take(len(bundles))
     (total,) = take(1)
-    gather = Gather(*given, targets, take(Gather.room(len(bundles))))
+    gather = Gather(given, targets, take(Gather.room(len(bundles))), eager=True)
     steps = gather.steps()
+    blocks = targets[0].shape[1]
     step = pl.program_id(0)
 
     @pl.when(step == 0)
     def _():
         gather.link.greet()
         gather.start()
-        gather.start_local()
         total[...] = jnp.zeros_like(total)
 
     w_in, w_out = square(w_in_ref[...]), w_out_ref[...]
@@ -628,14 +640,17 @@
             res_ref[rows, :] = result
             rest_ref[:, rows] = result.T
             branch_ref[rows, :] = branch.astype(BF)
+        for index, action in enumerate(steps):
+            if FEED_AT[index] == 2 * blocks:
+                action()
         gather.finish()
 
 
-def feed(low, w_in, b_in, w_out, b_out, mid, hot, mod, slices, shards, collective):
+def feed(low, w_in, b_in, w_out, b_out, mid, hot, mod, cuts, shards, collective):
     tokens, width = low.shape
     seq, blocks, per, cut = w_in.shape
     hidden = blocks * cut
-    flat = list(slices) + [array for shard in shards for array in shard]
+    flat = [array for shard in shards for array in shard]
     return call(
         functools.partial(feed_kernel, bundles=[len(shard) for shard in shards]),
         (blocks,),
@@ -657,11 +672,11 @@
             ((width, tokens), BF, fixed((width, tokens))),
             ((tokens, width), BF, fixed((tokens, width))),
         ]
-        + [(shape.shape, BF, ANY) for shape in gathered(slices, shards)],
+        + [(shape.shape, BF, ANY) for shape in gathered(cuts, shards)],
         [low, w_in, b_in, w_out, b_out, mid, hot, mod] + flat,
         "feed",
         4 * tokens * width * hidden,
-        [pltpu.VMEM((tokens, width), F32)] + Gather.scratch(gathered(slices, shards)),
+        [pltpu.VMEM((tokens, width), F32)] + Gather.scratch(gathered(cuts, shards)),
         collective=collective,
     )
 
@@ -1032,9 +1047,10 @@
 
 
 class Gather:
-    def __init__(self, slices, shards, targets, sems):
+    def __init__(self, shards, targets, sems, eager=False, after=None):
         self.link = Link()
-        self.slices, self.shards, self.targets = slices, shards, targets
+        self.shards, self.targets = shards, targets
+        self.eager, self.after = eager, after
         self.z_sems, self.p_sems, self.c_sems, self.local_sems, self.out_sems = sems[:5]
         self.bufs = sems[5:]
 
@@ -1058,40 +1074,33 @@
         half = target.shape[2] // 2
         return pl.ds(pl.multiple_of(self.link.c * half, half), half)
 
-    def locals(self):
-        for k, (shard, target) in enumerate(zip(self.shards, self.targets)):
-            width = target.shape[3]
-            block = 0
-            for array in shard:
-                if len(array.shape) == 3:
-                    parts = [array.at[index] for index in range(array.shape[0])]
-                else:
-                    parts = [
-                        array.at[:, pl.ds(start, width)]
-                        for start in range(0, array.shape[1], width)
-                    ]
-                for part in parts:
-                    yield pltpu.make_async_copy(
-                        part, self.bufs[k].at[block], self.local_sems.at[k, block]
-                    )
-                    block += 1
+    def locals(self, k):
+        target = self.targets[k]
+        width = target.shape[3]
+        block = 0
+        for array in self.shards[k]:
+            if len(array.shape) == 3:
+                parts = [array.at[index] for index in range(array.shape[0])]
+            else:
+                parts = [
+                    array.at[:, pl.ds(start, width)] for start in range(0, array.shape[1], width)
+                ]
+            for part in parts:
+                yield pltpu.make_async_copy(
+                    part, self.bufs[k].at[block], self.local_sems.at[k, block]
+                )
+                block += 1
 
     def stored(self, k):
         return pltpu.make_async_copy(
             self.bufs[k], self.targets[k].at[self.link.z], self.out_sems.at[k]
         )
 
-    def store(self):
-        for copy in self.locals():
-            copy.wait()
-        for k in range(len(self.targets)):
-            self.stored(k).start()
-
     def along(self, k, shift, incoming):
         link, target = self.link, self.targets[k]
         place = link.behind(shift) if incoming else link.z
         return link.copy(
-            self.slices[k],
+            self.bufs[k].at[link.p, self.rows(target), :],
             target.at[place, link.p, self.rows(target), :],
             (self.z_sems.at[0, k, shift - 1], self.z_sems.at[1, k, shift - 1]),
             "seq",
@@ -1134,24 +1143,38 @@
         )
 
     def start(self):
-        for k in range(len(self.targets)):
-            for shift in (1, 3, 2):
+        count = range(len(self.targets))
+        for k in count:
+            for copy in self.locals(k):
+                copy.start()
+        for k in count:
+            for copy in self.locals(k):
+                copy.wait()
+            if k == 0:
+                self.issue(0)
+            self.stored(k).start()
+
+    def issue(self, k):
+        if k < len(self.targets):
+            for shift in (1, 3) if self.eager else (1, 3, 2):
                 self.along(k, shift, False).start()
 
-    def start_local(self):
-        for copy in self.locals():
-            copy.start()
-
     def steps(self):
-        return [self.store] + [
+        return [
             functools.partial(stage, k, shift)
+            for stage in (self.spread, self.relay, self.pair)
             for k in range(len(self.targets))
-            for stage in (self.spread, self.relay, self.pair)
             for shift in (1, 3, 2)
         ]
 
     def spread(self, k, shift):
         self.along(k, shift, True).wait_recv()
+        if self.eager and shift == 1:
+            self.along(k, 2, False).start()
+        if self.eager and shift == 3:
+            self.issue(k + 1)
+        if shift == 1 and self.after is not None:
+            self.after()
         for index in (0, 3, 1, 2):
             self.across(k, shift, index, False).start()
 
@@ -1367,27 +1390,24 @@
 def bring_kernel(*refs, bundles, rounds):
     refs = list(refs)
     take = lambda count: [refs.pop(0) for _ in range(count)]
-    slices = take(len(bundles))
     shards = [take(count) for count in bundles]
     sources = take(rounds)
     targets = take(len(bundles))
     arrived = take(rounds)
-    gather = Gather(slices, shards, targets, take(Gather.room(len(bundles))))
+    gather_refs = take(Gather.room(len(bundles)))
     tokens = Rounds(sources, arrived, take(2))
+    gather = Gather(shards, targets, gather_refs, after=tokens.start)
     gather.link.greet()
     gather.start()
-    tokens.start()
-    gather.start_local()
     for step in gather.steps():
         step()
     tokens.finish()
     gather.finish()
 
 
-def gathered(slices, shards):
+def gathered(cuts, shards):
     shapes = []
-    for piece, shard in zip(slices, shards):
-        cut = piece.shape[1]
+    for cut, shard in zip(cuts, shards):
         if shard[0].ndim == 3:
             blocks, per = shard[0].shape[:2]
         else:
@@ -1396,10 +1416,10 @@
     return shapes
 
 
-def bring(slices, shards, sources, collective):
+def bring(cuts, shards, sources, collective):
     flat = [array for shard in shards for array in shard]
-    shapes = gathered(slices, shards) + [jax.ShapeDtypeStruct(array.shape, array.dtype) for array in sources]
-    args = list(slices) + flat + list(sources)
+    shapes = gathered(cuts, shards) + [jax.ShapeDtypeStruct(array.shape, array.dtype) for array in sources]
+    args = flat + list(sources)
     return pl.pallas_call(
         functools.partial(
             bring_kernel, bundles=[len(shard) for shard in shards], rounds=len(sources)
@@ -1407,7 +1427,7 @@
         in_specs=[ANY] * len(args),
         out_specs=[ANY] * len(shapes),
         out_shape=shapes,
-        scratch_shapes=Gather.scratch(gathered(slices, shards)) + Rounds.scratch(len(sources)),
+        scratch_shapes=Gather.scratch(gathered(cuts, shards)) + Rounds.scratch(len(sources)),
         compiler_params=pltpu.CompilerParams(
             collective_id=collective, has_side_effects=True, vmem_limit_bytes=60 * MIB
         ),
@@ -1767,14 +1787,8 @@
     tokens = rows * span
     where = lax.axis_index("core").reshape(1).astype(jnp.int32)
 
-    slice1, _ = own_slice([qkv_weight, attn_out_weight], width)
-    slice2, _ = own_slice([mlp_in_weight], width)
-    slice3, _ = own_slice([mlp_out_weight], width)
-    slice4, _ = own_slice([proj_in_weight], inner // planes)
-    slice5, _ = own_slice([proj_mid_weight], inner)
-    slice6, _ = own_slice([proj_out_weight], goal_width)
     w1, x, seg_own = bring(
-        [slice1],
+        [width],
         [[qkv_weight, attn_out_weight]],
         [block_input, segment_ids.reshape(rows, -1, LANES)],
         0,
@@ -1796,7 +1810,7 @@
     by_rows = lambda weight: weight.reshape(planes, -1, weight.shape[1])
     qkv, mod1t, attended, totals, w2, w3, goals = project(
         x, hot, mod, w1, full_bias[None, :], seg_column, heads,
-        [slice2, slice3], [[mlp_in_weight], [by_rows(mlp_out_weight)]], targets, 3,
+        [width, width], [[mlp_in_weight], [by_rows(mlp_out_weight)]], targets, 3,
     )
     goals = goals.reshape(tokens, goal_width)
     parts = ((qkv, 0), (qkv, 1), (qkv, 2))
@@ -1804,7 +1818,7 @@
     w3 = w3.reshape(hidden, width)
     actt, slope, out_low, outt, mlp_branch, w4, w5, w6 = feed(
         low2, w2, vector(mlp_in_bias), w3, vector(mlp_out_bias), mid, hot, mod,
-        [slice4, slice5, slice6],
+        [inner // planes, inner, goal_width],
         [[proj_in_weight], [by_rows(proj_mid_weight)], [by_rows(proj_out_weight)]],
         5,
     )

time: 885 us -> 871 us (0.984)
  no operation moved by 1% of the time
where the time goes in v4:
time: 871 us; the launch traced here: 858 us
  Pallas kernels  801 us (92%)
  local copies, waits for them, and re-layouts  25.1 us (3%)
  between operations  14.9 us (2%)
  other arithmetic  11.3 us (1%)
    pallas_call x23, Pallas kernels, call(): pl.pallas_call(kernel, grid_spec=grid_spec, out_shape=[jax.ShapeDtypeStru...  499 us
    pallas_call x2, Pallas kernels, settle(): pl.pallas_call(functools.partial(settle_kernel, sums=len(sums), shares=le...  128 us
    pallas_call x1, Pallas kernels, attend_backward(): pl.pallas_call(functools.partial(attend_backward_kernel, block=min(256, c...  87.9 us
    pallas_call x1, Pallas kernels, bring(): pl.pallas_call(functools.partial(bring_kernel, bundles=[len(shard) for sh...  85.2 us
  transfers between devices with their start and end apart: 13, of which 1 were waited for; matrix products, arithmetic and copies ran while one was open for 2% of the time, Pallas kernels for 44%

profile of v4, /device:TPU:9, one launch (start us, length us, event | category | flops | bytes accessed | tf_op | source)
XLA Modules:
  0.0 858.2 jit_solution(7817825203242022305)
XLA Ops:
  7.3 1.3 reshape.167.refs_3_
  8.6 85.2 %bring.1 = (bf16[4,4,288,1152]{3,2,1,0:T(8,128)(2,1)}, bf16[4,256,1152]{2,1,0:T(8,128)(2,1)}, s32[4,2,128]{2,1,0:T(2,128)}) custom-call(bf16[288,3456]{1,0:T(8,128)(2,1)} %refs_0_.3, bf16[288,1152]{1,0:T(8,128)(2,1)} %refs_1_.1, bf16[4,256,1152]{2,1,0:T(8,128)(2,1)} %refs_2_.2, s32[4,2,128]{2,1,0:T(2,128)} %reshape.167.refs_3_), custom_call_target="tpu_custom_call" | custom-call | bytes 300000000 | tf_op jit(solution)/shard_map/bring/pallas_call | solution.py:1423
  93.8 1.6 fusion.hot_ref
  95.4 1.7 copy.35.seg_ref.segq_ref.segk_ref
  102.1 117.3 %project.1 = (bf16[1024,3456]{1,0:T(8,128)(2,1)}, bf16[1152,1024]{1,0:T(8,128)(2,1)}, bf16[1024,1152]{1,0:T(8,128)(2,1)}, f32[16,1024]{1,0:T(8,128)}, bf16[4,4,2...) custom-call(bf16[1024,1152]{1,0:T(8,128)(2,1)} %bitcast.63, ...), custom_call_target="tpu_custom_call" | custom-call | flops 25333596160 | bytes 55019008 | tf_op jit(solution)/shard_map/project/pallas_call | solution.py:419
  219.5 10.8 %merge.1 = (bf16[1024,1152]{1,0:T(8,128)(2,1)}, f32[1024,1152]{1,0:T(8,128)}, bf16[1024,1152]{1,0:T(8,128)(2,1)}, bf16[1152,1024]{1,0:T(8,128)(2,1)}, bf16[1152,1024]{1,0:T(8,128)(2,1)}) custom-call(bf16[1024,1152]{1,0:T(8,128)(2,1)} %get-tuple-element.120.out_ref, bf16[1024,1152]{1,0:T(8,128)(2,1)} %bitcast.64, bf16[1024,16]{1,0:T(8,128)(2,1)} %fusion.hot_ref, ...), custom_call_target="tpu_custom_call" | custom-call | flops 2717908992 | bytes 30192128 | tf_op jit(solution)/shard_map/merge/pallas_call | solution.py:419
  230.2 84.8 %feed.1 = (bf16[4608,1024]{1,0:T(8,128)(2,1)}, bf16[1024,4608]{1,0:T(8,128)(2,1)}, bf16[1024,1152]{1,0:T(8,128)(2,1)}, bf16[1152,1024]{1,0:T(8,128)(2,1)}, bf16[...) custom-call(bf16[1024,1152]{1,0:T(8,128)(2,1)} %get-tuple-element.12, ...), custom_call_target="tpu_custom_call" | custom-call | flops 21743271936 | bytes 74856960 | tf_op jit(solution)/shard_map/feed/pallas_call | solution.py:419
  315.0 63.9 %align.1 = (bf16[2048,1024]{1,0:T(8,128)(2,1)}, bf16[2048,1024]{1,0:T(8,128)(2,1)}, bf16[1024,768]{1,0:T(8,128)(2,1)}, bf16[1024,2048]{1,0:T(8,128)(2,1)}, bf16[...) custom-call(bf16[1024,1152]{1,0:T(8,128)(2,1)} %get-tuple-element.125.res_ref, ...), custom_call_target="tpu_custom_call" | custom-call | flops 33285996544 | bytes 47991808 | tf_op jit(solution)/shard_map/align/pallas_call | solution.py:419
  379.0 5.6 weight_other.7
  385.1 8.4 weight_other.8
  393.5 6.4 weight_other.9
  399.9 1.1 copy-done.4
  401.1 5.6 weight_own.7
  407.3 9.5 %weight_own.8 = bf16[4,4,256,512]{3,2,1,0:T(8,128)(2,1)} custom-call(s32[1]{0:T(128)} %bitcast.14.where_ref, bf16[4,2,256,1024]{3,2,1,0:T(8,128)(2,1)} %bitcast.60, bf16[1024,2048]{1,0:T(8,128)(2,1)} %get-tuple-element.146.right_ref, bf16[4,4,256,512]{3,2,1,0:T(8,128)(2,1)} %collective-permute-done.1.refs_0_), custom_call_target="tpu_custom_call" | custom-call | flops 4294967296 | bytes 16777216 | tf_op jit(solution)/shard_map/weight_own/pallas_call | solution.py:419
  416.8 1.4 copy-done.3
  418.2 6.8 weight_own.9
  426.5 37.3 %feed_back.1 = (bf16[1024,1152]{1,0:T(8,128)(2,1)}, bf16[1024,4608]{1,0:T(8,128)(2,1)}, f32[1024,1152]{1,0:T(8,128)}, f32[16,1152]{1,0:T(8,128)}) custom-call(f32[1024,1152]{1,0:T(8,128)} %get-tuple-element.148.gout_ref, bf16[1024,1152]{1,0:T(8,128)(2,1)} %get-tuple-element.149.branch_ref, bf16[1024,16]{1,0:T(8,128)(2,1)} %fusion.hot_ref, ...), custom_call_target="tpu_custom_call" | custom-call | flops 21743271936 | bytes 54624256 | tf_op jit(solution)/shard_map/feed_back/pallas_call | solution.py:419
  463.7 11.2 %weight_other.10 = (bf16[4,4,144,1152]{3,2,1,0:T(8,128)(2,1)}, f32[16,1152]{1,0:T(8,128)}) custom-call(s32[1]{0:T(128)} %bitcast.14.where_ref, bf16[4,4,2,144,1024]{4,3,2,1,0:T(8,128)(2,1)} %bitcast.55, bf16[1024,1152]{1,0:T(8,128)(2,1)} %get-tuple-element.160.right_ref), custom_call_target="tpu_custom_call" | custom-call | flops 5435817984 | bytes 17178624 | tf_op jit(solution)/shard_map/weight_other/pallas_call | solution.py:419
  475.0 11.3 %weight_other.11 = (bf16[4,4,144,1152]{3,2,1,0:T(8,128)(2,1)}, f32[16,4608]{1,0:T(8,128)}) custom-call(s32[1]{0:T(128)} %bitcast.14.where_ref, bf16[4,2,144,1024]{3,2,1,0:T(8,128)(2,1)} %bitcast.66, bf16[1024,4608]{1,0:T(8,128)(2,1)} %get-tuple-element.167.right_ref), custom_call_target="tpu_custom_call" | custom-call | flops 5435817984 | bytes 17399808 | tf_op jit(solution)/shard_map/weight_other/pallas_call | solution.py:419
  486.4 11.6 %weight_own.10 = bf16[4,4,144,1152]{3,2,1,0:T(8,128)(2,1)} custom-call(s32[1]{0:T(128)} %bitcast.14.where_ref, bf16[4,4,2,144,1024]{4,3,2,1,0:T(8,128)(2,1)} %bitcast.56, bf16[1024,1152]{1,0:T(8,128)(2,1)} %get-tuple-element.160.right_ref, bf16[4,4,144,1152]{3,2,1,0:T(8,128)(2,1)} %collective-permute-done.3.refs_0_), custom_call_target="tpu_custom_call" | custom-call | flops 5435817984 | bytes 22413312 | tf_op jit(solution)/shard_map/weight_own/pallas_call | solution.py:419
  498.4 15.4 %merge_back.1 = (f32[1024,1152]{1,0:T(8,128)}, bf16[1024,1152]{1,0:T(8,128)(2,1)}, bf16[1024,1152]{1,0:T(8,128)(2,1)}, f32[16,1152]{1,0:T(8,128)}, f32[16,1152]{1,0:T(8,128)}, /*index=5*/f32[16,1152]{1,0:T(8,128)}) custom-call(f32[1024,1152]{1,0:T(8,128)} %get-tuple-element.148.gout_ref, f32[1024,1152]{1,0:T(8,128)} %get-tuple-element.161.gmod_ref, ...), custom_call_target="tpu_custom_call" | custom-call | flops 2717908992 | bytes 37298176 | tf_op jit(solution)/shard_map/merge_back/pallas_call | solution.py:419
  513.8 5.1 weight_other.12
  518.9 11.4 %weight_own.11 = bf16[4,4,144,1152]{3,2,1,0:T(8,128)(2,1)} custom-call(s32[1]{0:T(128)} %bitcast.14.where_ref, bf16[4,2,144,1024]{3,2,1,0:T(8,128)(2,1)} %bitcast.67, bf16[1024,4608]{1,0:T(8,128)(2,1)} %get-tuple-element.167.right_ref, bf16[4,4,144,1152]{3,2,1,0:T(8,128)(2,1)} %collective-permute-done.4.refs_0_), custom_call_target="tpu_custom_call" | custom-call | flops 5435817984 | bytes 22413312 | tf_op jit(solution)/shard_map/weight_own/pallas_call | solution.py:419
  530.3 1.2 copy-done.21
  531.8 2.8 collective-permute-done.5.refs_0_
  534.7 1.1 copy-done.5
  535.7 5.1 weight_own.12
  540.9 87.9 %attend_backward.1 = (bf16[1024,3584]{1,0:T(8,128)(2,1)}, bf16[64,768]{1,0:T(8,128)(2,1)}, bf16[144,512]{1,0:T(8,128)(2,1)}, bf16[256,512]{1,0:T(8,128)(2,1)}, bf16[144,1152]{1,0:T(8,128)(2,1)}) custom-call(bf16[1024,3456]{1,0:T(8,128)(2,1)} %get-tuple-element.168.q_ref.k_ref.v_ref, bf16[1024,3456]{1,0:T(8,128)(2,1)} %get-tuple-element.168.q_ref.k_ref.v_ref, ...), custom_call_target="tpu_custom_call" | custom-call | flops 42949672960 | bytes 18874368 | tf_op jit(solution)/shard_map/attend_backward/pallas_call | solution.py:239
  628.8 9.4 %weight_other.13 = (bf16[4,4,144,896]{3,2,1,0:T(8,128)(2,1)}, f32[16,3584]{1,0:T(8,128)}) custom-call(s32[1]{0:T(128)} %bitcast.14.where_ref, bf16[4,2,144,1024]{3,2,1,0:T(8,128)(2,1)} %bitcast.69, bf16[1024,3584]{1,0:T(8,128)(2,1)} %get-tuple-element.184.right_ref.gqkv_ref), custom_call_target="tpu_custom_call" | custom-call | flops 4227858432 | bytes 14057472 | tf_op jit(solution)/shard_map/weight_other/pallas_call | solution.py:419
  638.9 37.8 %project_back.1 = (bf16[1024,1152]{1,0:T(8,128)(2,1)}, f32[16,1152]{1,0:T(8,128)}, f32[16,1152]{1,0:T(8,128)}, bf16[144,1152]{1,0:T(8,128)(2,1)}) custom-call(bf16[1024,3584]{1,0:T(8,128)(2,1)} %get-tuple-element.184.right_ref.gqkv_ref, bf16[1024,1152]{1,0:T(8,128)(2,1)} %bitcast.65, f32[1024,1152]{1,0:T(8,128)} %get-tuple-element.180.gmid_ref, ...), custom_call_target="tpu_custom_call" | custom-call | flops 8153726976 | bytes 29487104 | tf_op jit(solution)/shard_map/project_back/pallas_call | solution.py:419
  676.7 9.9 %weight_own.13 = bf16[4,4,144,896]{3,2,1,0:T(8,128)(2,1)} custom-call(s32[1]{0:T(128)} %bitcast.14.where_ref, bf16[4,2,144,1024]{3,2,1,0:T(8,128)(2,1)} %bitcast.70, bf16[1024,3584]{1,0:T(8,128)(2,1)} %get-tuple-element.184.right_ref.gqkv_ref, bf16[4,4,144,896]{3,2,1,0:T(8,128)(2,1)} %collective-permute-done.6.refs_0_), custom_call_target="tpu_custom_call" | custom-call | flops 4227858432 | bytes 17956864 | tf_op jit(solution)/shard_map/weight_own/pallas_call | solution.py:419
  686.7 1.0 slice_reduce_fusion.2
  687.7 0.9 slice_reduce_fusion.1
  688.5 0.8 slice_reduce_fusion.7
  689.4 1.0 slice_reduce_fusion
  690.3 0.8 slice_reduce_fusion.3
  691.2 0.8 slice_reduce_fusion.4
  692.1 0.8 slice_reduce_fusion.6
  694.1 82.9 %settle.2 = (bf16[144,1152]{1,0:T(8,128)(2,1)}, bf16[4,2,64,768]{3,2,1,0:T(8,128)(2,1)}, bf16[4,2,256,512]{3,2,1,0:T(8,128)(2,1)}, bf16[4,2,144,512]{3,2,1,0:T(8...) custom-call(bf16[4,144,1152]{2,1,0:T(8,128)(2,1)} %bitcast.75, ...), custom_call_target="tpu_custom_call" | custom-call | bytes 200000000 | tf_op jit(solution)/shard_map/settle/pallas_call | solution.py:1490
  777.1 4.2 convert_element_type.40
  781.2 8.0 unpack.3
  789.3 1.2 bitcast_convert_fusion
  791.2 45.5 %settle.3 = (bf16[144,896]{1,0:T(8,128)(2,1)}, f32[32,128]{1,0:T(8,128)}, bf16[4,2,144,1152]{3,2,1,0:T(8,128)(2,1)}, bf16[4,2,144,896]{3,2,1,0:T(8,128)(2,1)}, f...) custom-call(bf16[4,144,896]{2,1,0:T(8,128)(2,1)} %bitcast.77, f32[4,32,128]{2,1,0:T(8,128)} %bitcast.78, ...), custom_call_target="tpu_custom_call" | custom-call | bytes 200000000 | tf_op jit(solution)/shard_map/settle/pallas_call | solution.py:1490
  836.7 0.7 fusion.4
  840.6 1.0 slice_convert_fusion
  841.6 0.9 reshape.206
  843.1 6.5 unpack.2
  849.6 1.4 copy.47
  (112 shorter events, 15.0 us)
Async XLA Ops:
  7.2 94.2 %copy-start = (bf16[4,4,6912]{2,1,0:T(4,128)(2,1)S(1)}, bf16[4,4,6912]{2,1,0:T(4,128)(2,1)}, u32[]{:S(2)}) copy-start(bf16[4,4,6912]{2,1,0:T(4,128)(2,1)} %param.19) | copy-start | bytes 663556
  7.2 533.7 %reduce-scatter.9.cloned.1.call-start = ((), (), s32[]{:S(2)}) async-start(), calls=%async_computation.7 | async-start | bytes 1966080 | tf_op jit(solution)/shard_map/reduce_scatter | solution.py:1731
  8.6 88.5 %copy-start.13 = (bf16[2304]{0:T(1024)(128)(2,1)S(1)}, bf16[2304]{0:T(1024)(128)(2,1)}, u32[]{:S(2)}) copy-start(bf16[2304]{0:T(1024)(128)(2,1)} %param.22) | copy-start | bytes 13828
  8.6 89.2 %copy-start.18 = (bf16[1152]{0:T(1024)(128)(2,1)S(1)}, bf16[1152]{0:T(1024)(128)(2,1)}, u32[]{:S(2)}) copy-start(bf16[1152]{0:T(1024)(128)(2,1)} %param.24) | copy-start | bytes 6916
  8.6 89.8 %copy-start.15 = (bf16[4608]{0:T(1024)(128)(2,1)S(1)}, bf16[4608]{0:T(1024)(128)(2,1)}, u32[]{:S(2)}) copy-start(bf16[4608]{0:T(1024)(128)(2,1)} %param.26) | copy-start | bytes 27652
  8.6 90.4 %copy-start.19 = (bf16[1152]{0:T(1024)(128)(2,1)S(1)}, bf16[1152]{0:T(1024)(128)(2,1)}, u32[]{:S(2)}) copy-start(bf16[1152]{0:T(1024)(128)(2,1)} %param.28) | copy-start | bytes 6916
  8.6 91.0 %copy-start.16 = (bf16[2048]{0:T(1024)(128)(2,1)S(1)}, bf16[2048]{0:T(1024)(128)(2,1)}, u32[]{:S(2)}) copy-start(bf16[2048]{0:T(1024)(128)(2,1)} %param.32) | copy-start | bytes 12292
  8.6 91.6 %copy-start.17 = (bf16[2048]{0:T(1024)(128)(2,1)S(1)}, bf16[2048]{0:T(1024)(128)(2,1)}, u32[]{:S(2)}) copy-start(bf16[2048]{0:T(1024)(128)(2,1)} %param.30) | copy-start | bytes 12292
  8.6 92.2 %copy-start.20 = (bf16[768]{0:T(1024)(128)(2,1)S(1)}, bf16[768]{0:T(1024)(128)(2,1)}, u32[]{:S(2)}) copy-start(bf16[768]{0:T(1024)(128)(2,1)} %param.34) | copy-start | bytes 4612
  384.6 15.3 %collective-permute-start = (bf16[4,4,64,768]{3,2,1,0:T(8,128)(2,1)}, bf16[4,4,64,768]{3,2,1,0:T(8,128)(2,1)S(1)}, u32[]{:S(2)}, u32[]{:S(2)}) collective-permute-start(bf16[4,4,64,768]{3,2,1,0:T(8,128)(2,1)} %get-tuple-element.140), channel_id=1, source_target_pairs={{0,4},{4,0},{1,5},{5,1},{2,6},{6,2},{3,7},{7,3},{8,12},{12,8},{9,1... | collective-permute-start | bytes 4718600 | tf_op jit(solution)/shard_map/ppermute | solution.py:1719
  393.5 13.8 %collective-permute-start.1 = (bf16[4,4,256,512]{3,2,1,0:T(8,128)(2,1)}, bf16[4,4,256,512]{3,2,1,0:T(8,128)(2,1)}, u32[]{:S(2)}, u32[]{:S(2)}) collective-permute-start(bf16[4,4,256,512]{3,2,1,0:T(8,128)(2,1)} %get-tuple-element.142), channel_id=1, source_target_pairs={{0,4},{4,0},{1,5},{5,1},{2,6},{6,2},{3,7},{7,3},{8,12},{12,8},{9,1... | collective-permute-start | bytes 12582920 | tf_op jit(solution)/shard_map/ppermute | solution.py:1719
  399.9 1.1 copy-start.4
  406.7 134.2 %reduce-scatter.11.cloned.1.call-start = ((), (), s32[]{:S(2)}) async-start(), calls=%async_computation.8 | async-start | bytes 2949120 | tf_op jit(solution)/shard_map/reduce_scatter | solution.py:1731
  406.8 10.0 %collective-permute-start.2 = (bf16[4,4,144,512]{3,2,1,0:T(8,128)(2,1)}, bf16[4,4,144,512]{3,2,1,0:T(8,128)(2,1)S(1)}, u32[]{:S(2)}, u32[]{:S(2)}) collective-permute-start(bf16[4,4,144,512]{3,2,1,0:T(8,128)(2,1)} %get-tuple-element.144), channel_id=1, source_target_pairs={{0,4},{4,0},{1,5},{5,1},{2,6},{6,2},{3,7},{7,3},{8,12},{12,8},{9,1... | collective-permute-start | bytes 7077896 | tf_op jit(solution)/shard_map/ppermute | solution.py:1719
  416.8 1.4 copy-start.3
  425.1 0.8 copy-start.14
  425.1 115.8 %reduce-scatter.13.cloned.1.call-start = ((), (), s32[]{:S(2)}) async-start(), calls=%async_computation.9 | async-start | bytes 5242880 | tf_op jit(solution)/shard_map/reduce_scatter | solution.py:1731
  425.8 213.1 %reduce-scatter.15.cloned.1.call-start = ((), (), s32[]{:S(2)}) async-start(), calls=%async_computation.10 | async-start | bytes 6635520 | tf_op jit(solution)/shard_map/reduce_scatter | solution.py:1731
  474.9 11.4 %collective-permute-start.3 = (bf16[4,4,144,1152]{3,2,1,0:T(8,128)(2,1)}, bf16[4,4,144,1152]{3,2,1,0:T(8,128)(2,1)}, u32[]{:S(2)}, u32[]{:S(2)}) collective-permute-start(bf16[4,4,144,1152]{3,2,1,0:T(8,128)(2,1)} %get-tuple-element.157), channel_id=1, source_target_pairs={{0,4},{4,0},{1,5},{5,1},{2,6},{6,2},{3,7},{7,3},{8,12},{12,8},{9,1... | collective-permute-start | bytes 15925256 | tf_op jit(solution)/shard_map/ppermute | solution.py:1719
  498.0 196.1 %reduce-scatter.7.cloned.1.call-start = ((), (), s32[]{:S(2)}) async-start(), calls=%async_computation.6 | async-start | bytes 6635520 | tf_op jit(solution)/shard_map/reduce_scatter | solution.py:1731
  498.1 20.8 %collective-permute-start.4 = (bf16[4,4,144,1152]{3,2,1,0:T(8,128)(2,1)}, bf16[4,4,144,1152]{3,2,1,0:T(8,128)(2,1)}, u32[]{:S(2)}, u32[]{:S(2)}) collective-permute-start(bf16[4,4,144,1152]{3,2,1,0:T(8,128)(2,1)} %get-tuple-element.159), channel_id=1, source_target_pairs={{0,4},{4,0},{1,5},{5,1},{2,6},{6,2},{3,7},{7,3},{8,12},{12,8},{9,1... | collective-permute-start | bytes 15925256 | tf_op jit(solution)/shard_map/ppermute | solution.py:1719
  530.3 1.3 copy-start.21
  530.3 260.2 %reduce-scatter.17.cloned.1.call-start = ((), (), s32[]{:S(2)}) async-start(), calls=%async_computation.11 | async-start | bytes 5160960 | tf_op jit(solution)/shard_map/reduce_scatter | solution.py:1731
  531.6 3.1 collective-permute-start.5
  534.7 1.1 copy-start.5
  638.2 38.5 %collective-permute-start.6 = (bf16[4,4,144,896]{3,2,1,0:T(8,128)(2,1)}, bf16[4,4,144,896]{3,2,1,0:T(8,128)(2,1)}, u32[]{:S(2)}, u32[]{:S(2)}) collective-permute-start(bf16[4,4,144,896]{3,2,1,0:T(8,128)(2,1)} %get-tuple-element.178), channel_id=1, source_target_pairs={{0,4},{4,0},{1,5},{5,1},{2,6},{6,2},{3,7},{7,3},{8,12},{12,8},{9,1... | collective-permute-start | bytes 12386312 | tf_op jit(solution)/shard_map/ppermute | solution.py:1719
  686.6 7.3 copy-start.12
  686.6 7.3 copy-start.11
  686.6 7.3 copy-start.10
  686.6 7.3 copy-start.9
  686.6 7.4 copy-start.8
  686.6 7.4 copy-start.7
  781.2 8.0 copy-start.6
  843.1 6.5 copy-start.2
  849.6 1.4 copy-start.1
Sparse Core Ops, SparseCore 0:
  406.8 29.0 reduce-scatter.8
  438.9 37.3 reduce-scatter.10
  479.9 52.6 reduce-scatter.12
  536.4 61.9 reduce-scatter.14
  602.1 61.9 reduce-scatter.6
  686.8 93.3 reduce-scatter.16

commit v5 on v4

--- a/solution.py
+++ b/solution.py
@@ -60,7 +60,6 @@
 GATHER_AT = (7, 7, 7, 16, 17, 17, 11, 11, 11, 18, 18, 18, 14, 14, 14, 18, 18, 18)
 SECOND_AT, THIRD_AT = 6, 15
 FEED_AT = (1, 1, 4, 5, 5, 8, 7, 7, 8, 3, 3, 6, 7, 7, 8, 8, 8, 8, 5, 5, 7, 8, 8, 8, 8, 8, 8)
-SETTLE_AT = (4, 7, 12, 15)
 
 
 def head_window(head, width):
@@ -165,8 +164,6 @@
             work.link.greet()
             work.start()
 
-        for k in range(carried):
-            pl.when(head == SETTLE_AT[k])(functools.partial(work.add, k))
     else:
         grads, dots = rest[:-1], rest[-1]
     dq_ref, dk_ref, dv_ref = grads if len(grads) == 3 else grads * 3
@@ -216,7 +213,12 @@
     put(dk_ref, every, base + columns[1], mine, grad_keys * HEAD_DIM ** (-0.5))
     put(dv_ref, every, base + columns[2], mine, grad_values)
     if work is not None:
-        pl.when(head == pl.num_programs(0) - 1)(work.finish)
+
+        @pl.when(head == pl.num_programs(0) - 1)
+        def _():
+            for k in range(carried):
+                work.add(k)
+            work.finish()
 
 
 def put(ref, rows, base, mine, value):

time: 871 us -> 869 us (level)
  no operation moved by 1% of the time
where the time goes in v5:
time: 869 us; the launch traced here: 856 us
  Pallas kernels  799 us (92%)
  local copies, waits for them, and re-layouts  25.1 us (3%)
  between operations  14.9 us (2%)
  other arithmetic  11.4 us (1%)
    pallas_call x23, Pallas kernels, call(): pl.pallas_call(kernel, grid_spec=grid_spec, out_shape=[jax.ShapeDtypeStru...  499 us
    pallas_call x2, Pallas kernels, settle(): pl.pallas_call(functools.partial(settle_kernel, sums=len(sums), shares=le...  129 us
    pallas_call x1, Pallas kernels, bring(): pl.pallas_call(functools.partial(bring_kernel, bundles=[len(shard) for sh...  85.2 us
    pallas_call x1, Pallas kernels, attend_backward(): pl.pallas_call(functools.partial(attend_backward_kernel, block=min(256, c...  85 us
  transfers between devices with their start and end apart: 13, of which 1 were waited for; matrix products, arithmetic and copies ran while one was open for 2% of the time, Pallas kernels for 44%

profile of v5, /device:TPU:9, one launch (start us, length us, event | category | flops | bytes accessed | tf_op | source)
XLA Modules:
  0.0 856.5 jit_solution(15530345656488961052)
XLA Ops:
  7.3 1.3 reshape.167.refs_3_
  8.6 85.2 %bring.1 = (bf16[4,4,288,1152]{3,2,1,0:T(8,128)(2,1)}, bf16[4,256,1152]{2,1,0:T(8,128)(2,1)}, s32[4,2,128]{2,1,0:T(2,128)}) custom-call(bf16[288,3456]{1,0:T(8,128)(2,1)} %refs_0_.3, bf16[288,1152]{1,0:T(8,128)(2,1)} %refs_1_.1, bf16[4,256,1152]{2,1,0:T(8,128)(2,1)} %refs_2_.2, s32[4,2,128]{2,1,0:T(2,128)} %reshape.167.refs_3_), custom_call_target="tpu_custom_call" | custom-call | bytes 300000000 | tf_op jit(solution)/shard_map/bring/pallas_call | solution.py:1425
  93.8 1.6 fusion.hot_ref
  95.4 1.7 copy.35.seg_ref.segq_ref.segk_ref
  102.1 117.3 %project.1 = (bf16[1024,3456]{1,0:T(8,128)(2,1)}, bf16[1152,1024]{1,0:T(8,128)(2,1)}, bf16[1024,1152]{1,0:T(8,128)(2,1)}, f32[16,1024]{1,0:T(8,128)}, bf16[4,4,2...) custom-call(bf16[1024,1152]{1,0:T(8,128)(2,1)} %bitcast.63, ...), custom_call_target="tpu_custom_call" | custom-call | flops 25333596160 | bytes 55019008 | tf_op jit(solution)/shard_map/project/pallas_call | solution.py:421
  219.5 10.8 %merge.1 = (bf16[1024,1152]{1,0:T(8,128)(2,1)}, f32[1024,1152]{1,0:T(8,128)}, bf16[1024,1152]{1,0:T(8,128)(2,1)}, bf16[1152,1024]{1,0:T(8,128)(2,1)}, bf16[1152,1024]{1,0:T(8,128)(2,1)}) custom-call(bf16[1024,1152]{1,0:T(8,128)(2,1)} %get-tuple-element.120.out_ref, bf16[1024,1152]{1,0:T(8,128)(2,1)} %bitcast.64, bf16[1024,16]{1,0:T(8,128)(2,1)} %fusion.hot_ref, ...), custom_call_target="tpu_custom_call" | custom-call | flops 2717908992 | bytes 30192128 | tf_op jit(solution)/shard_map/merge/pallas_call | solution.py:421
  230.2 84.8 %feed.1 = (bf16[4608,1024]{1,0:T(8,128)(2,1)}, bf16[1024,4608]{1,0:T(8,128)(2,1)}, bf16[1024,1152]{1,0:T(8,128)(2,1)}, bf16[1152,1024]{1,0:T(8,128)(2,1)}, bf16[...) custom-call(bf16[1024,1152]{1,0:T(8,128)(2,1)} %get-tuple-element.12, ...), custom_call_target="tpu_custom_call" | custom-call | flops 21743271936 | bytes 74856960 | tf_op jit(solution)/shard_map/feed/pallas_call | solution.py:421
  315.0 63.9 %align.1 = (bf16[2048,1024]{1,0:T(8,128)(2,1)}, bf16[2048,1024]{1,0:T(8,128)(2,1)}, bf16[1024,768]{1,0:T(8,128)(2,1)}, bf16[1024,2048]{1,0:T(8,128)(2,1)}, bf16[...) custom-call(bf16[1024,1152]{1,0:T(8,128)(2,1)} %get-tuple-element.125.res_ref, ...), custom_call_target="tpu_custom_call" | custom-call | flops 33285996544 | bytes 47991808 | tf_op jit(solution)/shard_map/align/pallas_call | solution.py:421
  379.0 5.6 weight_other.7
  385.1 8.4 weight_other.8
  393.5 6.4 weight_other.9
  399.9 1.1 copy-done.4
  401.1 5.6 weight_own.7
  407.3 9.5 %weight_own.8 = bf16[4,4,256,512]{3,2,1,0:T(8,128)(2,1)} custom-call(s32[1]{0:T(128)} %bitcast.14.where_ref, bf16[4,2,256,1024]{3,2,1,0:T(8,128)(2,1)} %bitcast.60, bf16[1024,2048]{1,0:T(8,128)(2,1)} %get-tuple-element.146.right_ref, bf16[4,4,256,512]{3,2,1,0:T(8,128)(2,1)} %collective-permute-done.1.refs_0_), custom_call_target="tpu_custom_call" | custom-call | flops 4294967296 | bytes 16777216 | tf_op jit(solution)/shard_map/weight_own/pallas_call | solution.py:421
  416.8 1.4 copy-done.3
  418.2 6.8 weight_own.9
  426.5 37.3 %feed_back.1 = (bf16[1024,1152]{1,0:T(8,128)(2,1)}, bf16[1024,4608]{1,0:T(8,128)(2,1)}, f32[1024,1152]{1,0:T(8,128)}, f32[16,1152]{1,0:T(8,128)}) custom-call(f32[1024,1152]{1,0:T(8,128)} %get-tuple-element.148.gout_ref, bf16[1024,1152]{1,0:T(8,128)(2,1)} %get-tuple-element.149.branch_ref, bf16[1024,16]{1,0:T(8,128)(2,1)} %fusion.hot_ref, ...), custom_call_target="tpu_custom_call" | custom-call | flops 21743271936 | bytes 54624256 | tf_op jit(solution)/shard_map/feed_back/pallas_call | solution.py:421
  463.7 11.2 %weight_other.10 = (bf16[4,4,144,1152]{3,2,1,0:T(8,128)(2,1)}, f32[16,1152]{1,0:T(8,128)}) custom-call(s32[1]{0:T(128)} %bitcast.14.where_ref, bf16[4,4,2,144,1024]{4,3,2,1,0:T(8,128)(2,1)} %bitcast.55, bf16[1024,1152]{1,0:T(8,128)(2,1)} %get-tuple-element.160.right_ref), custom_call_target="tpu_custom_call" | custom-call | flops 5435817984 | bytes 17178624 | tf_op jit(solution)/shard_map/weight_other/pallas_call | solution.py:421
  475.0 11.3 %weight_other.11 = (bf16[4,4,144,1152]{3,2,1,0:T(8,128)(2,1)}, f32[16,4608]{1,0:T(8,128)}) custom-call(s32[1]{0:T(128)} %bitcast.14.where_ref, bf16[4,2,144,1024]{3,2,1,0:T(8,128)(2,1)} %bitcast.66, bf16[1024,4608]{1,0:T(8,128)(2,1)} %get-tuple-element.167.right_ref), custom_call_target="tpu_custom_call" | custom-call | flops 5435817984 | bytes 17399808 | tf_op jit(solution)/shard_map/weight_other/pallas_call | solution.py:421
  486.4 11.6 %weight_own.10 = bf16[4,4,144,1152]{3,2,1,0:T(8,128)(2,1)} custom-call(s32[1]{0:T(128)} %bitcast.14.where_ref, bf16[4,4,2,144,1024]{4,3,2,1,0:T(8,128)(2,1)} %bitcast.56, bf16[1024,1152]{1,0:T(8,128)(2,1)} %get-tuple-element.160.right_ref, bf16[4,4,144,1152]{3,2,1,0:T(8,128)(2,1)} %collective-permute-done.3.refs_0_), custom_call_target="tpu_custom_call" | custom-call | flops 5435817984 | bytes 22413312 | tf_op jit(solution)/shard_map/weight_own/pallas_call | solution.py:421
  498.4 15.4 %merge_back.1 = (f32[1024,1152]{1,0:T(8,128)}, bf16[1024,1152]{1,0:T(8,128)(2,1)}, bf16[1024,1152]{1,0:T(8,128)(2,1)}, f32[16,1152]{1,0:T(8,128)}, f32[16,1152]{1,0:T(8,128)}, /*index=5*/f32[16,1152]{1,0:T(8,128)}) custom-call(f32[1024,1152]{1,0:T(8,128)} %get-tuple-element.148.gout_ref, f32[1024,1152]{1,0:T(8,128)} %get-tuple-element.161.gmod_ref, ...), custom_call_target="tpu_custom_call" | custom-call | flops 2717908992 | bytes 37298176 | tf_op jit(solution)/shard_map/merge_back/pallas_call | solution.py:421
  513.8 5.1 weight_other.12
  518.9 11.4 %weight_own.11 = bf16[4,4,144,1152]{3,2,1,0:T(8,128)(2,1)} custom-call(s32[1]{0:T(128)} %bitcast.14.where_ref, bf16[4,2,144,1024]{3,2,1,0:T(8,128)(2,1)} %bitcast.67, bf16[1024,4608]{1,0:T(8,128)(2,1)} %get-tuple-element.167.right_ref, bf16[4,4,144,1152]{3,2,1,0:T(8,128)(2,1)} %collective-permute-done.4.refs_0_), custom_call_target="tpu_custom_call" | custom-call | flops 5435817984 | bytes 22413312 | tf_op jit(solution)/shard_map/weight_own/pallas_call | solution.py:421
  530.3 1.2 copy-done.21
  531.8 2.8 collective-permute-done.5.refs_0_
  534.7 1.1 copy-done.5
  535.7 5.1 weight_own.12
  540.9 85.0 %attend_backward.1 = (bf16[1024,3584]{1,0:T(8,128)(2,1)}, bf16[64,768]{1,0:T(8,128)(2,1)}, bf16[144,512]{1,0:T(8,128)(2,1)}, bf16[256,512]{1,0:T(8,128)(2,1)}, bf16[144,1152]{1,0:T(8,128)(2,1)}) custom-call(bf16[1024,3456]{1,0:T(8,128)(2,1)} %get-tuple-element.168.q_ref.k_ref.v_ref, bf16[1024,3456]{1,0:T(8,128)(2,1)} %get-tuple-element.168.q_ref.k_ref.v_ref, ...), custom_call_target="tpu_custom_call" | custom-call | flops 42949672960 | bytes 18874368 | tf_op jit(solution)/shard_map/attend_backward/pallas_call | solution.py:241
  625.9 9.5 %weight_other.13 = (bf16[4,4,144,896]{3,2,1,0:T(8,128)(2,1)}, f32[16,3584]{1,0:T(8,128)}) custom-call(s32[1]{0:T(128)} %bitcast.14.where_ref, bf16[4,2,144,1024]{3,2,1,0:T(8,128)(2,1)} %bitcast.69, bf16[1024,3584]{1,0:T(8,128)(2,1)} %get-tuple-element.184.right_ref.gqkv_ref), custom_call_target="tpu_custom_call" | custom-call | flops 4227858432 | bytes 14057472 | tf_op jit(solution)/shard_map/weight_other/pallas_call | solution.py:421
  635.3 0.8 collective-permute-start.6
  636.1 38.0 %project_back.1 = (bf16[1024,1152]{1,0:T(8,128)(2,1)}, f32[16,1152]{1,0:T(8,128)}, f32[16,1152]{1,0:T(8,128)}, bf16[144,1152]{1,0:T(8,128)(2,1)}) custom-call(bf16[1024,3584]{1,0:T(8,128)(2,1)} %get-tuple-element.184.right_ref.gqkv_ref, bf16[1024,1152]{1,0:T(8,128)(2,1)} %bitcast.65, f32[1024,1152]{1,0:T(8,128)} %get-tuple-element.180.gmid_ref, ...), custom_call_target="tpu_custom_call" | custom-call | flops 8153726976 | bytes 29487104 | tf_op jit(solution)/shard_map/project_back/pallas_call | solution.py:421
  674.1 9.9 %weight_own.13 = bf16[4,4,144,896]{3,2,1,0:T(8,128)(2,1)} custom-call(s32[1]{0:T(128)} %bitcast.14.where_ref, bf16[4,2,144,1024]{3,2,1,0:T(8,128)(2,1)} %bitcast.70, bf16[1024,3584]{1,0:T(8,128)(2,1)} %get-tuple-element.184.right_ref.gqkv_ref, bf16[4,4,144,896]{3,2,1,0:T(8,128)(2,1)} %collective-permute-done.6.refs_0_), custom_call_target="tpu_custom_call" | custom-call | flops 4227858432 | bytes 17956864 | tf_op jit(solution)/shard_map/weight_own/pallas_call | solution.py:421
  684.1 1.0 slice_reduce_fusion.2
  685.1 0.9 slice_reduce_fusion.1
  686.0 0.8 slice_reduce_fusion.7
  686.8 1.0 slice_reduce_fusion
  687.8 0.8 slice_reduce_fusion.3
  688.7 0.8 slice_reduce_fusion.4
  689.5 0.9 slice_reduce_fusion.6
  691.6 82.4 %settle.2 = (bf16[144,1152]{1,0:T(8,128)(2,1)}, bf16[4,2,64,768]{3,2,1,0:T(8,128)(2,1)}, bf16[4,2,256,512]{3,2,1,0:T(8,128)(2,1)}, bf16[4,2,144,512]{3,2,1,0:T(8...) custom-call(bf16[4,144,1152]{2,1,0:T(8,128)(2,1)} %bitcast.75, ...), custom_call_target="tpu_custom_call" | custom-call | bytes 200000000 | tf_op jit(solution)/shard_map/settle/pallas_call | solution.py:1492
  774.0 4.2 convert_element_type.40
  778.2 8.0 unpack.3
  786.2 1.2 bitcast_convert_fusion
  788.1 46.7 %settle.3 = (bf16[144,896]{1,0:T(8,128)(2,1)}, f32[32,128]{1,0:T(8,128)}, bf16[4,2,144,1152]{3,2,1,0:T(8,128)(2,1)}, bf16[4,2,144,896]{3,2,1,0:T(8,128)(2,1)}, f...) custom-call(bf16[4,144,896]{2,1,0:T(8,128)(2,1)} %bitcast.77, f32[4,32,128]{2,1,0:T(8,128)} %bitcast.78, ...), custom_call_target="tpu_custom_call" | custom-call | bytes 200000000 | tf_op jit(solution)/shard_map/settle/pallas_call | solution.py:1492
  838.9 1.0 slice_convert_fusion
  839.8 0.9 reshape.206
  841.3 6.5 unpack.2
  847.8 1.4 copy.47
  (112 shorter events, 15.0 us)
Async XLA Ops:
  7.2 94.2 %copy-start = (bf16[4,4,6912]{2,1,0:T(4,128)(2,1)S(1)}, bf16[4,4,6912]{2,1,0:T(4,128)(2,1)}, u32[]{:S(2)}) copy-start(bf16[4,4,6912]{2,1,0:T(4,128)(2,1)} %param.19) | copy-start | bytes 663556
  7.2 533.7 %reduce-scatter.9.cloned.1.call-start = ((), (), s32[]{:S(2)}) async-start(), calls=%async_computation.7 | async-start | bytes 1966080 | tf_op jit(solution)/shard_map/reduce_scatter | solution.py:1733
  8.6 88.5 %copy-start.13 = (bf16[2304]{0:T(1024)(128)(2,1)S(1)}, bf16[2304]{0:T(1024)(128)(2,1)}, u32[]{:S(2)}) copy-start(bf16[2304]{0:T(1024)(128)(2,1)} %param.22) | copy-start | bytes 13828
  8.6 89.2 %copy-start.18 = (bf16[1152]{0:T(1024)(128)(2,1)S(1)}, bf16[1152]{0:T(1024)(128)(2,1)}, u32[]{:S(2)}) copy-start(bf16[1152]{0:T(1024)(128)(2,1)} %param.24) | copy-start | bytes 6916
  8.6 89.8 %copy-start.15 = (bf16[4608]{0:T(1024)(128)(2,1)S(1)}, bf16[4608]{0:T(1024)(128)(2,1)}, u32[]{:S(2)}) copy-start(bf16[4608]{0:T(1024)(128)(2,1)} %param.26) | copy-start | bytes 27652
  8.6 90.4 %copy-start.19 = (bf16[1152]{0:T(1024)(128)(2,1)S(1)}, bf16[1152]{0:T(1024)(128)(2,1)}, u32[]{:S(2)}) copy-start(bf16[1152]{0:T(1024)(128)(2,1)} %param.28) | copy-start | bytes 6916
  8.6 91.0 %copy-start.16 = (bf16[2048]{0:T(1024)(128)(2,1)S(1)}, bf16[2048]{0:T(1024)(128)(2,1)}, u32[]{:S(2)}) copy-start(bf16[2048]{0:T(1024)(128)(2,1)} %param.32) | copy-start | bytes 12292
  8.6 91.6 %copy-start.17 = (bf16[2048]{0:T(1024)(128)(2,1)S(1)}, bf16[2048]{0:T(1024)(128)(2,1)}, u32[]{:S(2)}) copy-start(bf16[2048]{0:T(1024)(128)(2,1)} %param.30) | copy-start | bytes 12292
  8.6 92.2 %copy-start.20 = (bf16[768]{0:T(1024)(128)(2,1)S(1)}, bf16[768]{0:T(1024)(128)(2,1)}, u32[]{:S(2)}) copy-start(bf16[768]{0:T(1024)(128)(2,1)} %param.34) | copy-start | bytes 4612
  384.6 15.3 %collective-permute-start = (bf16[4,4,64,768]{3,2,1,0:T(8,128)(2,1)}, bf16[4,4,64,768]{3,2,1,0:T(8,128)(2,1)S(1)}, u32[]{:S(2)}, u32[]{:S(2)}) collective-permute-start(bf16[4,4,64,768]{3,2,1,0:T(8,128)(2,1)} %get-tuple-element.140), channel_id=1, source_target_pairs={{0,4},{4,0},{1,5},{5,1},{2,6},{6,2},{3,7},{7,3},{8,12},{12,8},{9,1... | collective-permute-start | bytes 4718600 | tf_op jit(solution)/shard_map/ppermute | solution.py:1721
  393.5 13.8 %collective-permute-start.1 = (bf16[4,4,256,512]{3,2,1,0:T(8,128)(2,1)}, bf16[4,4,256,512]{3,2,1,0:T(8,128)(2,1)}, u32[]{:S(2)}, u32[]{:S(2)}) collective-permute-start(bf16[4,4,256,512]{3,2,1,0:T(8,128)(2,1)} %get-tuple-element.142), channel_id=1, source_target_pairs={{0,4},{4,0},{1,5},{5,1},{2,6},{6,2},{3,7},{7,3},{8,12},{12,8},{9,1... | collective-permute-start | bytes 12582920 | tf_op jit(solution)/shard_map/ppermute | solution.py:1721
  399.9 1.1 copy-start.4
  406.7 134.2 %reduce-scatter.11.cloned.1.call-start = ((), (), s32[]{:S(2)}) async-start(), calls=%async_computation.8 | async-start | bytes 2949120 | tf_op jit(solution)/shard_map/reduce_scatter | solution.py:1733
  406.8 10.0 %collective-permute-start.2 = (bf16[4,4,144,512]{3,2,1,0:T(8,128)(2,1)}, bf16[4,4,144,512]{3,2,1,0:T(8,128)(2,1)S(1)}, u32[]{:S(2)}, u32[]{:S(2)}) collective-permute-start(bf16[4,4,144,512]{3,2,1,0:T(8,128)(2,1)} %get-tuple-element.144), channel_id=1, source_target_pairs={{0,4},{4,0},{1,5},{5,1},{2,6},{6,2},{3,7},{7,3},{8,12},{12,8},{9,1... | collective-permute-start | bytes 7077896 | tf_op jit(solution)/shard_map/ppermute | solution.py:1721
  416.8 1.4 copy-start.3
  425.1 0.8 copy-start.14
  425.1 115.8 %reduce-scatter.13.cloned.1.call-start = ((), (), s32[]{:S(2)}) async-start(), calls=%async_computation.9 | async-start | bytes 5242880 | tf_op jit(solution)/shard_map/reduce_scatter | solution.py:1733
  425.8 210.3 %reduce-scatter.15.cloned.1.call-start = ((), (), s32[]{:S(2)}) async-start(), calls=%async_computation.10 | async-start | bytes 6635520 | tf_op jit(solution)/shard_map/reduce_scatter | solution.py:1733
  474.9 11.4 %collective-permute-start.3 = (bf16[4,4,144,1152]{3,2,1,0:T(8,128)(2,1)}, bf16[4,4,144,1152]{3,2,1,0:T(8,128)(2,1)}, u32[]{:S(2)}, u32[]{:S(2)}) collective-permute-start(bf16[4,4,144,1152]{3,2,1,0:T(8,128)(2,1)} %get-tuple-element.157), channel_id=1, source_target_pairs={{0,4},{4,0},{1,5},{5,1},{2,6},{6,2},{3,7},{7,3},{8,12},{12,8},{9,1... | collective-permute-start | bytes 15925256 | tf_op jit(solution)/shard_map/ppermute | solution.py:1721
  498.0 193.6 %reduce-scatter.7.cloned.1.call-start = ((), (), s32[]{:S(2)}) async-start(), calls=%async_computation.6 | async-start | bytes 6635520 | tf_op jit(solution)/shard_map/reduce_scatter | solution.py:1733
  498.1 20.8 %collective-permute-start.4 = (bf16[4,4,144,1152]{3,2,1,0:T(8,128)(2,1)}, bf16[4,4,144,1152]{3,2,1,0:T(8,128)(2,1)}, u32[]{:S(2)}, u32[]{:S(2)}) collective-permute-start(bf16[4,4,144,1152]{3,2,1,0:T(8,128)(2,1)} %get-tuple-element.159), channel_id=1, source_target_pairs={{0,4},{4,0},{1,5},{5,1},{2,6},{6,2},{3,7},{7,3},{8,12},{12,8},{9,1... | collective-permute-start | bytes 15925256 | tf_op jit(solution)/shard_map/ppermute | solution.py:1721
  530.3 1.3 copy-start.21
  530.3 257.1 %reduce-scatter.17.cloned.1.call-start = ((), (), s32[]{:S(2)}) async-start(), calls=%async_computation.11 | async-start | bytes 5160960 | tf_op jit(solution)/shard_map/reduce_scatter | solution.py:1733
  531.6 3.1 collective-permute-start.5
  534.7 1.1 copy-start.5
  635.3 38.8 %collective-permute-start.6 = (bf16[4,4,144,896]{3,2,1,0:T(8,128)(2,1)}, bf16[4,4,144,896]{3,2,1,0:T(8,128)(2,1)}, u32[]{:S(2)}, u32[]{:S(2)}) collective-permute-start(bf16[4,4,144,896]{3,2,1,0:T(8,128)(2,1)} %get-tuple-element.178), channel_id=1, source_target_pairs={{0,4},{4,0},{1,5},{5,1},{2,6},{6,2},{3,7},{7,3},{8,12},{12,8},{9,1... | collective-permute-start | bytes 12386312 | tf_op jit(solution)/shard_map/ppermute | solution.py:1721
  684.0 7.3 copy-start.12
  684.0 7.3 copy-start.11
  684.1 7.3 copy-start.10
  684.1 7.3 copy-start.9
  684.1 7.4 copy-start.8
  684.1 7.4 copy-start.7
  778.2 8.0 copy-start.6
  841.3 6.5 copy-start.2
  847.8 1.4 copy-start.1
Sparse Core Ops, SparseCore 0:
  406.8 29.0 reduce-scatter.8
  438.9 37.3 reduce-scatter.10
  479.9 52.6 reduce-scatter.12
  536.4 61.9 reduce-scatter.14
  602.1 61.9 reduce-scatter.6
  684.2 93.1 reduce-scatter.16
